TPU v7x, 32 devices: a whole 2x2x4 slice. The times are simulated.
32 devices in a mesh: dp: 8 (over y, x, core), mp: 4 (over z).
Axes of the slice: x: 2, y: 2, z: 4, core: 2. Of those that a mesh axis runs over, the one named last changes fastest.
Arguments:
- block_in: bfloat16 [16384, 1536], P(('dp', 'mp')), may hold values from -12 to 12
- cotangent: bfloat16 [16384, 1536], P(('dp', 'mp')), may hold values from -6 to 6
- segment_ids: int32 [32, 512], P(('dp', 'mp')), may hold values from 0 to 3, never falling along the last dimension, each value on 1 to 256 neighbouring positions
- granularity: int32 [32], P('dp'), may hold values from 0 to 3, as said below
- w_qkv: bfloat16 [1536, 4608], P('dp'), may hold values from -0.15625 to 0.15625
- w_out: bfloat16 [1536, 1536], P('dp'), may hold values from -0.625 to 0.625
- w_up: bfloat16 [1536, 6144], P('dp', 'mp'), may hold values from -0.15625 to 0.15625
- w_down: bfloat16 [6144, 1536], P('mp', 'dp'), may hold values from -0.15625 to 0.15625
- norm1_gain: float32 [1536], replicated, may hold values from 0.1 to 1.9
- norm1_bias: float32 [1536], replicated, may hold values from -1.75 to 1.75
- norm2_gain: float32 [1536], replicated, may hold values from 0.1 to 1.9
- norm2_bias: float32 [1536], replicated, may hold values from -1.75 to 1.75
Outputs:
- block_out: bfloat16 [16384, 1536], P(('dp', 'mp'))
- grad_input: float32 [16384, 1536], P(('dp', 'mp'))
- grad_w_qkv: float32 [1536, 4608], P('dp')
- grad_w_out: float32 [1536, 1536], P('dp')
- grad_w_up: float32 [1536, 6144], P('dp', 'mp')
- grad_w_down: float32 [6144, 1536], P('mp', 'dp')
- grad_norm1_gain: float32 [1536], replicated
- grad_norm1_bias: float32 [1536], replicated
- grad_norm2_gain: float32 [1536], replicated
- grad_norm2_bias: float32 [1536], replicated
Inputs may be any that keep to these rules, and one draw needn't show every extreme that they name: Each aligned run of the sequences of one index of dp holds at least one sequence of granularity 3.
All inputs are finite; a program needn't handle non-finite values.
Results may differ from a plain program's by a relative error of at most 0.019.
Values may be sent and summed in bfloat16 or wider, within the bound.
No kernel may reach another device: no remote copies, remote signals or barrier semaphores. Data moves between devices by JAX's collectives and lax.ppermute only.
A program may use at most 256 MiB of HBM per device.

v0:
```python
import jax
import jax.numpy as jnp
from jax import lax
from jax.sharding import PartitionSpec as P

HEADS = 12
HEAD_DIM = 128
BLOCK = 768


epsilon = 1e-05
theta_base = 10000.0
contract_rows = (((0,), (0,)), ((), ()))
contract_cols = (((1,), (1,)), ((), ()))


def layer_norm(values, norm_gain, norm_shift):
    average = jnp.mean(values, axis=-1, keepdims=True)
    centred = values - average
    variance = jnp.mean(centred * centred, axis=-1, keepdims=True)
    return centred * lax.rsqrt(variance + epsilon) * norm_gain + norm_shift


def rotary_tables(length, head_width):
    halfway = head_width // 2
    frequency = theta_base ** (-2.0 * jnp.arange(halfway, dtype=jnp.float32) / head_width)
    angles = jnp.arange(length, dtype=jnp.float32)[:, None] * frequency[None, :]
    angles = jnp.concatenate([angles, angles], axis=1)
    return (jnp.cos(angles), jnp.sin(angles))


def rotate(values, cosine_table, sine_table):
    halfway = values.shape[-1] // 2
    turned = jnp.concatenate([-values[..., halfway:], values[..., :halfway]], axis=-1)
    return values * cosine_table[:, None, :] + turned * sine_table[:, None, :]


def gelu_slope(values):
    normal_cdf = 0.5 * (1.0 + jax.scipy.special.erf(values * 0.7071067811865476))
    return normal_cdf + values * jnp.exp(-0.5 * values * values) * 0.3989422804014327


def on_device(
    block_in,
    cotangent,
    segment_ids,
    granularity,
    w_qkv,
    w_out,
    w_up,
    w_down,
    norm1_gain,
    norm1_bias,
    norm2_gain,
    norm2_bias,
):
    seq_len = block_in.shape[0]
    width = block_in.shape[1]
    unit_dev = w_up.shape[1]
    head_width = HEAD_DIM
    head_count = HEADS
    score_scale = HEAD_DIM ** (-0.5)
    wide_qkv, wide_out = (
        lax.all_gather(w_qkv, "dp", axis=0, tiled=True),
        lax.all_gather(w_out, "dp", axis=0, tiled=True),
    )
    wide_up, wide_down = (
        lax.all_gather(w_up, "dp", axis=0, tiled=True),
        lax.all_gather(w_down, "dp", axis=1, tiled=True),
    )
    inputs = block_in.astype(jnp.float32)
    normed1, norm1_back = jax.vjp(layer_norm, inputs, norm1_gain, norm1_bias)
    normed1_low = normed1.astype(jnp.bfloat16)
    joined_qkv = jnp.dot(normed1_low, wide_qkv, preferred_element_type=jnp.float32)
    pieces = joined_qkv.reshape(seq_len, 3, head_count, head_width)
    cosine_table, sine_table = rotary_tables(seq_len, head_width)

    def turn_both(query_raw, key_raw):
        return (
            rotate(query_raw, cosine_table, sine_table),
            rotate(key_raw, cosine_table, sine_table),
        )

    (query_rot, key_rot), turn_back = jax.vjp(turn_both, pieces[:, 0], pieces[:, 1])
    query_low = query_rot.astype(jnp.bfloat16)
    key_low = key_rot.astype(jnp.bfloat16)
    value_low = pieces[:, 2].astype(jnp.bfloat16)
    segment = segment_ids[0]
    places = jnp.arange(seq_len)
    allowed = (places[:, None] >= places[None, :]) & (segment[:, None] == segment[None, :])

    def score_block():
        raw_scores = jnp.einsum(
            "shd,thd->hst", query_low, key_low, preferred_element_type=jnp.float32
        )
        return jnp.where(allowed[None], raw_scores * score_scale, -1000000000.0)

    scores = score_block()
    row_max = jnp.max(scores, axis=-1, keepdims=True)
    exponent = jnp.exp(scores - row_max)
    row_sum = jnp.sum(exponent, axis=-1, keepdims=True)
    log_total = row_max + jnp.log(row_sum)
    probs_low = (exponent / row_sum).astype(jnp.bfloat16)
    context = jnp.einsum("hst,thd->shd", probs_low, value_low, preferred_element_type=jnp.float32)
    context_low = context.reshape(seq_len, width).astype(jnp.bfloat16)
    hidden1 = inputs + jnp.dot(context_low, wide_out, preferred_element_type=jnp.float32)
    normed2, norm2_back = jax.vjp(layer_norm, hidden1, norm2_gain, norm2_bias)
    normed2_low = normed2.astype(jnp.bfloat16)
    unit_start = lax.axis_index("mp") * unit_dev
    prefix_units = BLOCK * jnp.power(2, granularity)
    seq_slots = jnp.arange(granularity.shape[0])

    def unit_mask(row_count):
        owners = jnp.arange(row_count) // seq_len
        row_limit = jnp.sum(
            jnp.where(owners[:, None] == seq_slots[None, :], prefix_units[None, :], 0), axis=1
        )
        unit_ids = unit_start + jnp.arange(unit_dev)
        return (unit_ids[None, :] < row_limit[:, None]).astype(jnp.float32)

    piece_rows = lax.all_gather(normed2_low, "mp", axis=0, tiled=True)
    preact = jnp.dot(piece_rows, wide_up, preferred_element_type=jnp.float32)
    active = jax.nn.gelu(preact, approximate=False) * unit_mask(piece_rows.shape[0])
    expand_active_low = active.astype(jnp.bfloat16)
    block_rows = expand_active_low
    ffn_part = lax.psum_scatter(
        jnp.dot(block_rows, wide_down, preferred_element_type=jnp.float32).astype(jnp.bfloat16),
        "mp",
        scatter_dimension=0,
        tiled=True,
    ).astype(jnp.float32)
    block_out = (hidden1 + ffn_part).astype(jnp.bfloat16)
    grad_out = cotangent.astype(jnp.float32)
    piece_rows = lax.all_gather(cotangent, "mp", axis=0, tiled=True)
    grad_part = lax.dot_general(
        piece_rows, wide_down, contract_cols, preferred_element_type=jnp.float32
    )
    ffn_inputs = lax.all_gather(normed2_low, "mp", axis=0, tiled=True)
    ffn_preact = jnp.dot(ffn_inputs, wide_up, preferred_element_type=jnp.float32)
    full_mask = unit_mask(ffn_inputs.shape[0])
    grad_preact_low = (grad_part * full_mask * gelu_slope(ffn_preact)).astype(jnp.bfloat16)
    grad_down_local = lax.dot_general(
        expand_active_low, piece_rows, contract_rows, preferred_element_type=jnp.float32
    )
    grad_up_local = lax.dot_general(
        ffn_inputs, grad_preact_low, contract_rows, preferred_element_type=jnp.float32
    )
    block_rows = grad_preact_low
    grad_normed2 = lax.psum_scatter(
        lax.dot_general(
            block_rows, wide_up, contract_cols, preferred_element_type=jnp.float32
        ).astype(jnp.bfloat16),
        "mp",
        scatter_dimension=0,
        tiled=True,
    ).astype(jnp.float32)
    grad_hidden_norm, grad_gain2, grad_bias2 = norm2_back(grad_normed2)
    grad_hidden1 = grad_out + grad_hidden_norm
    grad_attn_low = grad_hidden1.astype(jnp.bfloat16)
    grad_out_local = lax.dot_general(
        context_low, grad_attn_low, contract_rows, preferred_element_type=jnp.float32
    )
    grad_context = lax.dot_general(
        grad_attn_low, wide_out, contract_cols, preferred_element_type=jnp.float32
    )
    grad_context_low = grad_context.astype(jnp.bfloat16).reshape(seq_len, head_count, head_width)
    probs_again = jnp.exp(score_block() - log_total)
    probs_again_low = probs_again.astype(jnp.bfloat16)
    grad_probs = jnp.einsum(
        "shd,thd->hst", grad_context_low, value_low, preferred_element_type=jnp.float32
    )
    grad_value = jnp.einsum(
        "hst,shd->thd", probs_again_low, grad_context_low, preferred_element_type=jnp.float32
    )
    weighted = jnp.sum(probs_again * grad_probs, axis=-1, keepdims=True)
    grad_scores_low = (probs_again * (grad_probs - weighted) * score_scale).astype(jnp.bfloat16)
    grad_query = jnp.einsum(
        "hst,thd->shd", grad_scores_low, key_low, preferred_element_type=jnp.float32
    )
    grad_key = jnp.einsum(
        "hst,shd->thd", grad_scores_low, query_low, preferred_element_type=jnp.float32
    )
    grad_query_raw, grad_key_raw = turn_back((grad_query, grad_key))
    grad_joined = jnp.stack([grad_query_raw, grad_key_raw, grad_value], axis=1)
    grad_joined_low = grad_joined.reshape(seq_len, 3 * width).astype(jnp.bfloat16)
    grad_qkv_local = lax.dot_general(
        normed1_low, grad_joined_low, contract_rows, preferred_element_type=jnp.float32
    )
    grad_normed1 = lax.dot_general(
        grad_joined_low, wide_qkv, contract_cols, preferred_element_type=jnp.float32
    )
    grad_input_norm, grad_gain1, grad_bias1 = norm1_back(grad_normed1)
    grad_input = grad_hidden1 + grad_input_norm
    grad_up, grad_down = (
        lax.psum_scatter(
            grad_up_local.astype(jnp.bfloat16), "dp", scatter_dimension=0, tiled=True
        ).astype(jnp.float32),
        lax.psum_scatter(
            grad_down_local.astype(jnp.bfloat16), "dp", scatter_dimension=1, tiled=True
        ).astype(jnp.float32),
    )
    shares = (
        lax.psum_scatter(
            grad_qkv_local.astype(jnp.bfloat16), "dp", scatter_dimension=0, tiled=True
        ).astype(jnp.float32),
        lax.psum_scatter(
            grad_out_local.astype(jnp.bfloat16), "dp", scatter_dimension=0, tiled=True
        ).astype(jnp.float32),
    )
    grad_qkv, grad_proj = (
        lax.psum(shares[0].astype(jnp.bfloat16), "mp").astype(jnp.float32),
        lax.psum(shares[1].astype(jnp.bfloat16), "mp").astype(jnp.float32),
    )
    norm_totals = lax.psum((grad_gain1, grad_bias1, grad_gain2, grad_bias2), ("dp", "mp"))
    return (
        block_out,
        grad_input,
        grad_qkv,
        grad_proj,
        grad_up,
        grad_down,
        norm_totals[0],
        norm_totals[1],
        norm_totals[2],
        norm_totals[3],
    )


def solution(mesh):
    return jax.shard_map(
        on_device,
        mesh=mesh,
        in_specs=(
            P(("dp", "mp"), None),
            P(("dp", "mp"), None),
            P(("dp", "mp"), None),
            P("dp"),
            P("dp", None),
            P("dp", None),
            P("dp", "mp"),
            P("mp", "dp"),
            P(),
            P(),
            P(),
            P(),
        ),
        out_specs=(
            P(("dp", "mp"), None),
            P(("dp", "mp"), None),
            P("dp", None),
            P("dp", None),
            P("dp", "mp"),
            P("mp", "dp"),
            P(),
            P(),
            P(),
            P(),
        ),
        check_vma=False,
    )
```

profile of v0, /device:TPU:0, one launch (start us, length us, event | category | flops | bytes accessed | tf_op | source)
XLA Modules:
  0.0 1091.6 jit_solution(17617461324383245413)
XLA Ops:
  7.3 0.7 all-gather.7.cloned.1.call-update
  8.0 0.7 all-gather.9.cloned.1.call-update
  8.8 0.7 all-gather.13.cloned.1.call-update
  9.5 1.7 convert_reduce_fusion.1
  11.2 0.6 fusion.64
  12.5 1.0 fusion.93
  13.5 77.9 %all-gather.7.cloned.1.call-done = bf16[1536,4608]{1,0:T(8,128)(2,1)} async-done(((bf16[192,4608]{1,0:T(8,128)(2,1)}), bf16[1536,4608]{1,0:T(8,128)(2,1)}) %all-gather.7.cloned.1.call-update) | async-done | bytes 14155792 | tf_op jit(solution)/shard_map/all_gather | solution.py:64
  91.5 10.8 fusion.115
  102.4 0.7 slice_bitcast_fusion
  103.1 1.3 slice_negate_fusion.2
  104.5 2.4 copy-done.6
  106.9 1.8 fusion.70
  108.7 2.3 fusion.19
  111.1 2.6 fusion.18
  113.8 1.9 copy-done.2
  115.7 0.6 copy-done.25
  116.3 5.9 fusion.78
  122.2 10.1 all-gather.9.cloned.1.call-done
  132.3 4.8 fusion.122
  137.6 0.9 copy-done.39
  138.8 0.6 copy-done.33
  139.3 1.7 add_convert_fusion.1
  142.5 30.7 %all-gather.13.cloned.1.call-done = bf16[1536,1536]{1,0:T(8,128)(2,1)} async-done(((bf16[192,1536]{1,0:T(8,128)(2,1)}), bf16[1536,1536]{1,0:T(8,128)(2,1)}) %all-gather.13.cloned.1.call-update) | async-done | bytes 4718608 | tf_op jit(solution)/shard_map/all_gather | solution.py:68
  173.1 117.4 %all-gather.11.cloned.1.call-done = bf16[2048,1536]{1,0:T(8,128)(2,1)} async-done(((bf16[512,1536]{1,0:T(8,128)(2,1)}), bf16[2048,1536]{1,0:T(8,128)(2,1)}) %all-gather.11.cloned.1.call-update) | async-done | bytes 6291472 | tf_op jit(solution)/shard_map/all_gather | solution.py:121
  290.5 41.9 %fusion.1 = (bf16[2048,1536]{1,0:T(8,128)(2,1)}, f32[2048,1536]{1,0:T(8,128)}) fusion(s32[1536]{0:T(1024)S(1)} %iota_add_fusion, s32[2048]{0:T(1024)S(1)} %select_reduce_fusion, bf16[2048,1536]{1,0:T(8,128)(2,1)} %all-gather.11.cloned.1.call-done, bf16[1536,1536]{1,0:T(8,128)(2,1)} %all-gather.13.cloned.1.call-done), kind=kOutput, calls=%fused_computation.6 | convolution fusion | flops 9874440192 | bytes 29898752 | tf_op jit(solution)/shard_map/dot_general | solution.py:122
  332.4 113.9 %all-gather.17.cloned.1.call-done = bf16[2048,1536]{1,0:T(8,128)(2,1)} async-done(((bf16[512,1536]{1,0:T(8,128)(2,1)}), bf16[2048,1536]{1,0:T(8,128)(2,1)}) %all-gather.17.cloned.1.call-update) | async-done | bytes 6291472 | tf_op jit(solution)/shard_map/all_gather | solution.py:134
  446.3 17.5 %fusion.3 = bf16[2048,1536]{1,0:T(8,128)(2,1)S(1)} fusion(f32[2048,1536]{1,0:T(8,128)} %get-tuple-element.49, bf16[2048,1536]{1,0:T(8,128)(2,1)} %all-gather.17.cloned.1.call-done, bf16[1536,1536]{0,1:T(8,128)(2,1)} %all-gather.15.cloned.1.call-done, s32[1536]{0:T(1024)S(1)} %iota_add_fusion, s32[2048]{0:T(1024)S(1)} %select_reduce_fusion), kind=kOutput, calls=%fused_computation.8 | convolution fusion | flops 9701425152 | bytes 29898752 | tf_op jit(solution)/shard_map/dot_general | solution.py:135
  463.8 2.6 copy-done.49
  466.4 12.7 %convolution_convert_fusion.2 = bf16[2048,1536]{1,0:T(8,128)(2,1)} fusion(bf16[2048,1536]{1,0:T(8,128)(2,1)S(1)} %fusion.3, bf16[1536,1536]{1,0:T(8,128)(2,1)S(1)} %copy-done.45), kind=kOutput, calls=%fused_computation.40 | convolution fusion | flops 9666822144 | bytes 17301504 | tf_op jit(solution)/shard_map/dot_general | solution.py:150
  479.2 15.1 %convolution_convert_fusion.3 = bf16[2048,1536]{1,0:T(8,128)(2,1)} fusion(bf16[2048,1536]{1,0:T(8,128)(2,1)} %get-tuple-element.48, bf16[1536,1536]{0,1:T(8,128)(2,1)} %all-gather.15.cloned.1.call-done), kind=kOutput, calls=%fused_computation.41 | convolution fusion | flops 9666822144 | bytes 17301504 | tf_op jit(solution)/shard_map/dot_general | solution.py:127
  494.3 15.5 %convolution_convert_fusion.4 = bf16[1536,1536]{0,1:T(8,128)(2,1)} fusion(bf16[2048,1536]{1,0:T(8,128)(2,1)} %get-tuple-element.48, bf16[2048,1536]{1,0:T(8,128)(2,1)} %all-gather.17.cloned.1.call-done), kind=kOutput, calls=%fused_computation.42 | convolution fusion | flops 9666035712 | bytes 17301504 | tf_op jit(solution)/shard_map/dot_general | solution.py:142
  509.9 16.1 %convolution_convert_fusion.5 = bf16[1536,1536]{1,0:T(8,128)(2,1)} fusion(bf16[2048,1536]{1,0:T(8,128)(2,1)} %all-gather.11.cloned.1.call-done, bf16[2048,1536]{1,0:T(8,128)(2,1)} %copy-done.49), kind=kOutput, calls=%fused_computation.43 | convolution fusion | flops 9666035712 | bytes 17301504 | tf_op jit(solution)/shard_map/dot_general | solution.py:145
  526.1 62.2 %reduce-scatter.9.cloned.1.call-done = bf16[512,1536]{1,0:T(8,128)(2,1)} async-done(((bf16[2048,1536]{1,0:T(8,128)(2,1)}), bf16[512,1536]{1,0:T(8,128)(2,1)}) %reduce-scatter.9.cloned.1.call-update) | async-done | bytes 1572880 | tf_op jit(solution)/shard_map/reduce_scatter | solution.py:149
  588.3 2.5 fusion.66
  590.7 111.1 %reduce-scatter.7.cloned.1.call-done = bf16[512,1536]{1,0:T(8,128)(2,1)} async-done(((bf16[2048,1536]{1,0:T(8,128)(2,1)}), bf16[512,1536]{1,0:T(8,128)(2,1)}) %reduce-scatter.7.cloned.1.call-update) | async-done | bytes 1572880 | tf_op jit(solution)/shard_map/reduce_scatter | solution.py:126
  701.9 3.7 fusion.119
  705.6 1.7 copy-done.5
  708.1 4.3 convolution_convert_fusion.1
  712.5 0.7 copy-done.24
  713.3 6.8 convolution_convert_fusion.6
  720.1 1.7 copy.48
  721.8 8.7 fusion.89
  730.5 20.8 %fusion.24 = f32[12,128,512]{2,1,0:T(8,128)} fusion(bf16[512,12,128]{0,2,1:T(8,128)(2,1)} %copy-done.13, f32[12,512,512]{1,2,0:T(8,128)} %fusion.89, f32[12,512,512]{1,2,0:T(8,128)} %copy-done.2, f32[12,512]{1,0:T(8,128)S(1)} %log_add_fusion, pred[512,512]{0,1:T(8,128)(4,1)} %copy-done.20), kind=kOutput, calls=%fused_computation.45 | convolution fusion | flops 839916032 | bytes 30171136 | tf_op jit(solution)/shard_map/hst,shd->thd/dot_general | solution.py:180
  751.3 24.3 %bitcast_multiply_fusion.2 = (f32[512,12,128]{0,2,1:T(8,128)}, f32[512,12,128]{0,2,1:T(8,128)}, f32[12,128,512]{2,1,0:T(8,128)}) fusion(f32[512,128]{0,1:T(8,128)S(1)} %copy-done.22, f32[12,128,512]{2,1,0:T(8,128)} %fusion.24, bf16[512,12,128]{0,2,1:T(8,128)(2,1)} %copy-done.12, f32[12,512,512]{1,2,0:T(8,128)} %fusion.89, f32[12,512,512]{1,2,0:T(8,128)} %copy-done.2, ...), kind=kOutput, calls=%fused_computation.99 | convolution fusion | flops 841488896 | bytes 39870464 | tf_op jit(solution)/shard_map/hst,thd->shd/dot_general | solution.py:177
  775.7 4.4 fusion.120
  780.1 2.1 fusion.121
  782.2 9.2 fusion.82
  791.5 4.4 fusion.85
  795.9 0.6 pad_maximum_fusion
  796.5 2.2 copy-done.14
  798.7 11.2 %convolution_convert_fusion = bf16[1536,4608]{1,0:T(8,128)(2,1)} fusion(bf16[512,4608]{0,1:T(8,128)(2,1)S(1)} %bitcast.85, bf16[512,1536]{1,0:T(8,128)(2,1)S(1)} %copy-done.4, f32[1536]{0:T(1024)S(1)} %copy-done.47, f32[1536]{0:T(1024)S(1)} %copy-done.32, f32[512]{0:T(512)S(1)} %copy-done.42, f32[512]{0:T(512)S(1)} %copy-done.36), kind=kOutput, calls=%fused_computation.1 | convolution fusion | flops 7259553792 | bytes 20463616 | tf_op jit(solution)/shard_map/dot_general | solution.py:186
  810.0 2.2 convert_element_type.131
  812.2 5.1 reduce-scatter.15.cloned.1.call-done
  817.4 2.2 convert_element_type.129
  819.6 55.1 %reduce-scatter.13.cloned.1.call-done = bf16[192,1536]{1,0:T(8,128)(2,1)} async-done(((bf16[1536,1536]{1,0:T(8,128)(2,1)}), bf16[192,1536]{1,0:T(8,128)(2,1)}) %reduce-scatter.13.cloned.1.call-update) | async-done | bytes 589840 | tf_op jit(solution)/shard_map/reduce_scatter | solution.py:206
  874.7 104.6 %reduce-scatter.11.cloned.1.call-done = bf16[192,4608]{1,0:T(8,128)(2,1)} async-done(((bf16[1536,4608]{1,0:T(8,128)(2,1)}), bf16[192,4608]{1,0:T(8,128)(2,1)}) %reduce-scatter.11.cloned.1.call-update) | async-done | bytes 1769488 | tf_op jit(solution)/shard_map/reduce_scatter | solution.py:203
  979.4 12.2 %fusion.118 = (f32[1536]{0:T(1024)S(1)}, f32[512]{0:T(512)S(1)}, f32[512,1536]{1,0:T(8,128)S(1)}) fusion(f32[1536]{0:T(1024)S(1)} %copy-done.32, f32[512]{0:T(512)S(1)} %copy-done.36, bf16[512,1536]{1,0:T(8,128)(2,1)S(1)} %copy-done.4, bf16[512,4608]{0,1:T(8,128)(2,1)} %bitcast.86, bf16[1536,4608]{1,0:T(8,128)(2,1)} %all-gather.7.cloned.1.call-done), kind=kOutput, calls=%fused_computation.169 | convolution fusion | flops 7252473856 | bytes 23609344 | tf_op jit(solution)/shard_map/dot_general | solution.py:189
  991.7 1.6 copy-done.9
  993.3 1.4 fusion.62
  994.7 43.7 %all-reduce.4 = (f32[1536]{0:T(1024)}, f32[1536]{0:T(1024)}, f32[1536]{0:T(1024)}, f32[1536]{0:T(1024)}) all-reduce(f32[1536]{0:T(1024)S(1)} %get-tuple-element.10, f32[1536]{0:T(1024)S(1)} %get-tuple-element.14, f32[1536]{0:T(1024)S(1)} %get-tuple-element.12, ...), channel_id=1, replica_groups=mesh['dp'=8,'mp'=4] {'dp','mp'}, use_global_device_ids=true, to_apply=%region_21.22 | all-reduce | flops 6144 | bytes 49152 | tf_op jit(solution)/shard_map/psum | solution.py:214
  1038.4 4.8 add_add_fusion.2
  1043.2 35.8 %all-reduce.8.cloned.1.call-done = (bf16[192,4608]{1,0:T(8,128)(2,1)}, bf16[192,1536]{1,0:T(8,128)(2,1)}) async-done(((bf16[192,4608]{1,0:T(8,128)(2,1)}, bf16[192,1536]{1,0:T(8,128)(2,1)}), (bf16[192,4608]{1,0:T(8,128)(2,1)}, bf16[192,1536]{1,0:T(8,128)(2,1)})) %all-reduce.8.cloned.1.call-update) | async-done | bytes 2359312 | tf_op jit(solution)/shard_map/psum | solution.py:211
  1079.0 2.2 convert_element_type.127
  1081.2 3.7 convert_element_type.125
  (140 shorter events, 4.4 us)
Async XLA Ops:
  7.2 4.0 copy-start.3
  7.2 5.1 copy-start.44
  7.2 84.3 %copy-start.31 = (f32[1536]{0:T(1024)S(1)}, f32[1536]{0:T(1024)}, u32[]{:S(2)}) copy-start(f32[1536]{0:T(1024)} %param.20) | copy-start | bytes 18436
  7.2 84.3 %copy-start.46 = (f32[1536]{0:T(1024)S(1)}, f32[1536]{0:T(1024)}, u32[]{:S(2)}) copy-start(f32[1536]{0:T(1024)} %param.21) | copy-start | bytes 18436
  7.2 84.2 %all-gather.7.cloned.1.call-start = ((), (), s32[]{:S(2)}) async-start(), calls=%async_computation.6 | async-start | bytes 15925248 | tf_op jit(solution)/shard_map/all_gather | solution.py:64
  8.0 124.3 %all-gather.9.cloned.1.call-start = ((), (), s32[]{:S(2)}) async-start(), calls=%async_computation.7 | async-start | bytes 5308416 | tf_op jit(solution)/shard_map/all_gather | solution.py:65
  8.7 164.4 %all-gather.13.cloned.1.call-start = ((), (), s32[]{:S(2)}) async-start(), calls=%async_computation.9 | async-start | bytes 5308416 | tf_op jit(solution)/shard_map/all_gather | solution.py:68
  9.4 281.1 %all-gather.11.cloned.1.call-start = ((), (), s32[]{:S(2)}) async-start(), calls=%async_computation.8 | async-start | bytes 7864320 | tf_op jit(solution)/shard_map/all_gather | solution.py:121
  11.2 91.1 %copy-start.35 = (f32[512]{0:T(512)}, f32[512]{0:T(512)S(1)}, u32[]{:S(2)}) copy-start(f32[512]{0:T(512)S(1)} %broadcast_multiply_fusion.1) | copy-start | bytes 6148
  11.8 90.5 %copy-start.41 = (f32[512]{0:T(512)}, f32[512]{0:T(512)S(1)}, u32[]{:S(2)}) copy-start(f32[512]{0:T(512)S(1)} %fusion.97) | copy-start | bytes 6148
  12.5 101.2 %copy-start.20 = (pred[512,512]{0,1:T(8,128)(4,1)}, pred[512,512]{0,1:T(8,128)(4,1)S(1)}, u32[]{:S(2)}) copy-start(pred[512,512]{0,1:T(8,128)(4,1)S(1)} %fusion.88) | copy-start | bytes 786436
  13.5 90.9 %copy-start.18 = (f32[512,128]{0,1:T(8,128)}, f32[512,128]{0,1:T(8,128)S(1)}, u32[]{:S(2)}) copy-start(f32[512,128]{0,1:T(8,128)S(1)} %get-tuple-element.42) | copy-start | bytes 786436
  13.5 90.9 %copy-start.21 = (f32[512,128]{0,1:T(8,128)}, f32[512,128]{0,1:T(8,128)S(1)}, u32[]{:S(2)}) copy-start(f32[512,128]{0,1:T(8,128)S(1)} %get-tuple-element.43) | copy-start | bytes 786436
  102.3 4.5 copy-start.6
  108.7 2.4 copy-start.12
  108.7 2.4 copy-start.13
  111.1 4.6 copy-start.2
  111.1 4.6 copy-start.23
  115.7 0.6 copy-start.25
  122.2 14.9 %copy-start.16 = (bf16[12,128,512]{2,1,0:T(8,128)(2,1)}, bf16[12,128,512]{2,1,0:T(8,128)(2,1)S(1)}, u32[]{:S(2)}) copy-start(bf16[12,128,512]{2,1,0:T(8,128)(2,1)S(1)} %fusion.78) | copy-start | bytes 4718596
  132.3 7.1 copy-start.27
  132.3 7.1 copy-start.43
  137.1 1.7 copy-start
  137.1 1.6 copy-start.29
  137.6 0.9 copy-start.39
  138.5 3.8 copy-start.48
  141.1 191.3 %all-gather.15.cloned.1.call-start = ((), (), s32[]{:S(2)}) async-start(), calls=%async_computation.10 | async-start | bytes 5308416 | tf_op jit(solution)/shard_map/all_gather | solution.py:69
  141.7 304.6 %all-gather.17.cloned.1.call-start = ((), (), s32[]{:S(2)}) async-start(), calls=%async_computation.12 | async-start | bytes 7864320 | tf_op jit(solution)/shard_map/all_gather | solution.py:134
  142.3 446.0 %reduce-scatter.9.cloned.1.call-start = ((), (), s32[]{:S(2)}) async-start(), calls=%async_computation.13 | async-start | bytes 7864320 | tf_op jit(solution)/shard_map/reduce_scatter | solution.py:149
  446.3 20.1 %copy-start.45 = (bf16[1536,1536]{1,0:T(8,128)(2,1)S(1)}, bf16[1536,1536]{1,0:T(8,128)(2,1)}, u32[]{:S(2)}) copy-start(bf16[1536,1536]{1,0:T(8,128)(2,1)} %all-gather.13.cloned.1.call-done) | copy-start | bytes 14155780
  463.8 2.6 copy-start.49
  479.1 222.7 %reduce-scatter.7.cloned.1.call-start = ((), (), s32[]{:S(2)}) async-start(), calls=%async_computation.11 | async-start | bytes 7864320 | tf_op jit(solution)/shard_map/reduce_scatter | solution.py:126
  494.3 315.8 %reduce-scatter.17.cloned.1.call-start = ((), (), s32[]{:S(2)}) async-start(), calls=%async_computation.17 | async-start | bytes 5308416 | tf_op jit(solution)/shard_map/reduce_scatter | solution.py:198
  509.8 307.5 %reduce-scatter.15.cloned.1.call-start = ((), (), s32[]{:S(2)}) async-start(), calls=%async_computation.16 | async-start | bytes 5308416 | tf_op jit(solution)/shard_map/reduce_scatter | solution.py:195
  526.0 62.3 %copy-start.1 = (f32[512,1536]{1,0:T(8,128)S(1)}, f32[512,1536]{1,0:T(8,128)}, u32[]{:S(2)}) copy-start(f32[512,1536]{1,0:T(8,128)} %copy-done) | copy-start | bytes 9437188
  526.0 62.3 %copy-start.28 = (f32[1536]{0:T(1024)S(1)}, f32[1536]{0:T(1024)}, u32[]{:S(2)}) copy-start(f32[1536]{0:T(1024)} %param.22) | copy-start | bytes 18436
  526.0 62.3 %copy-start.30 = (f32[512]{0:T(512)S(1)}, f32[512]{0:T(512)}, u32[]{:S(2)}) copy-start(f32[512]{0:T(512)} %copy-done.29) | copy-start | bytes 6148
  526.0 62.3 %copy-start.34 = (f32[512]{0:T(512)S(1)}, f32[512]{0:T(512)}, u32[]{:S(2)}) copy-start(f32[512]{0:T(512)} %copy-done.33) | copy-start | bytes 6148
  526.0 64.7 %copy-start.40 = (f32[512]{0:T(512)S(1)}, f32[512]{0:T(512)}, u32[]{:S(2)}) copy-start(f32[512]{0:T(512)} %copy-done.39) | copy-start | bytes 6148
  526.0 348.7 %reduce-scatter.13.cloned.1.call-start = ((), (), s32[]{:S(2)}) async-start(), calls=%async_computation.15 | async-start | bytes 5308416 | tf_op jit(solution)/shard_map/reduce_scatter | solution.py:206
  701.9 5.4 copy-start.7
  705.6 1.7 copy-start.5
  705.6 2.5 copy-start.17
  712.5 0.8 copy-start.24
  712.5 0.8 copy-start.26
  712.5 266.9 %reduce-scatter.11.cloned.1.call-start = ((), (), s32[]{:S(2)}) async-start(), calls=%async_computation.14 | async-start | bytes 15925248 | tf_op jit(solution)/shard_map/reduce_scatter | solution.py:203
  730.5 20.8 %copy-start.22 = (f32[512,128]{0,1:T(8,128)S(1)}, f32[512,128]{0,1:T(8,128)}, u32[]{:S(2)}) copy-start(f32[512,128]{0,1:T(8,128)} %copy-done.21) | copy-start | bytes 786436
  775.6 4.4 copy-start.15
  775.7 15.8 %slice-start = ((s8[12582912]{0:T(1024)(128)(4,1)}), s8[4194304]{0:T(1024)(128)(4,1)S(1)}, s32[]{:S(2)}) async-start(s8[12582912]{0:T(1024)(128)(4,1)} %bitcast.77), calls=%async_computation.19 | async-start | bytes 8388608
  780.1 2.1 copy-start.19
  780.1 11.4 %slice-start.1 = ((s8[12582912]{0:T(1024)(128)(4,1)}), s8[4194304]{0:T(1024)(128)(4,1)S(1)}, s32[]{:S(2)}) async-start(s8[12582912]{0:T(1024)(128)(4,1)} %bitcast.77), calls=%async_computation.20 | async-start | bytes 8388608
  782.2 9.2 slice-start.2
  791.5 4.4 copy-start.10
  791.5 4.4 copy-start.11
  795.9 2.9 copy-start.4
  795.9 2.9 copy-start.32
  795.9 2.9 copy-start.36
  795.9 2.8 copy-start.42
  795.9 2.8 copy-start.47
  796.5 2.2 copy-start.14
  810.0 269.0 %all-reduce.8.cloned.1.call-start = ((), (), s32[]{:S(2)}) async-start(), calls=%async_computation.18 | async-start | bytes 4718592 | tf_op jit(solution)/shard_map/psum | solution.py:211
  979.4 12.3 %copy-start.38 = (f32[512]{0:T(512)S(1)}, f32[512]{0:T(512)}, u32[]{:S(2)}) copy-start(f32[512]{0:T(512)} %copy-done.37) | copy-start | bytes 6148
  991.7 1.7 copy-start.9
  991.7 46.8 %copy-start.8 = (bf16[512,1536]{1,0:T(8,128)(2,1)S(1)}, bf16[512,1536]{1,0:T(8,128)(2,1)}, u32[]{:S(2)}) copy-start(bf16[512,1536]{1,0:T(8,128)(2,1)} %param.13) | copy-start | bytes 4718596
  (2 other events, 1.1 us)
Sparse Core Ops, SparseCore 0:
  9.9 81.4 all-gather.6
  93.3 38.9 all-gather.8
  134.2 38.9 all-gather.12
  175.1 115.3 all-gather.10
  292.2 37.1 all-gather.14
  330.9 115.3 all-gather.16
  479.2 108.9 reduce-scatter.8
  590.5 111.2 reduce-scatter.6
  705.3 54.3 reduce-scatter.16
  763.4 53.9 reduce-scatter.14
  820.8 53.8 reduce-scatter.12
  878.6 100.7 reduce-scatter.10
  981.9 96.9 all-reduce.7
where the time goes:
time: 1100 us; the launch traced here: 1090 us
  waiting for transfers between devices  727 us (66%)
  matrix products  235 us (21%)
  other arithmetic  51 us (5%)
  blocking collectives  43.7 us (4%)
  local copies, waits for them, and re-layouts  19.1 us (2%)
  between operations  14.8 us (1%)
    all_gather x1, waiting for transfers between devices, on_device(): piece_rows = lax.all_gather(normed2_low, 'mp', axis=0, tiled=True)  117 us
    all_gather x1, waiting for transfers between devices, on_device(): piece_rows = lax.all_gather(cotangent, 'mp', axis=0, tiled=True)  114 us
    reduce_scatter x1, waiting for transfers between devices, on_device(): lax.psum_scatter(jnp.dot(block_rows, wide_down, preferred_element_type=jn...  111 us
    reduce_scatter x1, waiting for transfers between devices, on_device(): lax.psum_scatter(grad_qkv_local.astype(jnp.bfloat16), 'dp', scatter_dimen...  105 us
    all_gather x1, waiting for transfers between devices, on_device(): lax.all_gather(w_qkv, 'dp', axis=0, tiled=True)  77.9 us
    reduce_scatter x1, waiting for transfers between devices, on_device(): lax.psum_scatter(lax.dot_general(block_rows, wide_up, contract_cols, pref...  62.2 us
    reduce_scatter x1, waiting for transfers between devices, on_device(): lax.psum_scatter(grad_out_local.astype(jnp.bfloat16), 'dp', scatter_dimen...  55.1 us
    psum x1, blocking collectives, on_device(): lax.psum((grad_gain1, grad_bias1, grad_gain2, grad_bias2), ('dp', 'mp'))  43.7 us
  transfers between devices with their start and end apart: 13, of which 11 were waited for; matrix products, arithmetic and copies ran while one was open for 23% of the time, Pallas kernels for 0%

commit v1 on v0

v1 whole, which is shorter than its diff:
```python
import functools

import jax
import jax.numpy as jnp
from jax import lax
from jax.experimental import pallas as pl
from jax.experimental.pallas import tpu as pltpu
from jax.sharding import PartitionSpec as P

HEADS = 12
HEAD_DIM = 128
BLOCK = 768
AXES = ("dp", "mp")
PAIR = 2

epsilon = 1e-05
theta_base = 10000.0
score_scale = HEAD_DIM ** (-0.5)
contract_rows = (((0,), (0,)), ((), ()))
contract_cols = (((1,), (1,)), ((), ()))
f32 = jnp.float32
bf16 = jnp.bfloat16
VMEM_LIMIT = 56 * 1024 * 1024


def layer_norm_stats(values):
    average = jnp.mean(values, axis=-1, keepdims=True)
    centred = values - average
    variance = jnp.mean(centred * centred, axis=-1, keepdims=True)
    inverse = lax.rsqrt(variance + epsilon)
    return average, inverse


def layer_norm_back(q, normal, inverse, gain):
    c = q * gain
    mean_c = jnp.mean(c, axis=-1, keepdims=True)
    mean_cn = jnp.mean(c * normal, axis=-1, keepdims=True)
    return (c - mean_c - normal * mean_cn) * inverse


def rotary_tables(length, head_width):
    halfway = head_width // 2
    frequency = theta_base ** (-2.0 * jnp.arange(halfway, dtype=f32) / head_width)
    angles = jnp.arange(length, dtype=f32)[:, None] * frequency[None, :]
    angles = jnp.concatenate([angles, angles], axis=1)
    return (jnp.cos(angles), jnp.sin(angles))


def turn(values):
    halfway = values.shape[-1] // 2
    return jnp.concatenate([-values[:, halfway:], values[:, :halfway]], axis=-1)


def turn_back(values):
    halfway = values.shape[-1] // 2
    return jnp.concatenate([values[:, halfway:], -values[:, :halfway]], axis=-1)


def allowed_block(seg_col, seg_row, row_start, block, extent):
    row_place = row_start + lax.broadcasted_iota(jnp.int32, (block, extent), 0)
    col_place = lax.broadcasted_iota(jnp.int32, (block, extent), 1)
    return (row_place >= col_place) & (seg_col == seg_row)


def attend_kernel(chips, seq_len, offs_ref, norm_ref, cos_ref, sin_ref, segc_ref, segr_ref, *refs):
    pieces = refs[:chips]
    wide_ref, qkv_ref, ctx_ref, lse_ref = refs[chips:]
    span = pieces[0].shape[0]
    for j in range(chips):
        wide_ref[pl.ds(pl.multiple_of(offs_ref[j], span), span), :] = pieces[j][...]
    hd = HEAD_DIM
    block = seq_len // 2

    def project(i, carry):
        start = pl.multiple_of(i * block, block)
        rows = pl.ds(start, block)
        joined = jnp.dot(norm_ref[rows, :], wide_ref[...], preferred_element_type=f32)
        table = pl.ds(pl.multiple_of((i % 2) * block, block), block)
        cosine, sine = cos_ref[table, :], sin_ref[table, :]
        for h in range(2 * PAIR):
            part = joined[:, h * hd : (h + 1) * hd]
            qkv_ref[rows, h * hd : (h + 1) * hd] = (part * cosine + turn(part) * sine).astype(bf16)
        qkv_ref[rows, 2 * PAIR * hd :] = joined[:, 2 * PAIR * hd :].astype(bf16)
        return carry

    lax.fori_loop(0, 4, project, 0)

    lane = lax.broadcasted_iota(jnp.int32, (block, hd), 1)

    def sequence(s, carry):
        base = s * seq_len
        for r in range(2):
            extent = (r + 1) * block
            rows = pl.ds(pl.multiple_of(base + r * block, block), block)
            cols = pl.ds(pl.multiple_of(base, block), extent)
            allowed = allowed_block(
                segc_ref[s, r * block : (r + 1) * block, :],
                segr_ref[s, :, :extent],
                r * block,
                block,
                extent,
            )
            logs = jnp.zeros((block, hd), f32)
            for h in range(PAIR):
                query = qkv_ref[rows, h * hd : (h + 1) * hd]
                key = qkv_ref[cols, (PAIR + h) * hd : (PAIR + h + 1) * hd]
                value = qkv_ref[cols, (2 * PAIR + h) * hd : (2 * PAIR + h + 1) * hd]
                scores = lax.dot_general(query, key, contract_cols, preferred_element_type=f32)
                scores = jnp.where(allowed, scores * score_scale, -1000000000.0)
                top = jnp.max(scores, axis=-1, keepdims=True)
                weight = jnp.exp(scores - top)
                total = jnp.sum(weight, axis=-1, keepdims=True)
                probs = (weight * (1.0 / total)).astype(bf16)
                ctx_ref[rows, h * hd : (h + 1) * hd] = jnp.dot(
                    probs, value, preferred_element_type=f32
                ).astype(bf16)
                logs = jnp.where(lane == h, top + jnp.log(total), logs)
            lse_ref[rows, :] = logs
        return carry

    lax.fori_loop(0, 2, sequence, 0)


def attend_back_kernel(seq_len, qkv_ref, lse_ref, grad_ref, cos_ref, sin_ref, segc_ref, segr_ref, out_ref, gq, gk, gv):
    hd = HEAD_DIM
    block = seq_len // 2

    def sequence(s, carry):
        base = s * seq_len
        for h in range(PAIR):
            for r in (1, 0):
                extent = (r + 1) * block
                rows = pl.ds(pl.multiple_of(base + r * block, block), block)
                cols = pl.ds(pl.multiple_of(base, block), extent)
                allowed = allowed_block(
                    segc_ref[s, r * block : (r + 1) * block, :],
                    segr_ref[s, :, :extent],
                    r * block,
                    block,
                    extent,
                )
                query = qkv_ref[rows, h * hd : (h + 1) * hd]
                key = qkv_ref[cols, (PAIR + h) * hd : (PAIR + h + 1) * hd]
                value = qkv_ref[cols, (2 * PAIR + h) * hd : (2 * PAIR + h + 1) * hd]
                grad = grad_ref[rows, h * hd : (h + 1) * hd]
                scores = lax.dot_general(query, key, contract_cols, preferred_element_type=f32)
                scores = jnp.where(allowed, scores * score_scale, -1000000000.0)
                probs = jnp.exp(scores - lse_ref[rows, h : h + 1])
                grad_probs = lax.dot_general(grad, value, contract_cols, preferred_element_type=f32)
                weighted = jnp.sum(probs * grad_probs, axis=-1, keepdims=True)
                grad_scores = (probs * (grad_probs - weighted) * score_scale).astype(bf16)
                probs = probs.astype(bf16)
                gq[r * block : (r + 1) * block, :] = jnp.dot(grad_scores, key, preferred_element_type=f32)
                grad_key = lax.dot_general(grad_scores, query, contract_rows, preferred_element_type=f32)
                grad_value = lax.dot_general(probs, grad, contract_rows, preferred_element_type=f32)
                if r == 1:
                    gk[...] = grad_key
                    gv[...] = grad_value
                else:
                    gk[:block, :] = gk[:block, :] + grad_key
                    gv[:block, :] = gv[:block, :] + grad_value
            sine, cosine = sin_ref[...], cos_ref[...]
            rows = pl.ds(pl.multiple_of(base, seq_len), seq_len)
            grad_query, grad_key = gq[...], gk[...]
            out_ref[rows, h * hd : (h + 1) * hd] = (
                grad_query * cosine + turn_back(grad_query * sine)
            ).astype(bf16)
            out_ref[rows, (PAIR + h) * hd : (PAIR + h + 1) * hd] = (
                grad_key * cosine + turn_back(grad_key * sine)
            ).astype(bf16)
            out_ref[rows, (2 * PAIR + h) * hd : (2 * PAIR + h + 1) * hd] = gv[...].astype(bf16)
        return carry

    lax.fori_loop(0, 2, sequence, 0)


SMEM_SPEC = pl.BlockSpec(memory_space=pltpu.SMEM)
VMEM_SPEC = pl.BlockSpec(memory_space=pltpu.VMEM)


def attend(offsets, normed, cosine, sine, seg_col, seg_row, pieces):
    chips = len(pieces)
    rows, width = normed.shape
    cols = pieces[0].shape[1]
    return pl.pallas_call(
        functools.partial(attend_kernel, chips, rows // 2),
        out_shape=(
            jax.ShapeDtypeStruct((width, cols), bf16),
            jax.ShapeDtypeStruct((rows, cols), bf16),
            jax.ShapeDtypeStruct((rows, PAIR * HEAD_DIM), bf16),
            jax.ShapeDtypeStruct((rows, HEAD_DIM), f32),
        ),
        in_specs=[SMEM_SPEC] + [VMEM_SPEC] * (5 + chips),
        out_specs=(VMEM_SPEC,) * 4,
        compiler_params=pltpu.CompilerParams(vmem_limit_bytes=VMEM_LIMIT),
        name="attend",
    )(offsets, normed, cosine, sine, seg_col, seg_row, *pieces)


def attend_back(qkv, lse, grad, cosine, sine, seg_col, seg_row):
    rows, cols = qkv.shape
    seq_len = rows // 2
    return pl.pallas_call(
        functools.partial(attend_back_kernel, seq_len),
        out_shape=jax.ShapeDtypeStruct((rows, cols), bf16),
        in_specs=[VMEM_SPEC] * 7,
        out_specs=VMEM_SPEC,
        scratch_shapes=[pltpu.VMEM((seq_len, HEAD_DIM), f32)] * 3,
        compiler_params=pltpu.CompilerParams(vmem_limit_bytes=VMEM_LIMIT),
        name="attend_back",
    )(qkv, lse, grad, cosine, sine, seg_col, seg_row)


def tie(value, *others):
    return lax.optimization_barrier((value, *others))[0]


def build(dp_size, mp_size):
    total = dp_size * mp_size
    chip_bits = []
    bit = 2 * mp_size
    while bit < total:
        chip_bits.append(bit)
        bit *= 2
    core_bit = mp_size
    near_bit = 1
    far_bits = []
    bit = 2
    while bit < mp_size:
        far_bits.append(bit)
        bit *= 2
    chips = dp_size // 2

    def flip(value, bit):
        return lax.ppermute(value, AXES, [(i, i ^ bit) for i in range(total)])

    def gather_chips(piece, way):
        if len(chip_bits) == 2:
            first, second = chip_bits
            from_x = flip(piece, first)
            from_y = flip(piece, second)
            corner = flip(from_x, second) if way == 0 else flip(from_y, first)
            return [piece, from_x, from_y, corner]
        held = [piece]
        for bit in chip_bits:
            held = held + [flip(value, bit) for value in held]
        return held

    def add(a, b):
        return a.astype(f32) + b.astype(f32)

    def scatter_chips(pieces, way):
        if len(chip_bits) == 2:
            first, second = chip_bits
            own, to_x, to_y, corner = pieces
            if way == 0:
                to_y = add(to_y, flip(corner, first)).astype(bf16)
            else:
                to_x = add(to_x, flip(corner, second)).astype(bf16)
            return own.astype(f32) + flip(to_x, first).astype(f32) + flip(to_y, second).astype(f32)
        held = list(pieces)
        for bit in reversed(chip_bits):
            middle = len(held) // 2
            low, high = held[:middle], held[middle:]
            held = [add(a, flip(b.astype(bf16), bit)) for a, b in zip(low, high)]
        return held[0].astype(f32)

    def on_device(
        block_in,
        cotangent,
        segment_ids,
        granularity,
        w_qkv,
        w_out,
        w_up,
        w_down,
        norm1_gain,
        norm1_bias,
        norm2_gain,
        norm2_bias,
    ):
        seq_len, width = block_in.shape
        rows = width // dp_size
        units = w_up.shape[1]
        half_units = units // 2
        dp = lax.axis_index("dp")
        mp = lax.axis_index("mp")
        core = dp % 2
        chip = dp // 2
        span = 2 * rows
        offsets = jnp.stack([(chip ^ j) * span for j in range(chips)]).astype(jnp.int32)
        core_heads = HEADS // 2
        chunks = core_heads // PAIR
        chunk_cols = 3 * PAIR * HEAD_DIM

        def chip_order(value):
            return jnp.concatenate(
                [lax.dynamic_slice_in_dim(value, offsets[j], span, axis=1) for j in range(chips)],
                axis=1,
            )

        def by_core(own, other):
            return jnp.where(core == 0, own, other), jnp.where(core == 0, other, own)

        def both_rows(own, other):
            return jnp.concatenate(list(by_core(own, other)), axis=0)

        shard = w_qkv.reshape(rows, 3, 2, chunks, PAIR * HEAD_DIM)
        keep, send = by_core(shard[:, :, 0], shard[:, :, 1])
        other_in = flip(block_in, core_bit)
        got = flip(send, core_bit)
        qkv_pieces = []
        for p in range(chunks):
            own_p = both_rows(keep[:, :, p], got[:, :, p]).reshape(span, chunk_cols)
            qkv_pieces.append(gather_chips(own_p, p % 2))

        small = jnp.concatenate([segment_ids, jnp.broadcast_to(granularity[:, None], (mp_size, seq_len))])
        small_other = flip(small, core_bit)
        segments = jnp.stack([small[0], small_other[0]])
        levels = jnp.concatenate([small[1:, 0], small_other[1:, 0]])
        seg_col = segments[:, :, None]
        seg_row = segments[:, None, :]
        cosine, sine = rotary_tables(seq_len, HEAD_DIM)

        out_pieces = gather_chips(w_out, 1)
        out_others = [flip(v, core_bit) for v in out_pieces]
        wide_out = jnp.concatenate([both_rows(a, b) for a, b in zip(out_pieces, out_others)], axis=0)

        pair = jnp.stack([w_up, w_down.T])
        keep, send = by_core(pair[:, :, :half_units], pair[:, :, half_units:])
        got = flip(send, core_bit)
        mine = jnp.concatenate(list(by_core(keep, got)), axis=1).reshape(2 * span, half_units)
        slices = [mine]
        for bit in far_bits:
            slices = slices + [flip(v, bit) for v in slices]
        cot_z = flip(cotangent, near_bit)
        cot_rows = [cotangent, flip(cotangent, core_bit), cot_z, flip(cot_z, core_bit)]
        cot_rows = chip_order(jnp.concatenate(cot_rows, axis=0))
        up_blocks, down_blocks = [], []
        for k, v in enumerate(slices):
            got = gather_chips(v, k % 2)
            up_blocks.append(jnp.concatenate([g[:span] for g in got], axis=0))
            down_blocks.append(jnp.concatenate([g[span:] for g in got], axis=0))

        inputs = block_in.astype(f32)
        average1, inverse1 = layer_norm_stats(inputs)
        normal1 = (inputs - average1) * inverse1
        other_inputs = other_in.astype(f32)
        other_average, other_inverse = layer_norm_stats(other_inputs)
        other_normal = (other_inputs - other_average) * other_inverse
        normed1 = jnp.concatenate(
            [
                (normal1 * norm1_gain + norm1_bias).astype(bf16),
                (other_normal * norm1_gain + norm1_bias).astype(bf16),
            ]
        )
        qkv_wide, qkv_low, contexts, logs = [], [], [], []
        for p in range(chunks):
            a, b, c, d = attend(offsets, normed1, cosine, sine, seg_col, seg_row, qkv_pieces[p])
            qkv_wide.append(a)
            qkv_low.append(b)
            contexts.append(c)
            logs.append(d)
        context_mine = jnp.concatenate(contexts, axis=1)
        context_got = flip(context_mine[seq_len:], core_bit)
        context_low = jnp.concatenate(list(by_core(context_mine[:seq_len], context_got)), axis=1)
        hidden1 = inputs + jnp.dot(chip_order(context_low), wide_out, preferred_element_type=f32)
        average2, inverse2 = layer_norm_stats(hidden1)
        normal2 = (hidden1 - average2) * inverse2
        normed2_low = chip_order((normal2 * norm2_gain + norm2_bias).astype(bf16))

        norm_z = flip(normed2_low, near_bit)
        norm_rows = [normed2_low, flip(normed2_low, core_bit), norm_z, flip(norm_z, core_bit)]
        norm_rows = jnp.concatenate(norm_rows, axis=0)

        own_level = lax.dynamic_index_in_dim(levels, mp, keepdims=False)
        core_level = lax.dynamic_index_in_dim(levels, mp_size + mp, keepdims=False)
        near_level = lax.dynamic_index_in_dim(levels, mp ^ 1, keepdims=False)
        both_level = lax.dynamic_index_in_dim(levels, mp_size + (mp ^ 1), keepdims=False)
        limits = jnp.stack([own_level, core_level, near_level, both_level])
        limits = jnp.repeat(BLOCK * jnp.power(2, limits), seq_len)

        out_part = 0.0
        back_part = 0.0
        shares = []
        for k, (up_k, down_k) in enumerate(zip(up_blocks, down_blocks)):
            start = (mp ^ (2 * k)) * units + core * half_units
            unit_ids = start + jnp.arange(half_units)
            mask = (unit_ids[None, :] < limits[:, None]).astype(f32)
            preact = jnp.dot(norm_rows, up_k, preferred_element_type=f32)
            grad_active = jnp.dot(cot_rows, down_k, preferred_element_type=f32)
            cdf = 0.5 * (1.0 + lax.erf(preact * 0.7071067811865476))
            active = (preact * cdf * mask).astype(bf16)
            slope = cdf + preact * jnp.exp(-0.5 * preact * preact) * 0.3989422804014327
            grad_preact = (grad_active * mask * slope).astype(bf16)
            back_part = back_part + lax.dot_general(
                grad_preact, up_k, contract_cols, preferred_element_type=f32
            )
            out_part = out_part + lax.dot_general(
                active, down_k, contract_cols, preferred_element_type=f32
            )
            grad_up = lax.dot_general(
                norm_rows, grad_preact, contract_rows, preferred_element_type=f32
            ).astype(bf16)
            grad_down = lax.dot_general(
                cot_rows, active, contract_rows, preferred_element_type=f32
            ).astype(bf16)
            shares.append(
                scatter_chips(
                    [
                        jnp.concatenate([g[j * span : (j + 1) * span] for g in (grad_up, grad_down)])
                        for j in range(chips)
                    ],
                    k % 2,
                )
            )

        def group_sum(part):
            own, beside, near, both = [part[i * seq_len : (i + 1) * seq_len] for i in range(4)]
            near = add(near, flip(both.astype(bf16), core_bit)).astype(bf16)
            own = own + flip(beside.astype(bf16), core_bit).astype(f32)
            return chip_order(own + flip(near, near_bit).astype(f32))

        grad_normed2 = group_sum(back_part)
        block_out = (hidden1 + group_sum(out_part)).astype(bf16)

        held = shares
        for bit in reversed(far_bits):
            middle = len(held) // 2
            held = [add(a, flip(b.astype(bf16), bit)) for a, b in zip(held[:middle], held[middle:])]
        summed = held[0].reshape(2, 2, rows, half_units)
        keep, send = by_core(summed[:, 0], summed[:, 1])
        got = flip(send.astype(bf16), core_bit)
        pair = jnp.concatenate(list(by_core(keep, got.astype(f32))), axis=2)
        grad_w_up = pair[0]
        grad_w_down = pair[1].T

        grad_gain2 = jnp.sum(grad_normed2 * normal2, axis=0)
        grad_bias2 = jnp.sum(grad_normed2, axis=0)
        grad_hidden1 = cotangent.astype(f32) + layer_norm_back(
            grad_normed2, normal2, inverse2, norm2_gain
        )
        grad_attn_low = grad_hidden1.astype(bf16)

        def over_mp(share):
            low = share.astype(bf16)
            bits = [near_bit] + far_bits
            held = low
            for bit in bits:
                size = held.shape[0] // 2
                upper = (mp // bit) % 2 == 1
                keep = jnp.where(upper, held[size:], held[:size])
                send = jnp.where(upper, held[:size], held[size:])
                held = add(keep, flip(send, bit)).astype(bf16)
            for bit in reversed(bits):
                got = flip(held, bit)
                upper = (mp // bit) % 2 == 1
                held = jnp.concatenate(
                    [jnp.where(upper, got, held), jnp.where(upper, held, got)], axis=0
                )
            return held

        grad_context = lax.dot_general(
            grad_attn_low, wide_out, contract_cols, preferred_element_type=f32
        ).astype(bf16)
        grad_context = chip_order(grad_context)
        half = width // 2
        keep, send = by_core(grad_context[:, :half], grad_context[:, half:])
        grad_context = jnp.concatenate([keep, flip(send, core_bit)])

        ordered = chip_order(context_low).reshape(seq_len, chips, 2, rows)
        keep, send = by_core(ordered[:, :, 0], ordered[:, :, 1])
        other = lax.dot_general(send.reshape(seq_len, half), grad_attn_low, contract_rows, preferred_element_type=f32)
        own = lax.dot_general(keep.reshape(seq_len, half), grad_attn_low, contract_rows, preferred_element_type=f32)
        chip_sum = add(own, flip(other.astype(bf16), core_bit)).astype(bf16)
        grad_w_out = over_mp(
            scatter_chips([chip_sum[j * rows : (j + 1) * rows] for j in range(chips)], 1)
        ).astype(f32)

        normed1_rel = chip_order(normed1)
        grad_low, qkv_shares = [], []
        for p in range(chunks):
            cols = slice(p * PAIR * HEAD_DIM, (p + 1) * PAIR * HEAD_DIM)
            low = attend_back(
                qkv_low[p], logs[p], grad_context[:, cols], cosine, sine, seg_col, seg_row
            )
            grad_low.append(low)
            parts = [
                lax.dot_general(
                    normed1_rel[:, j * span : (j + 1) * span],
                    low,
                    contract_rows,
                    preferred_element_type=f32,
                ).astype(bf16)
                for j in range(chips)
            ]
            share = scatter_chips(parts, p % 2)
            qkv_shares.append(over_mp(share))
        back = 0.0
        for p in range(chunks):
            back = back + lax.dot_general(
                grad_low[p], qkv_wide[p], contract_cols, preferred_element_type=f32
            )
        grad_normed1 = back[:seq_len] + flip(back[seq_len:].astype(bf16), core_bit).astype(f32)
        grad_gain1 = jnp.sum(grad_normed1 * normal1, axis=0)
        grad_bias1 = jnp.sum(grad_normed1, axis=0)
        grad_input = grad_hidden1 + layer_norm_back(grad_normed1, normal1, inverse1, norm1_gain)

        shares = jnp.stack(qkv_shares, axis=1).reshape(2, rows, chunks, 3, PAIR * HEAD_DIM)
        keep, send = by_core(shares[0], shares[1])
        got = flip(send, core_bit)
        sides = jnp.stack(list(by_core(keep, got)), axis=1)
        grad_w_qkv = sides.transpose(0, 3, 1, 2, 4).reshape(rows, 3 * width).astype(f32)

        def sum_all(value):
            bit = 1
            while bit < total:
                value = value + flip(value, bit)
                bit *= 2
            return value

        sums2 = sum_all(jnp.stack([grad_gain2, grad_bias2]))
        sums1 = sum_all(jnp.stack([grad_gain1, grad_bias1]))
        return (
            block_out,
            grad_input,
            grad_w_qkv,
            grad_w_out,
            grad_w_up,
            grad_w_down,
            sums1[0],
            sums1[1],
            sums2[0],
            sums2[1],
        )

    return on_device


def solution(mesh):
    return jax.shard_map(
        build(mesh.shape["dp"], mesh.shape["mp"]),
        mesh=mesh,
        in_specs=(
            P(("dp", "mp"), None),
            P(("dp", "mp"), None),
            P(("dp", "mp"), None),
            P("dp"),
            P("dp", None),
            P("dp", None),
            P("dp", "mp"),
            P("mp", "dp"),
            P(),
            P(),
            P(),
            P(),
        ),
        out_specs=(
            P(("dp", "mp"), None),
            P(("dp", "mp"), None),
            P("dp", None),
            P("dp", None),
            P("dp", "mp"),
            P("mp", "dp"),
            P(),
            P(),
            P(),
            P(),
        ),
        check_vma=False,
    )
```

time: 1100 us -> 768 us (0.70)
  waiting for transfers between devices: 727 us -> 284 us
  starting transfers between devices: 0.52 us -> 77.1 us
  matrix products: 235 us -> 163 us
  Pallas kernels: 0 us -> 58 us
  local copies, waits for them, and re-layouts: 19.1 us -> 75.4 us
  other arithmetic: 51 us -> 98.6 us
  blocking collectives: 43.7 us -> 0 us
  between operations: 14.8 us -> 2.94 us
    all_gather x6 -> x0, waiting for transfers between devices: 350 us -> none  [the longest x1 117 us: on_device(): piece_rows = lax.all_gather(normed2_low, 'mp', axis=0, tiled=True)]
    reduce_scatter x6 -> x0, waiting for transfers between devices: 338 us -> none  [the longest x1 111 us: on_device(): lax.psum_scatter(jnp.dot(block_rows, wide_down, preferred_element_type=jn...]
    ppermute x0 -> x90, waiting for transfers between devices: none -> 284 us  [flip(): return lax.ppermute(value, AXES, [(i, i ^ bit) for i in range(total)])]
    ppermute x0 -> x90, starting transfers between devices: none -> 77.1 us  [flip(): return lax.ppermute(value, AXES, [(i, i ^ bit) for i in range(total)])]
    dot_general x17 -> x30, matrix products: 228 us -> 160 us  [the longest x2 27.7 us: on_device(): lax.dot_general(grad_preact, up_k, contract_cols, preferred_element_type=...]
    pallas_call x0 -> x6, Pallas kernels: none -> 58 us  [the longest x3 33.8 us: attend(): pl.pallas_call(functools.partial(attend_kernel, chips, rows // 2), out_sh...]
    psum x1 -> x0, blocking collectives: 43.7 us -> none  [on_device(): lax.psum((grad_gain1, grad_bias1, grad_gain2, grad_bias2), ('dp', 'mp'))]
    psum x1 -> x0, waiting for transfers between devices: 35.8 us -> none  [on_device(): lax.psum(shares[0].astype(jnp.bfloat16), 'mp').astype(jnp.float32)]
  transfers between devices with their start and end apart: 13 -> 90, of which waited for: 11 -> 35; matrix products, arithmetic and copies ran while one was open for 23% -> 29% of each run, Pallas kernels for 0% -> 8%
where the time goes in v1:
time: 768 us; the launch traced here: 758 us
  waiting for transfers between devices  284 us (37%)
  matrix products  163 us (21%)
  other arithmetic  98.6 us (13%)
  starting transfers between devices  77.1 us (10%)
  local copies, waits for them, and re-layouts  75.4 us (10%)
  Pallas kernels  58 us (8%)
    ppermute x90, waiting for transfers between devices, flip(): return lax.ppermute(value, AXES, [(i, i ^ bit) for i in range(total)])  284 us
    ppermute x90, starting transfers between devices, flip(): return lax.ppermute(value, AXES, [(i, i ^ bit) for i in range(total)])  77.1 us
    pallas_call x3, Pallas kernels, attend(): pl.pallas_call(functools.partial(attend_kernel, chips, rows // 2), out_sh...  33.8 us
    dot_general x2, matrix products, on_device(): lax.dot_general(grad_preact, up_k, contract_cols, preferred_element_type=...  27.7 us
    pallas_call x3, Pallas kernels, attend_back(): pl.pallas_call(functools.partial(attend_back_kernel, seq_len), out_shape=...  24.2 us
    dot_general x2, matrix products, on_device(): lax.dot_general(active, down_k, contract_cols, preferred_element_type=f32)  24 us
    dot_general x2, matrix products, on_device(): grad_active = jnp.dot(cot_rows, down_k, preferred_element_type=f32)  20.2 us
    dot_general x12, matrix products, on_device(): lax.dot_general(normed1_rel[:, j * span:(j + 1) * span], low, contract_ro...  19.2 us
  transfers between devices with their start and end apart: 90, of which 35 were waited for; matrix products, arithmetic and copies ran while one was open for 29% of the time, Pallas kernels for 8%

profile of v1, /device:TPU:0, one launch (start us, length us, event | category | flops | bytes accessed | tf_op | source)
XLA Modules:
  0.0 758.4 jit_solution(593758598159616782)
XLA Ops:
  11.5 5.2 reshape.169
  16.6 2.8 constant_dynamic-update-slice_fusion.12
  38.2 9.4 %fusion.73 = (bf16[192,3,256]{2,1,0:T(4,128)(2,1)S(1)}, bf16[192,3,256]{2,1,0:T(4,128)(2,1)S(1)}, bf16[192,3,256]{2,1,0:T(4,128)(2,1)S(1)}, bf16[192,3,256]{2,1,...) fusion(pred[]{:T(512)S(6)} %eq.24, ...), kind=kLoop, calls=%fused_computation.201 | loop fusion | flops 884736 | bytes 3538945 | tf_op jit(solution)/shard_map/jit(_where)/select_n | solution.py:303
  60.4 15.7 %collective-permute-done.7.refs_2_ = bf16[384,768]{1,0:T(8,128)(2,1)} collective-permute-done((bf16[384,768]{1,0:T(8,128)(2,1)}, bf16[384,768]{1,0:T(8,128)(2,1)}, u32[]{:S(2)}, u32[]{:S(2)}) %collective-permute-start.7) | collective-permute-done | bytes 589856 | tf_op jit(solution)/shard_map/ppermute | solution.py:235
  76.4 3.6 collective-permute-done.3.refs_1_
  85.9 30.2 %collective-permute-done.11.refs_3_ = bf16[384,768]{1,0:T(8,128)(2,1)S(1)} collective-permute-done((bf16[384,768]{1,0:T(8,128)(2,1)S(1)}, bf16[384,768]{1,0:T(8,128)(2,1)S(1)}, u32[]{:S(2)}, u32[]{:S(2)}) %collective-permute-start.11) | collective-permute-done | bytes 589856 | tf_op jit(solution)/shard_map/ppermute | solution.py:235
  117.9 11.3 %attend.5 = (bf16[1536,768]{1,0:T(8,128)(2,1)}, bf16[1024,768]{1,0:T(8,128)(2,1)}, bf16[1024,256]{1,0:T(8,128)(2,1)}, f32[1024,128]{1,0:T(8,128)}) custom-call(s32[4]{0:T(128)} %pad_add_fusion.2.offs_ref, bf16[1024,1536]{1,0:T(8,128)(2,1)} %pad_maximum_fusion.2.norm_ref, f32[512,128]{1,0:T(8,128)} %get-tuple-element.164.cos_ref, ...), custom_call_target="tpu_custom_call" | custom-call | tf_op jit(solution)/shard_map/attend/pallas_call | solution.py:185
  131.4 11.2 %attend.4 = (bf16[1536,768]{1,0:T(8,128)(2,1)}, bf16[1024,768]{1,0:T(8,128)(2,1)}, bf16[1024,256]{1,0:T(8,128)(2,1)}, f32[1024,128]{1,0:T(8,128)}) custom-call(s32[4]{0:T(128)} %pad_add_fusion.2.offs_ref, bf16[1024,1536]{1,0:T(8,128)(2,1)} %pad_maximum_fusion.2.norm_ref, f32[512,128]{1,0:T(8,128)} %get-tuple-element.164.cos_ref, ...), custom_call_target="tpu_custom_call" | custom-call | tf_op jit(solution)/shard_map/attend/pallas_call | solution.py:185
  145.8 11.3 %attend.3 = (bf16[1536,768]{1,0:T(8,128)(2,1)}, bf16[1024,768]{1,0:T(8,128)(2,1)}, bf16[1024,256]{1,0:T(8,128)(2,1)}, f32[1024,128]{1,0:T(8,128)}) custom-call(s32[4]{0:T(128)} %pad_add_fusion.2.offs_ref, bf16[1024,1536]{1,0:T(8,128)(2,1)} %pad_maximum_fusion.2.norm_ref, f32[512,128]{1,0:T(8,128)} %get-tuple-element.164.cos_ref, ...), custom_call_target="tpu_custom_call" | custom-call | tf_op jit(solution)/shard_map/attend/pallas_call | solution.py:185
  165.4 2.7 fusion.128
  171.6 2.7 constant_dynamic-update-slice_fusion.11
  174.3 15.0 %collective-permute-done.35 = bf16[512,1536]{1,0:T(8,128)(2,1)} collective-permute-done((bf16[512,1536]{1,0:T(8,128)(2,1)S(1)}, bf16[512,1536]{1,0:T(8,128)(2,1)}, u32[]{:S(2)}, u32[]{:S(2)}) %collective-permute-start.35) | collective-permute-done | bytes 1572896 | tf_op jit(solution)/shard_map/ppermute | solution.py:235
  189.3 2.7 constant_dynamic-update-slice_fusion.10
  192.0 5.0 collective-permute-done.27
  211.0 15.2 %collective-permute-done.29 = bf16[768,768]{1,0:T(8,128)(2,1)} collective-permute-done((bf16[768,768]{1,0:T(8,128)(2,1)}, bf16[768,768]{1,0:T(8,128)(2,1)}, u32[]{:S(2)}, u32[]{:S(2)}) %collective-permute-start.29) | collective-permute-done | bytes 1179680 | tf_op jit(solution)/shard_map/ppermute | solution.py:235
  231.8 17.6 %collective-permute-done.26 = bf16[768,768]{1,0:T(8,128)(2,1)} collective-permute-done((bf16[768,768]{1,0:T(8,128)(2,1)}, bf16[768,768]{1,0:T(8,128)(2,1)}, u32[]{:S(2)}, u32[]{:S(2)}) %collective-permute-start.26) | collective-permute-done | bytes 1179680 | tf_op jit(solution)/shard_map/ppermute | solution.py:235
  251.5 3.0 constant_dynamic-update-slice_fusion.9
  254.5 3.5 constant_dynamic-slice_fusion.11
  259.1 13.6 %pad_maximum_fusion = bf16[2048,1536]{1,0:T(8,128)(2,1)S(1)} fusion(bf16[512,1536]{1,0:T(8,128)(2,1)S(1)} %collective-permute-done.22, bf16[512,1536]{1,0:T(8,128)(2,1)} %collective-permute-done.21, bf16[512,1536]{1,0:T(8,128)(2,1)S(1)} %collective-permute-done.20, bf16[512,384]{1,0:T(8,128)(2,1)S(1)} %get-tuple-element.121, ...), kind=kLoop, calls=%fused_computation.22 | loop fusion | flops 44040192 | bytes 12582912 | tf_op jit(solution)/shard_map/concatenate | solution.py:374
  272.8 7.2 fusion.85
  280.0 11.0 %fusion.3 = (bf16[2048,768]{1,0:T(8,128)(2,1)S(1)}, bf16[2048,768]{1,0:T(8,128)(2,1)}, f32[2048,768]{1,0:T(8,128)}) fusion(s32[768]{0:T(1024)S(1)} %get-tuple-element.182, s32[2048]{0:T(1024)S(1)} %bitcast.165, f32[2048,768]{1,0:T(8,128)} %fusion.85, s32[768]{0:T(1024)S(1)} %get-tuple-element.183, bf16[2048,1536]{1,0:T(8,128)(2,1)S(1)} %pad_maximum_fusion, ...), kind=kOutput, calls=%fused_computation.11 | convolution fusion | flops 4863295488 | bytes 27539456 | tf_op jit(solution)/shard_map/dot_general | solution.py:390
  291.0 9.5 %convolution_convert_fusion.2 = bf16[1536,768]{1,0:T(8,128)(2,1)} fusion(bf16[2048,768]{1,0:T(8,128)(2,1)} %get-tuple-element.168, bf16[2048,384]{1,0:T(8,128)(2,1)S(1)} %get-tuple-element.58, bf16[2048,384]{1,0:T(8,128)(2,1)S(1)} %get-tuple-element.59, bf16[2048,384]{1,0:T(8,128)(2,1)S(1)} %get-tuple-element.60, bf16[2048,384]{1,0:T(8,128)(2,1)S(1)} %get-tuple-element.57), kind=kOutput, calls=%fused_computation.53 | convolution fusion | flops 4858183680 | bytes 11796480 | tf_op jit(solution)/shard_map/dot_general | solution.py:405
  300.5 10.7 %fusion.2 = bf16[2048,768]{1,0:T(8,128)(2,1)} fusion(f32[2048,768]{1,0:T(8,128)} %fusion.85, s32[768]{0:T(1024)S(1)} %get-tuple-element.183, s32[2048]{0:T(1024)S(1)} %bitcast.166, bf16[384,768]{1,0:T(8,128)(2,1)S(1)} %copy-done.57, bf16[384,768]{1,0:T(8,128)(2,1)S(1)} %copy-done.54, bf16[384,768]{1,0:T(8,128)(2,1)S(1)} %copy-done.53, ...), kind=kOutput, calls=%fused_computation.10 | convolution fusion | flops 4885315584 | bytes 18099200 | tf_op jit(solution)/shard_map/dot_general | solution.py:391
  311.2 12.3 %fusion.83 = f32[2048,1536]{1,0:T(8,128)} fusion(bf16[2048,768]{1,0:T(8,128)(2,1)} %get-tuple-element.168, bf16[384,768]{1,0:T(8,128)(2,1)S(1)} %copy-done.57, bf16[384,768]{1,0:T(8,128)(2,1)S(1)} %copy-done.54, bf16[384,768]{1,0:T(8,128)(2,1)S(1)} %copy-done.53, bf16[384,768]{1,0:T(8,128)(2,1)S(1)} %copy-done.48), kind=kOutput, calls=%fused_computation.233 | convolution fusion | flops 4841275392 | bytes 18087936 | tf_op jit(solution)/shard_map/dot_general | solution.py:399
  323.5 6.5 convolution_convert_fusion.3
  330.1 9.8 %fusion.84 = f32[2048,1536]{1,0:T(8,128)} fusion(bf16[2048,768]{1,0:T(8,128)(2,1)S(1)} %copy-done.80, bf16[384,768]{1,0:T(8,128)(2,1)S(1)} %copy-done.56, bf16[384,768]{1,0:T(8,128)(2,1)S(1)} %copy-done.52, bf16[384,768]{1,0:T(8,128)(2,1)S(1)} %copy-done.50, bf16[384,768]{1,0:T(8,128)(2,1)S(1)} %copy-done.47), kind=kOutput, calls=%fused_computation.234 | convolution fusion | flops 4841275392 | bytes 18087936 | tf_op jit(solution)/shard_map/dot_general | solution.py:396
  339.8 9.5 %fusion.5 = bf16[2048,768]{1,0:T(8,128)(2,1)S(1)} fusion(f32[2048,768]{1,0:T(8,128)} %get-tuple-element.179, s32[768]{0:T(1024)S(1)} %get-tuple-element.182, s32[2048]{0:T(1024)S(1)} %bitcast.167, bf16[384,768]{1,0:T(8,128)(2,1)S(1)} %copy-done.32, bf16[384,768]{1,0:T(8,128)(2,1)S(1)} %get-tuple-element.132, bf16[384,768]{1,0:T(8,128)(2,1)S(1)} %copy-done.30, ...), kind=kOutput, calls=%fused_computation.13 | convolution fusion | flops 4885315584 | bytes 18099200 | tf_op jit(solution)/shard_map/dot_general | solution.py:391
  349.4 5.7 convolution_convert_fusion.1
  357.6 7.9 %convolution_convert_fusion = bf16[1536,768]{1,0:T(8,128)(2,1)S(1)} fusion(bf16[2048,768]{1,0:T(8,128)(2,1)S(1)} %get-tuple-element.167, bf16[2048,384]{1,0:T(8,128)(2,1)S(1)} %copy-done.37, bf16[2048,384]{1,0:T(8,128)(2,1)S(1)} %copy-done.39, bf16[2048,384]{1,0:T(8,128)(2,1)} %copy-done.40, bf16[2048,384]{1,0:T(8,128)(2,1)S(1)} %copy-done.35), kind=kOutput, calls=%fused_computation.51 | convolution fusion | flops 4858183680 | bytes 11796480 | tf_op jit(solution)/shard_map/dot_general | solution.py:405
  368.3 11.7 %fusion.130 = (bf16[2048,1536]{1,0:T(8,128)(2,1)S(1)}, f32[2048,1536]{1,0:T(8,128)}) fusion(f32[2048,1536]{1,0:T(8,128)} %fusion.83, bf16[2048,768]{1,0:T(8,128)(2,1)S(1)} %get-tuple-element.167, bf16[384,768]{1,0:T(8,128)(2,1)} %get-tuple-element.134, bf16[384,768]{1,0:T(8,128)(2,1)} %copy-done.29, bf16[384,768]{1,0:T(8,128)(2,1)} %get-tuple-element.130, ...), kind=kOutput, calls=%fused_computation.377 | convolution fusion | flops 4847566848 | bytes 36962304 | tf_op jit(solution)/shard_map/dot_general | solution.py:399
  381.9 17.9 %fusion.129 = (bf16[2048,1536]{1,0:T(8,128)(2,1)}, f32[2048,1536]{1,0:T(8,128)}) fusion(f32[2048,1536]{1,0:T(8,128)} %fusion.84, bf16[2048,768]{1,0:T(8,128)(2,1)} %copy-done.14, bf16[384,768]{1,0:T(8,128)(2,1)} %copy-done.31, bf16[384,768]{1,0:T(8,128)(2,1)} %copy-done.27, bf16[384,768]{1,0:T(8,128)(2,1)} %copy-done.28, bf16[384,768]{1,0:T(8,128)(2,1)S(1)} %copy-done.25), kind=kOutput, calls=%fused_computation.376 | convolution fusion | flops 4847566848 | bytes 36962304 | tf_op jit(solution)/shard_map/dot_general | solution.py:396
  399.8 3.4 fusion.112
  414.4 3.3 fusion.36
  420.3 15.8 %collective-permute-done.73 = bf16[768,768]{1,0:T(8,128)(2,1)} collective-permute-done((bf16[768,768]{1,0:T(8,128)(2,1)}, bf16[768,768]{1,0:T(8,128)(2,1)}, u32[]{:S(2)}, u32[]{:S(2)}) %collective-permute-start.73) | collective-permute-done | bytes 1179680 | tf_op jit(solution)/shard_map/ppermute | solution.py:235
  441.2 19.1 %collective-permute-done.76 = bf16[768,768]{1,0:T(8,128)(2,1)S(1)} collective-permute-done((bf16[768,768]{1,0:T(8,128)(2,1)}, bf16[768,768]{1,0:T(8,128)(2,1)S(1)}, u32[]{:S(2)}, u32[]{:S(2)}) %collective-permute-start.76) | collective-permute-done | bytes 1179680 | tf_op jit(solution)/shard_map/ppermute | solution.py:235
  461.8 2.8 add_convert_fusion.2
  467.4 41.2 %collective-permute-done.39 = bf16[512,1536]{1,0:T(8,128)(2,1)} collective-permute-done((bf16[512,1536]{1,0:T(8,128)(2,1)}, bf16[512,1536]{1,0:T(8,128)(2,1)}, u32[]{:S(2)}, u32[]{:S(2)}) %collective-permute-start.39) | collective-permute-done | bytes 1572896 | tf_op jit(solution)/shard_map/ppermute | solution.py:235
  529.9 2.8 convolution_convert_fusion.4
  538.2 8.0 %attend_back.3 = bf16[1024,768]{1,0:T(8,128)(2,1)} custom-call(bf16[1024,768]{1,0:T(8,128)(2,1)} %get-tuple-element.25.qkv_ref, f32[1024,128]{1,0:T(8,128)} %get-tuple-element.26.lse_ref, bf16[1024,256]{1,0:T(8,128)(2,1)} %get-tuple-element.112.grad_ref, f32[512,128]{1,0:T(8,128)} %get-tuple-element.164.cos_ref, f32[512,128]{1,0:T(8,128)} %get-tuple-element.163.sin_ref, ...), custom_call_target="tpu_custom_call" | custom-call | tf_op jit(solution)/shard_map/attend_back/pallas_call | solution.py:203
  548.4 8.0 %attend_back.4 = bf16[1024,768]{1,0:T(8,128)(2,1)} custom-call(bf16[1024,768]{1,0:T(8,128)(2,1)} %get-tuple-element.28.qkv_ref, f32[1024,128]{1,0:T(8,128)} %get-tuple-element.29.lse_ref, bf16[1024,256]{1,0:T(8,128)(2,1)} %get-tuple-element.111.grad_ref, f32[512,128]{1,0:T(8,128)} %get-tuple-element.164.cos_ref, f32[512,128]{1,0:T(8,128)} %get-tuple-element.163.sin_ref, ...), custom_call_target="tpu_custom_call" | custom-call | tf_op jit(solution)/shard_map/attend_back/pallas_call | solution.py:203
  556.4 3.1 convolution_convert_fusion.11
  559.4 8.2 %attend_back.5 = bf16[1024,768]{1,0:T(8,128)(2,1)} custom-call(bf16[1024,768]{1,0:T(8,128)(2,1)} %get-tuple-element.31.qkv_ref, f32[1024,128]{1,0:T(8,128)} %get-tuple-element.32.lse_ref, bf16[1024,256]{1,0:T(8,128)(2,1)} %get-tuple-element.113.grad_ref, f32[512,128]{1,0:T(8,128)} %get-tuple-element.164.cos_ref, f32[512,128]{1,0:T(8,128)} %get-tuple-element.163.sin_ref, ...), custom_call_target="tpu_custom_call" | custom-call | tf_op jit(solution)/shard_map/attend_back/pallas_call | solution.py:203
  567.6 3.2 convolution_convert_fusion.6
  577.6 4.7 fusion.132
  582.3 5.2 add_add_fusion
  592.4 7.6 collective-permute-done.57
  606.7 8.0 %collective-permute-done.43 = bf16[384,768]{1,0:T(8,128)(2,1)S(1)} collective-permute-done((bf16[384,768]{1,0:T(8,128)(2,1)S(1)}, bf16[384,768]{1,0:T(8,128)(2,1)S(1)}, u32[]{:S(2)}, u32[]{:S(2)}) %collective-permute-start.43) | collective-permute-done | bytes 589856 | tf_op jit(solution)/shard_map/ppermute | solution.py:235
  621.0 10.0 %collective-permute-done.50 = bf16[384,768]{1,0:T(8,128)(2,1)S(1)} collective-permute-done((bf16[384,768]{1,0:T(8,128)(2,1)S(1)}, bf16[384,768]{1,0:T(8,128)(2,1)S(1)}, u32[]{:S(2)}, u32[]{:S(2)}) %collective-permute-start.50) | collective-permute-done | bytes 589856 | tf_op jit(solution)/shard_map/ppermute | solution.py:235
  632.1 8.9 %collective-permute-done.42 = bf16[384,768]{1,0:T(8,128)(2,1)S(1)} collective-permute-done((bf16[384,768]{1,0:T(8,128)(2,1)S(1)}, bf16[384,768]{1,0:T(8,128)(2,1)S(1)}, u32[]{:S(2)}, u32[]{:S(2)}) %collective-permute-start.42) | collective-permute-done | bytes 589856 | tf_op jit(solution)/shard_map/ppermute | solution.py:235
  645.4 10.1 %collective-permute-done.52 = bf16[192,768]{1,0:T(8,128)(2,1)S(1)} collective-permute-done((bf16[192,768]{1,0:T(8,128)(2,1)S(1)}, bf16[192,768]{1,0:T(8,128)(2,1)S(1)}, u32[]{:S(2)}, u32[]{:S(2)}) %collective-permute-start.52) | collective-permute-done | bytes 294944 | tf_op jit(solution)/shard_map/ppermute | solution.py:235
  655.7 2.9 collective-permute-done.45
  662.6 3.1 add_convert_fusion
  667.8 2.9 collective-permute-done.81
  679.0 11.2 %collective-permute-done.61 = bf16[96,768]{1,0:T(8,128)(2,1)S(1)} collective-permute-done((bf16[96,768]{1,0:T(8,128)(2,1)S(1)}, bf16[96,768]{1,0:T(8,128)(2,1)S(1)}, u32[]{:S(2)}, u32[]{:S(2)}) %collective-permute-start.61) | collective-permute-done | bytes 147488 | tf_op jit(solution)/shard_map/ppermute | solution.py:235
  693.4 3.1 collective-permute-done.47
  696.5 6.7 collective-permute-done.62
  704.7 4.9 collective-permute-done.55
  709.7 5.7 collective-permute-done.48
  720.3 5.1 collective-permute-done.68
  729.1 4.1 collective-permute-done.69
  734.5 2.7 fusion.27
  739.9 2.8 collective-permute-start.71
  745.5 4.6 copy.72
  750.1 6.6 reshape.173
  (515 shorter events, 214.5 us)
Async XLA Ops:
  0.7 35.6 %collective-permute-start.13 = (bf16[192,1536]{1,0:T(8,128)(2,1)}, bf16[192,1536]{1,0:T(8,128)(2,1)}, u32[]{:S(2)}, u32[]{:S(2)}) collective-permute-start(bf16[192,1536]{1,0:T(8,128)(2,1)} %param.17), channel_id=1, source_target_pairs={{0,4},{1,5},{2,6},{3,7},{4,0},{5,1},{6,2},{7,3},{8,12},{9,13},{10,... | collective-permute-start | bytes 1769480 | tf_op jit(solution)/shard_map/ppermute | solution.py:235
  1.2 30.4 %collective-permute-start.16 = (bf16[192,1536]{1,0:T(8,128)(2,1)}, bf16[192,1536]{1,0:T(8,128)(2,1)}, u32[]{:S(2)}, u32[]{:S(2)}) collective-permute-start(bf16[192,1536]{1,0:T(8,128)(2,1)} %param.17), channel_id=1, source_target_pairs={{0,16},{1,17},{2,18},{3,19},{4,20},{5,21},{6,22},{7,23},{8,24},{9,... | collective-permute-start | bytes 1769480 | tf_op jit(solution)/shard_map/ppermute | solution.py:235
  3.8 32.5 %collective-permute-start.14 = (bf16[192,1536]{1,0:T(8,128)(2,1)}, bf16[192,1536]{1,0:T(8,128)(2,1)}, u32[]{:S(2)}, u32[]{:S(2)}) collective-permute-start(bf16[192,1536]{1,0:T(8,128)(2,1)} %param.17), channel_id=1, source_target_pairs={{0,8},{1,9},{2,10},{3,11},{4,12},{5,13},{6,14},{7,15},{8,0},{9,1},... | collective-permute-start | bytes 1769480 | tf_op jit(solution)/shard_map/ppermute | solution.py:235
  6.7 19.1 %collective-permute-start.1 = (s32[5,512]{1,0:T(8,128)S(1)}, s32[5,512]{1,0:T(8,128)S(1)}, u32[]{:S(2)}, u32[]{:S(2)}) collective-permute-start(s32[5,512]{1,0:T(8,128)S(1)} %pad_add_fusion), channel_id=1, source_target_pairs={{0,4},{1,5},{2,6},{3,7},{4,0},{5,1},{6,2},{7,3},{8,12},{9,13},{10,... | collective-permute-start | bytes 30728 | tf_op jit(solution)/shard_map/ppermute | solution.py:235
  6.7 50.6 %collective-permute-start = (bf16[512,1536]{1,0:T(8,128)(2,1)}, bf16[512,1536]{1,0:T(8,128)(2,1)S(1)}, u32[]{:S(2)}, u32[]{:S(2)}) collective-permute-start(bf16[512,1536]{1,0:T(8,128)(2,1)} %param.12), channel_id=1, source_target_pairs={{0,4},{1,5},{2,6},{3,7},{4,0},{5,1},{6,2},{7,3},{8,12},{9,13},{10,... | collective-permute-start | bytes 4718600 | tf_op jit(solution)/shard_map/ppermute | solution.py:235
  31.5 27.3 %collective-permute-start.18 = (bf16[192,1536]{1,0:T(8,128)(2,1)}, bf16[192,1536]{1,0:T(8,128)(2,1)}, u32[]{:S(2)}, u32[]{:S(2)}) collective-permute-start(bf16[192,1536]{1,0:T(8,128)(2,1)} %collective-permute-done.16), channel_id=1, source_target_pairs={{0,8},{1,9},{2,10},{3,11},{4,12},{5,13},{6,14},{7,15},{8,0},{9,1},... | collective-permute-start | bytes 1769480 | tf_op jit(solution)/shard_map/ppermute | solution.py:235
  36.2 18.1 %collective-permute-start.17 = (bf16[192,1536]{1,0:T(8,128)(2,1)}, bf16[192,1536]{1,0:T(8,128)(2,1)S(1)}, u32[]{:S(2)}, u32[]{:S(2)}) collective-permute-start(bf16[192,1536]{1,0:T(8,128)(2,1)} %collective-permute-done.16), channel_id=1, source_target_pairs={{0,4},{1,5},{2,6},{3,7},{4,0},{5,1},{6,2},{7,3},{8,12},{9,13},{10,... | collective-permute-start | bytes 1769480 | tf_op jit(solution)/shard_map/ppermute | solution.py:235
  36.2 14.8 %collective-permute-start.15 = (bf16[192,1536]{1,0:T(8,128)(2,1)}, bf16[192,1536]{1,0:T(8,128)(2,1)S(1)}, u32[]{:S(2)}, u32[]{:S(2)}) collective-permute-start(bf16[192,1536]{1,0:T(8,128)(2,1)} %collective-permute-done.14), channel_id=1, source_target_pairs={{0,4},{1,5},{2,6},{3,7},{4,0},{5,1},{6,2},{7,3},{8,12},{9,13},{10,... | collective-permute-start | bytes 1769480 | tf_op jit(solution)/shard_map/ppermute | solution.py:235
  48.0 34.0 %collective-permute-start.10 = (bf16[384,768]{1,0:T(8,128)(2,1)S(1)}, bf16[384,768]{1,0:T(8,128)(2,1)S(1)}, u32[]{:S(2)}, u32[]{:S(2)}) collective-permute-start(bf16[384,768]{1,0:T(8,128)(2,1)S(1)} %constant_dynamic-update-slice_fusion.4.refs_0_), channel_id=1, source_target_pairs={{0,16},{1,17},{2,18},{3,19},{4,20},{5,21},{6,22},{7,23},{8,24},{9,... | collective-permute-start | bytes 1769480 | tf_op jit(solution)/shard_map/ppermute | solution.py:235
  51.1 32.4 %collective-permute-start.9 = (bf16[384,768]{1,0:T(8,128)(2,1)S(1)}, bf16[384,768]{1,0:T(8,128)(2,1)S(1)}, u32[]{:S(2)}, u32[]{:S(2)}) collective-permute-start(bf16[384,768]{1,0:T(8,128)(2,1)S(1)} %constant_dynamic-update-slice_fusion.4.refs_0_), channel_id=1, source_target_pairs={{0,8},{1,9},{2,10},{3,11},{4,12},{5,13},{6,14},{7,15},{8,0},{9,1},... | collective-permute-start | bytes 1769480 | tf_op jit(solution)/shard_map/ppermute | solution.py:235
  54.4 21.7 %collective-permute-start.7 = (bf16[384,768]{1,0:T(8,128)(2,1)}, bf16[384,768]{1,0:T(8,128)(2,1)}, u32[]{:S(2)}, u32[]{:S(2)}) collective-permute-start(bf16[384,768]{1,0:T(8,128)(2,1)} %constant_dynamic-update-slice_fusion.2.refs_0_), channel_id=1, source_target_pairs={{0,16},{1,17},{2,18},{3,19},{4,20},{5,21},{6,22},{7,23},{8,24},{9,... | collective-permute-start | bytes 1769480 | tf_op jit(solution)/shard_map/ppermute | solution.py:235
  57.3 22.7 %collective-permute-start.3 = (bf16[384,768]{1,0:T(8,128)(2,1)}, bf16[384,768]{1,0:T(8,128)(2,1)}, u32[]{:S(2)}, u32[]{:S(2)}) collective-permute-start(bf16[384,768]{1,0:T(8,128)(2,1)} %constant_dynamic-update-slice_fusion.refs_0_), channel_id=1, source_target_pairs={{0,8},{1,9},{2,10},{3,11},{4,12},{5,13},{6,14},{7,15},{8,0},{9,1},... | collective-permute-start | bytes 1769480 | tf_op jit(solution)/shard_map/ppermute | solution.py:235
  58.8 70.5 %collective-permute-start.6 = (bf16[384,768]{1,0:T(8,128)(2,1)}, bf16[384,768]{1,0:T(8,128)(2,1)}, u32[]{:S(2)}, u32[]{:S(2)}) collective-permute-start(bf16[384,768]{1,0:T(8,128)(2,1)} %constant_dynamic-update-slice_fusion.2.refs_0_), channel_id=1, source_target_pairs={{0,8},{1,9},{2,10},{3,11},{4,12},{5,13},{6,14},{7,15},{8,0},{9,1},... | collective-permute-start | bytes 1769480 | tf_op jit(solution)/shard_map/ppermute | solution.py:235
  76.1 66.5 %collective-permute-start.4 = (bf16[384,768]{1,0:T(8,128)(2,1)}, bf16[384,768]{1,0:T(8,128)(2,1)}, u32[]{:S(2)}, u32[]{:S(2)}) collective-permute-start(bf16[384,768]{1,0:T(8,128)(2,1)} %constant_dynamic-update-slice_fusion.refs_0_), channel_id=1, source_target_pairs={{0,16},{1,17},{2,18},{3,19},{4,20},{5,21},{6,22},{7,23},{8,24},{9,... | collective-permute-start | bytes 1769480 | tf_op jit(solution)/shard_map/ppermute | solution.py:235
  80.0 49.9 %collective-permute-start.8 = (bf16[384,768]{1,0:T(8,128)(2,1)}, bf16[384,768]{1,0:T(8,128)(2,1)}, u32[]{:S(2)}, u32[]{:S(2)}) collective-permute-start(bf16[384,768]{1,0:T(8,128)(2,1)} %collective-permute-done.7.refs_2_), channel_id=1, source_target_pairs={{0,8},{1,9},{2,10},{3,11},{4,12},{5,13},{6,14},{7,15},{8,0},{9,1},... | collective-permute-start | bytes 1769480 | tf_op jit(solution)/shard_map/ppermute | solution.py:235
  81.9 63.4 %collective-permute-start.5 = (bf16[384,768]{1,0:T(8,128)(2,1)}, bf16[384,768]{1,0:T(8,128)(2,1)}, u32[]{:S(2)}, u32[]{:S(2)}) collective-permute-start(bf16[384,768]{1,0:T(8,128)(2,1)} %collective-permute-done.3.refs_1_), channel_id=1, source_target_pairs={{0,16},{1,17},{2,18},{3,19},{4,20},{5,21},{6,22},{7,23},{8,24},{9,... | collective-permute-start | bytes 1769480 | tf_op jit(solution)/shard_map/ppermute | solution.py:235
  83.5 32.6 %collective-permute-start.11 = (bf16[384,768]{1,0:T(8,128)(2,1)S(1)}, bf16[384,768]{1,0:T(8,128)(2,1)S(1)}, u32[]{:S(2)}, u32[]{:S(2)}) collective-permute-start(bf16[384,768]{1,0:T(8,128)(2,1)S(1)} %collective-permute-done.9.refs_1_), channel_id=1, source_target_pairs={{0,16},{1,17},{2,18},{3,19},{4,20},{5,21},{6,22},{7,23},{8,24},{9,... | collective-permute-start | bytes 1769480 | tf_op jit(solution)/shard_map/ppermute | solution.py:235
  116.1 42.4 %collective-permute-start.19 = (bf16[192,1536]{1,0:T(8,128)(2,1)}, bf16[192,1536]{1,0:T(8,128)(2,1)S(1)}, u32[]{:S(2)}, u32[]{:S(2)}) collective-permute-start(bf16[192,1536]{1,0:T(8,128)(2,1)} %collective-permute-done.18), channel_id=1, source_target_pairs={{0,4},{1,5},{2,6},{3,7},{4,0},{5,1},{6,2},{7,3},{8,12},{9,13},{10,... | collective-permute-start | bytes 1769480 | tf_op jit(solution)/shard_map/ppermute | solution.py:235
  129.3 41.9 %collective-permute-start.34 = (bf16[512,1536]{1,0:T(8,128)(2,1)S(1)}, bf16[512,1536]{1,0:T(8,128)(2,1)}, u32[]{:S(2)}, u32[]{:S(2)}) collective-permute-start(bf16[512,1536]{1,0:T(8,128)(2,1)S(1)} %copy-done.12), channel_id=1, source_target_pairs={{0,4},{1,5},{2,6},{3,7},{4,0},{5,1},{6,2},{7,3},{8,12},{9,13},{10,... | collective-permute-start | bytes 4718600 | tf_op jit(solution)/shard_map/ppermute | solution.py:235
  129.9 59.5 %collective-permute-start.35 = (bf16[512,1536]{1,0:T(8,128)(2,1)S(1)}, bf16[512,1536]{1,0:T(8,128)(2,1)}, u32[]{:S(2)}, u32[]{:S(2)}) collective-permute-start(bf16[512,1536]{1,0:T(8,128)(2,1)S(1)} %copy-done.12), channel_id=1, source_target_pairs={{0,1},{1,0},{2,3},{3,2},{4,5},{5,4},{6,7},{7,6},{8,9},{9,8},{10,11... | collective-permute-start | bytes 4718600 | tf_op jit(solution)/shard_map/ppermute | solution.py:235
  142.6 54.4 %collective-permute-start.27 = (bf16[768,768]{1,0:T(8,128)(2,1)}, bf16[768,768]{1,0:T(8,128)(2,1)}, u32[]{:S(2)}, u32[]{:S(2)}) collective-permute-start(bf16[768,768]{1,0:T(8,128)(2,1)} %bitcast.11), channel_id=1, source_target_pairs={{0,2},{1,3},{2,0},{3,1},{4,6},{5,7},{6,4},{7,5},{8,10},{9,11},{10,... | collective-permute-start | bytes 3538952 | tf_op jit(solution)/shard_map/ppermute | solution.py:235
  145.3 57.8 %collective-permute-start.25 = (bf16[768,768]{1,0:T(8,128)(2,1)}, bf16[768,768]{1,0:T(8,128)(2,1)}, u32[]{:S(2)}, u32[]{:S(2)}) collective-permute-start(bf16[768,768]{1,0:T(8,128)(2,1)} %bitcast.11), channel_id=1, source_target_pairs={{0,16},{1,17},{2,18},{3,19},{4,20},{5,21},{6,22},{7,23},{8,24},{9,... | collective-permute-start | bytes 3538952 | tf_op jit(solution)/shard_map/ppermute | solution.py:235
  161.6 41.5 %collective-permute-start.24 = (bf16[768,768]{1,0:T(8,128)(2,1)}, bf16[768,768]{1,0:T(8,128)(2,1)}, u32[]{:S(2)}, u32[]{:S(2)}) collective-permute-start(bf16[768,768]{1,0:T(8,128)(2,1)} %bitcast.11), channel_id=1, source_target_pairs={{0,8},{1,9},{2,10},{3,11},{4,12},{5,13},{6,14},{7,15},{8,0},{9,1},... | collective-permute-start | bytes 3538952 | tf_op jit(solution)/shard_map/ppermute | solution.py:235
  171.2 55.1 %collective-permute-start.21 = (bf16[512,1536]{1,0:T(8,128)(2,1)}, bf16[512,1536]{1,0:T(8,128)(2,1)}, u32[]{:S(2)}, u32[]{:S(2)}) collective-permute-start(bf16[512,1536]{1,0:T(8,128)(2,1)} %pad_maximum_fusion.10), channel_id=1, source_target_pairs={{0,1},{1,0},{2,3},{3,2},{4,5},{5,4},{6,7},{7,6},{8,9},{9,8},{10,11... | collective-permute-start | bytes 4718600 | tf_op jit(solution)/shard_map/ppermute | solution.py:235
  197.0 29.2 %collective-permute-start.29 = (bf16[768,768]{1,0:T(8,128)(2,1)}, bf16[768,768]{1,0:T(8,128)(2,1)}, u32[]{:S(2)}, u32[]{:S(2)}) collective-permute-start(bf16[768,768]{1,0:T(8,128)(2,1)} %collective-permute-done.27), channel_id=1, source_target_pairs={{0,16},{1,17},{2,18},{3,19},{4,20},{5,21},{6,22},{7,23},{8,24},{9,... | collective-permute-start | bytes 3538952 | tf_op jit(solution)/shard_map/ppermute | solution.py:235
  199.2 28.9 %collective-permute-start.28 = (bf16[768,768]{1,0:T(8,128)(2,1)}, bf16[768,768]{1,0:T(8,128)(2,1)}, u32[]{:S(2)}, u32[]{:S(2)}) collective-permute-start(bf16[768,768]{1,0:T(8,128)(2,1)} %collective-permute-done.27), channel_id=1, source_target_pairs={{0,8},{1,9},{2,10},{3,11},{4,12},{5,13},{6,14},{7,15},{8,0},{9,1},... | collective-permute-start | bytes 3538952 | tf_op jit(solution)/shard_map/ppermute | solution.py:235
  203.1 48.5 %collective-permute-start.36 = (bf16[512,1536]{1,0:T(8,128)(2,1)}, bf16[512,1536]{1,0:T(8,128)(2,1)}, u32[]{:S(2)}, u32[]{:S(2)}) collective-permute-start(bf16[512,1536]{1,0:T(8,128)(2,1)} %collective-permute-done.35), channel_id=1, source_target_pairs={{0,4},{1,5},{2,6},{3,7},{4,0},{5,1},{6,2},{7,3},{8,12},{9,13},{10,... | collective-permute-start | bytes 4718600 | tf_op jit(solution)/shard_map/ppermute | solution.py:235
  203.1 46.3 %collective-permute-start.26 = (bf16[768,768]{1,0:T(8,128)(2,1)}, bf16[768,768]{1,0:T(8,128)(2,1)}, u32[]{:S(2)}, u32[]{:S(2)}) collective-permute-start(bf16[768,768]{1,0:T(8,128)(2,1)} %collective-permute-done.24), channel_id=1, source_target_pairs={{0,16},{1,17},{2,18},{3,19},{4,20},{5,21},{6,22},{7,23},{8,24},{9,... | collective-permute-start | bytes 3538952 | tf_op jit(solution)/shard_map/ppermute | solution.py:235
  226.3 32.8 %collective-permute-start.20 = (bf16[512,1536]{1,0:T(8,128)(2,1)}, bf16[512,1536]{1,0:T(8,128)(2,1)S(1)}, u32[]{:S(2)}, u32[]{:S(2)}) collective-permute-start(bf16[512,1536]{1,0:T(8,128)(2,1)} %pad_maximum_fusion.10), channel_id=1, source_target_pairs={{0,4},{1,5},{2,6},{3,7},{4,0},{5,1},{6,2},{7,3},{8,12},{9,13},{10,... | collective-permute-start | bytes 4718600 | tf_op jit(solution)/shard_map/ppermute | solution.py:235
  226.3 32.9 %collective-permute-start.22 = (bf16[512,1536]{1,0:T(8,128)(2,1)}, bf16[512,1536]{1,0:T(8,128)(2,1)S(1)}, u32[]{:S(2)}, u32[]{:S(2)}) collective-permute-start(bf16[512,1536]{1,0:T(8,128)(2,1)} %collective-permute-done.21), channel_id=1, source_target_pairs={{0,4},{1,5},{2,6},{3,7},{4,0},{5,1},{6,2},{7,3},{8,12},{9,13},{10,... | collective-permute-start | bytes 4718600 | tf_op jit(solution)/shard_map/ppermute | solution.py:235
  228.1 30.0 %collective-permute-start.30 = (bf16[768,768]{1,0:T(8,128)(2,1)}, bf16[768,768]{1,0:T(8,128)(2,1)S(1)}, u32[]{:S(2)}, u32[]{:S(2)}) collective-permute-start(bf16[768,768]{1,0:T(8,128)(2,1)} %collective-permute-done.29), channel_id=1, source_target_pairs={{0,8},{1,9},{2,10},{3,11},{4,12},{5,13},{6,14},{7,15},{8,0},{9,1},... | collective-permute-start | bytes 3538952 | tf_op jit(solution)/shard_map/ppermute | solution.py:235
  367.8 43.3 %collective-permute-start.75 = (bf16[768,768]{1,0:T(8,128)(2,1)}, bf16[768,768]{1,0:T(8,128)(2,1)}, u32[]{:S(2)}, u32[]{:S(2)}) collective-permute-start(bf16[768,768]{1,0:T(8,128)(2,1)} %pad_maximum_fusion.15), channel_id=1, source_target_pairs={{0,16},{1,17},{2,18},{3,19},{4,20},{5,21},{6,22},{7,23},{8,24},{9,... | collective-permute-start | bytes 3538952 | tf_op jit(solution)/shard_map/ppermute | solution.py:235
  381.9 31.8 %collective-permute-start.32 = (bf16[512,1536]{1,0:T(8,128)(2,1)}, bf16[512,1536]{1,0:T(8,128)(2,1)}, u32[]{:S(2)}, u32[]{:S(2)}) collective-permute-start(bf16[512,1536]{1,0:T(8,128)(2,1)} %get-tuple-element.62), channel_id=1, source_target_pairs={{0,4},{1,5},{2,6},{3,7},{4,0},{5,1},{6,2},{7,3},{8,12},{9,13},{10,... | collective-permute-start | bytes 4718600 | tf_op jit(solution)/shard_map/ppermute | solution.py:235
  406.9 29.1 %collective-permute-start.73 = (bf16[768,768]{1,0:T(8,128)(2,1)}, bf16[768,768]{1,0:T(8,128)(2,1)}, u32[]{:S(2)}, u32[]{:S(2)}) collective-permute-start(bf16[768,768]{1,0:T(8,128)(2,1)} %pad_maximum_fusion.14), channel_id=1, source_target_pairs={{0,8},{1,9},{2,10},{3,11},{4,12},{5,13},{6,14},{7,15},{8,0},{9,1},... | collective-permute-start | bytes 3538952 | tf_op jit(solution)/shard_map/ppermute | solution.py:235
  409.5 27.9 %collective-permute-start.77 = (bf16[768,768]{1,0:T(8,128)(2,1)}, bf16[768,768]{1,0:T(8,128)(2,1)}, u32[]{:S(2)}, u32[]{:S(2)}) collective-permute-start(bf16[768,768]{1,0:T(8,128)(2,1)} %pad_maximum_fusion.16), channel_id=1, source_target_pairs={{0,16},{1,17},{2,18},{3,19},{4,20},{5,21},{6,22},{7,23},{8,24},{9,... | collective-permute-start | bytes 3538952 | tf_op jit(solution)/shard_map/ppermute | solution.py:235
  411.0 53.5 %collective-permute-start.31 = (bf16[512,1536]{1,0:T(8,128)(2,1)S(1)}, bf16[512,1536]{1,0:T(8,128)(2,1)S(1)}, u32[]{:S(2)}, u32[]{:S(2)}) collective-permute-start(bf16[512,1536]{1,0:T(8,128)(2,1)S(1)} %copy-done.33), channel_id=1, source_target_pairs={{0,4},{1,5},{2,6},{3,7},{4,0},{5,1},{6,2},{7,3},{8,12},{9,13},{10,... | collective-permute-start | bytes 4718600 | tf_op jit(solution)/shard_map/ppermute | solution.py:235
  413.7 46.7 %collective-permute-start.76 = (bf16[768,768]{1,0:T(8,128)(2,1)}, bf16[768,768]{1,0:T(8,128)(2,1)S(1)}, u32[]{:S(2)}, u32[]{:S(2)}) collective-permute-start(bf16[768,768]{1,0:T(8,128)(2,1)} %add_convert_fusion.3), channel_id=1, source_target_pairs={{0,8},{1,9},{2,10},{3,11},{4,12},{5,13},{6,14},{7,15},{8,0},{9,1},... | collective-permute-start | bytes 3538952 | tf_op jit(solution)/shard_map/ppermute | solution.py:235
  417.7 48.4 %collective-permute-start.33 = (bf16[512,1536]{1,0:T(8,128)(2,1)}, bf16[512,1536]{1,0:T(8,128)(2,1)S(1)}, u32[]{:S(2)}, u32[]{:S(2)}) collective-permute-start(bf16[512,1536]{1,0:T(8,128)(2,1)} %fusion.36), channel_id=1, source_target_pairs={{0,1},{1,0},{2,3},{3,2},{4,5},{5,4},{6,7},{7,6},{8,9},{9,8},{10,11... | collective-permute-start | bytes 4718600 | tf_op jit(solution)/shard_map/ppermute | solution.py:235
  436.1 31.3 %collective-permute-start.37 = (bf16[512,1536]{1,0:T(8,128)(2,1)}, bf16[512,1536]{1,0:T(8,128)(2,1)}, u32[]{:S(2)}, u32[]{:S(2)}) collective-permute-start(bf16[512,1536]{1,0:T(8,128)(2,1)} %get-tuple-element.55), channel_id=1, source_target_pairs={{0,4},{1,5},{2,6},{3,7},{4,0},{5,1},{6,2},{7,3},{8,12},{9,13},{10,... | collective-permute-start | bytes 4718600 | tf_op jit(solution)/shard_map/ppermute | solution.py:235
  437.4 71.2 %collective-permute-start.39 = (bf16[512,1536]{1,0:T(8,128)(2,1)}, bf16[512,1536]{1,0:T(8,128)(2,1)}, u32[]{:S(2)}, u32[]{:S(2)}) collective-permute-start(bf16[512,1536]{1,0:T(8,128)(2,1)} %fusion.34), channel_id=1, source_target_pairs={{0,1},{1,0},{2,3},{3,2},{4,5},{5,4},{6,7},{7,6},{8,9},{9,8},{10,11... | collective-permute-start | bytes 4718600 | tf_op jit(solution)/shard_map/ppermute | solution.py:235
  460.3 73.4 %collective-permute-start.72 = (bf16[768,768]{1,0:T(8,128)(2,1)}, bf16[768,768]{1,0:T(8,128)(2,1)}, u32[]{:S(2)}, u32[]{:S(2)}) collective-permute-start(bf16[768,768]{1,0:T(8,128)(2,1)} %pad_maximum_fusion.13), channel_id=1, source_target_pairs={{0,8},{1,9},{2,10},{3,11},{4,12},{5,13},{6,14},{7,15},{8,0},{9,1},... | collective-permute-start | bytes 3538952 | tf_op jit(solution)/shard_map/ppermute | solution.py:235
  464.6 69.2 %collective-permute-start.74 = (bf16[768,768]{1,0:T(8,128)(2,1)}, bf16[768,768]{1,0:T(8,128)(2,1)S(1)}, u32[]{:S(2)}, u32[]{:S(2)}) collective-permute-start(bf16[768,768]{1,0:T(8,128)(2,1)} %add_convert_fusion.4), channel_id=1, source_target_pairs={{0,16},{1,17},{2,18},{3,19},{4,20},{5,21},{6,22},{7,23},{8,24},{9,... | collective-permute-start | bytes 3538952 | tf_op jit(solution)/shard_map/ppermute | solution.py:235
  466.1 67.7 %collective-permute-start.78 = (bf16[768,768]{1,0:T(8,128)(2,1)}, bf16[768,768]{1,0:T(8,128)(2,1)S(1)}, u32[]{:S(2)}, u32[]{:S(2)}) collective-permute-start(bf16[768,768]{1,0:T(8,128)(2,1)} %add_convert_fusion.2), channel_id=1, source_target_pairs={{0,2},{1,3},{2,0},{3,1},{4,6},{5,7},{6,4},{7,5},{8,10},{9,11},{10,... | collective-permute-start | bytes 3538952 | tf_op jit(solution)/shard_map/ppermute | solution.py:235
  533.1 129.5 %collective-permute-start.64 = (bf16[768,1536]{1,0:T(8,128)(2,1)}, bf16[768,1536]{1,0:T(8,128)(2,1)}, u32[]{:S(2)}, u32[]{:S(2)}) collective-permute-start(bf16[768,1536]{1,0:T(8,128)(2,1)} %convolution_convert_fusion.4), channel_id=1, source_target_pairs={{0,4},{1,5},{2,6},{3,7},{4,0},{5,1},{6,2},{7,3},{8,12},{9,13},{10,... | collective-permute-start | bytes 7077896 | tf_op jit(solution)/shard_map/ppermute | solution.py:235
  536.5 53.1 %collective-permute-start.79 = (bf16[2,192,768]{2,1,0:T(8,128)(2,1)}, bf16[2,192,768]{2,1,0:T(8,128)(2,1)S(1)}, u32[]{:S(2)}, u32[]{:S(2)}) collective-permute-start(bf16[2,192,768]{2,1,0:T(8,128)(2,1)} %fusion.74), channel_id=1, source_target_pairs={{0,4},{1,5},{2,6},{3,7},{4,0},{5,1},{6,2},{7,3},{8,12},{9,13},{10,... | collective-permute-start | bytes 1769480 | tf_op jit(solution)/shard_map/ppermute | solution.py:235
  571.6 45.3 %collective-permute-start.56 = (bf16[384,768]{1,0:T(8,128)(2,1)S(1)}, bf16[384,768]{1,0:T(8,128)(2,1)}, u32[]{:S(2)}, u32[]{:S(2)}) collective-permute-start(bf16[384,768]{1,0:T(8,128)(2,1)S(1)} %convolution_convert_fusion.8), channel_id=1, source_target_pairs={{0,8},{1,9},{2,10},{3,11},{4,12},{5,13},{6,14},{7,15},{8,0},{9,1},... | collective-permute-start | bytes 1769480 | tf_op jit(solution)/shard_map/ppermute | solution.py:235
  573.7 26.2 %collective-permute-start.57 = (bf16[384,768]{1,0:T(8,128)(2,1)}, bf16[384,768]{1,0:T(8,128)(2,1)}, u32[]{:S(2)}, u32[]{:S(2)}) collective-permute-start(bf16[384,768]{1,0:T(8,128)(2,1)} %convolution_convert_fusion.6), channel_id=1, source_target_pairs={{0,8},{1,9},{2,10},{3,11},{4,12},{5,13},{6,14},{7,15},{8,0},{9,1},... | collective-permute-start | bytes 1769480 | tf_op jit(solution)/shard_map/ppermute | solution.py:235
  573.8 29.8 %collective-permute-start.49 = (bf16[384,768]{1,0:T(8,128)(2,1)}, bf16[384,768]{1,0:T(8,128)(2,1)}, u32[]{:S(2)}, u32[]{:S(2)}) collective-permute-start(bf16[384,768]{1,0:T(8,128)(2,1)} %convolution_convert_fusion.11), channel_id=1, source_target_pairs={{0,16},{1,17},{2,18},{3,19},{4,20},{5,21},{6,22},{7,23},{8,24},{9,... | collective-permute-start | bytes 1769480 | tf_op jit(solution)/shard_map/ppermute | solution.py:235
  589.5 31.3 %collective-permute-start.51 = (bf16[384,768]{1,0:T(8,128)(2,1)S(1)}, bf16[384,768]{1,0:T(8,128)(2,1)S(1)}, u32[]{:S(2)}, u32[]{:S(2)}) collective-permute-start(bf16[384,768]{1,0:T(8,128)(2,1)S(1)} %convolution_convert_fusion.10), channel_id=1, source_target_pairs={{0,16},{1,17},{2,18},{3,19},{4,20},{5,21},{6,22},{7,23},{8,24},{9,... | collective-permute-start | bytes 1769480 | tf_op jit(solution)/shard_map/ppermute | solution.py:235
  614.7 16.3 %collective-permute-start.50 = (bf16[384,768]{1,0:T(8,128)(2,1)S(1)}, bf16[384,768]{1,0:T(8,128)(2,1)S(1)}, u32[]{:S(2)}, u32[]{:S(2)}) collective-permute-start(bf16[384,768]{1,0:T(8,128)(2,1)S(1)} %fusion.48), channel_id=1, source_target_pairs={{0,8},{1,9},{2,10},{3,11},{4,12},{5,13},{6,14},{7,15},{8,0},{9,1},... | collective-permute-start | bytes 1769480 | tf_op jit(solution)/shard_map/ppermute | solution.py:235
  616.9 24.1 %collective-permute-start.42 = (bf16[384,768]{1,0:T(8,128)(2,1)S(1)}, bf16[384,768]{1,0:T(8,128)(2,1)S(1)}, u32[]{:S(2)}, u32[]{:S(2)}) collective-permute-start(bf16[384,768]{1,0:T(8,128)(2,1)S(1)} %convolution_convert_fusion.16), channel_id=1, source_target_pairs={{0,8},{1,9},{2,10},{3,11},{4,12},{5,13},{6,14},{7,15},{8,0},{9,1},... | collective-permute-start | bytes 1769480 | tf_op jit(solution)/shard_map/ppermute | solution.py:235
  617.8 23.3 %collective-permute-start.44 = (bf16[384,768]{1,0:T(8,128)(2,1)S(1)}, bf16[384,768]{1,0:T(8,128)(2,1)S(1)}, u32[]{:S(2)}, u32[]{:S(2)}) collective-permute-start(bf16[384,768]{1,0:T(8,128)(2,1)S(1)} %fusion.55), channel_id=1, source_target_pairs={{0,16},{1,17},{2,18},{3,19},{4,20},{5,21},{6,22},{7,23},{8,24},{9,... | collective-permute-start | bytes 1769480 | tf_op jit(solution)/shard_map/ppermute | solution.py:235
  620.9 38.0 %collective-permute-start.41 = (bf16[512,1536]{1,0:T(8,128)(2,1)S(1)}, bf16[512,1536]{1,0:T(8,128)(2,1)S(1)}, u32[]{:S(2)}, u32[]{:S(2)}) collective-permute-start(bf16[512,1536]{1,0:T(8,128)(2,1)S(1)} %slice.653), channel_id=1, source_target_pairs={{0,4},{1,5},{2,6},{3,7},{4,0},{5,1},{6,2},{7,3},{8,12},{9,13},{10,... | collective-permute-start | bytes 4718600 | tf_op jit(solution)/shard_map/ppermute | solution.py:235
  642.1 16.6 %collective-permute-start.45 = (bf16[192,768]{1,0:T(8,128)(2,1)S(1)}, bf16[192,768]{1,0:T(8,128)(2,1)S(1)}, u32[]{:S(2)}, u32[]{:S(2)}) collective-permute-start(bf16[192,768]{1,0:T(8,128)(2,1)S(1)} %broadcast_select_fusion.29), channel_id=1, source_target_pairs={{0,1},{1,0},{2,3},{3,2},{4,5},{5,4},{6,7},{7,6},{8,9},{9,8},{10,11... | collective-permute-start | bytes 884744 | tf_op jit(solution)/shard_map/ppermute | solution.py:235
  644.3 29.0 %collective-permute-start.60 = (bf16[96,768]{1,0:T(8,128)(2,1)S(1)}, bf16[96,768]{1,0:T(8,128)(2,1)S(1)}, u32[]{:S(2)}, u32[]{:S(2)}) collective-permute-start(bf16[96,768]{1,0:T(8,128)(2,1)S(1)} %broadcast_select_fusion.35), channel_id=1, source_target_pairs={{0,2},{1,3},{2,0},{3,1},{4,6},{5,7},{6,4},{7,5},{8,10},{9,11},{10,... | collective-permute-start | bytes 442376 | tf_op jit(solution)/shard_map/ppermute | solution.py:235
  655.6 18.8 %collective-permute-start.53 = (bf16[96,768]{1,0:T(8,128)(2,1)S(1)}, bf16[96,768]{1,0:T(8,128)(2,1)S(1)}, u32[]{:S(2)}, u32[]{:S(2)}) collective-permute-start(bf16[96,768]{1,0:T(8,128)(2,1)S(1)} %broadcast_select_fusion.38), channel_id=1, source_target_pairs={{0,2},{1,3},{2,0},{3,1},{4,6},{5,7},{6,4},{7,5},{8,10},{9,11},{10,... | collective-permute-start | bytes 442376 | tf_op jit(solution)/shard_map/ppermute | solution.py:235
  658.8 17.0 %collective-permute-start.46 = (bf16[96,768]{1,0:T(8,128)(2,1)S(1)}, bf16[96,768]{1,0:T(8,128)(2,1)S(1)}, u32[]{:S(2)}, u32[]{:S(2)}) collective-permute-start(bf16[96,768]{1,0:T(8,128)(2,1)S(1)} %broadcast_select_fusion.41), channel_id=1, source_target_pairs={{0,2},{1,3},{2,0},{3,1},{4,6},{5,7},{6,4},{7,5},{8,10},{9,11},{10,... | collective-permute-start | bytes 442376 | tf_op jit(solution)/shard_map/ppermute | solution.py:235
  670.8 32.5 %collective-permute-start.65 = (bf16[192,1536]{1,0:T(8,128)(2,1)S(1)}, bf16[192,1536]{1,0:T(8,128)(2,1)S(1)}, u32[]{:S(2)}, u32[]{:S(2)}) collective-permute-start(bf16[192,1536]{1,0:T(8,128)(2,1)S(1)} %get-tuple-element.97), channel_id=1, source_target_pairs={{0,16},{1,17},{2,18},{3,19},{4,20},{5,21},{6,22},{7,23},{8,24},{9,... | collective-permute-start | bytes 1769480 | tf_op jit(solution)/shard_map/ppermute | solution.py:235
  672.1 43.4 %collective-permute-start.67 = (bf16[192,1536]{1,0:T(8,128)(2,1)S(1)}, bf16[192,1536]{1,0:T(8,128)(2,1)S(1)}, u32[]{:S(2)}, u32[]{:S(2)}) collective-permute-start(bf16[192,1536]{1,0:T(8,128)(2,1)S(1)} %get-tuple-element.98), channel_id=1, source_target_pairs={{0,16},{1,17},{2,18},{3,19},{4,20},{5,21},{6,22},{7,23},{8,24},{9,... | collective-permute-start | bytes 1769480 | tf_op jit(solution)/shard_map/ppermute | solution.py:235
  674.4 15.8 %collective-permute-start.61 = (bf16[96,768]{1,0:T(8,128)(2,1)S(1)}, bf16[96,768]{1,0:T(8,128)(2,1)S(1)}, u32[]{:S(2)}, u32[]{:S(2)}) collective-permute-start(bf16[96,768]{1,0:T(8,128)(2,1)S(1)} %add_convert_fusion.12), channel_id=1, source_target_pairs={{0,2},{1,3},{2,0},{3,1},{4,6},{5,7},{6,4},{7,5},{8,10},{9,11},{10,... | collective-permute-start | bytes 442376 | tf_op jit(solution)/shard_map/ppermute | solution.py:235
  675.8 17.5 %collective-permute-start.54 = (bf16[96,768]{1,0:T(8,128)(2,1)S(1)}, bf16[96,768]{1,0:T(8,128)(2,1)S(1)}, u32[]{:S(2)}, u32[]{:S(2)}) collective-permute-start(bf16[96,768]{1,0:T(8,128)(2,1)S(1)} %add_convert_fusion.13), channel_id=1, source_target_pairs={{0,2},{1,3},{2,0},{3,1},{4,6},{5,7},{6,4},{7,5},{8,10},{9,11},{10,... | collective-permute-start | bytes 442376 | tf_op jit(solution)/shard_map/ppermute | solution.py:235
  677.6 18.9 %collective-permute-start.47 = (bf16[96,768]{1,0:T(8,128)(2,1)S(1)}, bf16[96,768]{1,0:T(8,128)(2,1)S(1)}, u32[]{:S(2)}, u32[]{:S(2)}) collective-permute-start(bf16[96,768]{1,0:T(8,128)(2,1)S(1)} %add_convert_fusion.14), channel_id=1, source_target_pairs={{0,2},{1,3},{2,0},{3,1},{4,6},{5,7},{6,4},{7,5},{8,10},{9,11},{10,... | collective-permute-start | bytes 442376 | tf_op jit(solution)/shard_map/ppermute | solution.py:235
  690.2 47.1 %collective-permute-start.84 = (f32[2,1536]{1,0:T(2,128)S(1)}, f32[2,1536]{1,0:T(2,128)S(1)}, u32[]{:S(2)}, u32[]{:S(2)}) collective-permute-start(f32[2,1536]{1,0:T(2,128)S(1)} %add.410), channel_id=1, source_target_pairs={{0,16},{1,17},{2,18},{3,19},{4,20},{5,21},{6,22},{7,23},{8,24},{9,... | collective-permute-start | bytes 36872 | tf_op jit(solution)/shard_map/ppermute | solution.py:235
  739.9 16.8 %collective-permute-start.71 = (bf16[96,1536]{1,0:T(8,128)(2,1)S(1)}, bf16[96,1536]{1,0:T(8,128)(2,1)S(1)}, u32[]{:S(2)}, u32[]{:S(2)}) collective-permute-start(bf16[96,1536]{1,0:T(8,128)(2,1)S(1)} %pad_maximum_fusion.32), channel_id=1, source_target_pairs={{0,1},{1,0},{2,3},{3,2},{4,5},{5,4},{6,7},{7,6},{8,9},{9,8},{10,11... | collective-permute-start | bytes 884744 | tf_op jit(solution)/shard_map/ppermute | solution.py:235
  (115 other events, 1360.9 us)

commit v2 on v1

v2 whole, which is shorter than its diff:
```python
import functools

import jax
import jax.numpy as jnp
from jax import lax
from jax.experimental import pallas as pl
from jax.experimental.pallas import tpu as pltpu
from jax.sharding import PartitionSpec as P

HEADS = 12
HEAD_DIM = 128
BLOCK = 768
AXES = ("dp", "mp")
PAIR = 2
LANES = PAIR * HEAD_DIM

epsilon = 1e-05
theta_base = 10000.0
score_scale = HEAD_DIM ** (-0.5)
contract_rows = (((0,), (0,)), ((), ()))
contract_cols = (((1,), (1,)), ((), ()))
f32 = jnp.float32
bf16 = jnp.bfloat16
VMEM_LIMIT = 56 * 1024 * 1024
SMEM_SPEC = pl.BlockSpec(memory_space=pltpu.SMEM)
VMEM_SPEC = pl.BlockSpec(memory_space=pltpu.VMEM)


def rotary_tables(length, head_width):
    halfway = head_width // 2
    frequency = theta_base ** (-2.0 * jnp.arange(halfway, dtype=f32) / head_width)
    angles = jnp.arange(length, dtype=f32)[:, None] * frequency[None, :]
    angles = jnp.concatenate([angles, angles], axis=1)
    return (jnp.cos(angles), jnp.sin(angles))


def turn(values):
    halfway = values.shape[-1] // 2
    return jnp.concatenate([-values[:, halfway:], values[:, :halfway]], axis=-1)


def turn_back(values):
    halfway = values.shape[-1] // 2
    return jnp.concatenate([values[:, halfway:], -values[:, :halfway]], axis=-1)


def at(start, size):
    return pl.ds(pl.multiple_of(start, size), size)


def lanes(start, size):
    return pl.ds(pl.multiple_of(start, 128), size)


def normal_of(values):
    average = jnp.mean(values, axis=-1, keepdims=True)
    centred = values - average
    variance = jnp.mean(centred * centred, axis=-1, keepdims=True)
    inverse = lax.rsqrt(variance + epsilon)
    return centred * inverse, inverse


def norm_back(grad, normal, inverse, gain):
    scaled = grad * gain
    mean = jnp.mean(scaled, axis=-1, keepdims=True)
    mean_normal = jnp.mean(scaled * normal, axis=-1, keepdims=True)
    return (scaled - mean - normal * mean_normal) * inverse


COST = pl.CostEstimate(flops=1000000, bytes_accessed=0, transcendentals=0)


def run(name, kernel, outs, scalars, *args, scratch=()):
    many = isinstance(outs, (tuple, list))
    return pl.pallas_call(
        kernel,
        out_shape=outs,
        in_specs=[SMEM_SPEC] * len(scalars) + [VMEM_SPEC] * len(args),
        out_specs=[VMEM_SPEC] * len(outs) if many else VMEM_SPEC,
        scratch_shapes=list(scratch),
        cost_estimate=COST,
        compiler_params=pltpu.CompilerParams(vmem_limit_bytes=VMEM_LIMIT),
        name=name,
    )(*scalars, *args)


def shape(dims, kind=bf16):
    return jax.ShapeDtypeStruct(tuple(dims), kind)


def cut_attention_kernel(place, own_qkv, got_qkv, *outs):
    core = place[0]
    rows, width = own_qkv.shape
    width = width // 3
    half = width // 2
    mine, theirs = at(core * rows, rows), at((1 - core) * rows, rows)
    for p, out in enumerate(outs):
        for part in range(3):
            cols = lanes(core * half + (part * width + p * LANES), LANES)
            here = slice(part * LANES, (part + 1) * LANES)
            out[mine, here] = own_qkv[:, cols]
            out[theirs, here] = got_qkv[:, cols]


def cut_rest_kernel(place, own_out, own_up, own_down, got, out_piece, out_piece_got, ff_piece):
    core = place[0]
    rows, width = own_out.shape
    half = width // 2
    for out, part in ((out_piece, core), (out_piece_got, 1 - core)):
        cols = lanes(part * half, half)
        out[at(core * rows, rows), :] = own_out[:, cols]
        out[at((1 - core) * rows, rows), :] = got[:rows, cols]
    half = own_up.shape[1] // 2
    cols = lanes(core * half, half)
    units = own_up.shape[1]
    for i, own in enumerate((own_up, own_down)):
        ff_piece[at(core * rows + i * 2 * rows, rows), :] = own[:, cols]
        if units == width:
            ff_piece[at((1 - core) * rows + i * 2 * rows, rows), :] = got[(1 + i) * rows : (2 + i) * rows, cols]
        else:
            cols_got = lanes(core * half + i * units, half)
            ff_piece[at((1 - core) * rows + i * 2 * rows, rows), :] = got[rows:, cols_got]


def join(place, chips, pieces, outs):
    parts = len(outs)
    span = pieces[0].shape[0] // parts
    for j in range(min(chips, len(pieces))):
        for i, out in enumerate(outs):
            rows = at(place[1 + j], span)
            if len(pieces) == chips or j < chips - 1:
                out[rows, :] = pieces[j][i * span : (i + 1) * span, :]
            elif parts == 1:
                half = span // 2
                out[pl.ds(pl.multiple_of(place[1 + j], half), half), :] = pieces[j][...]
                out[pl.ds(pl.multiple_of(place[1 + j] + half, half), half), :] = pieces[j + 1][...]
            else:
                out[rows, :] = pieces[j + i][...]


def join_kernel(chips, many, place, *refs):
    *pieces, mine, got = refs
    join(place, chips, pieces[:many], [mine])
    join(place, chips, pieces[many:], [got])


def norm_kernel(own, other, gain, bias, out):
    seq_len = own.shape[0]
    block = 128

    def step(i, carry):
        rows = at(i * block, block)
        for k, ref in enumerate((own, other)):
            normal, _ = normal_of(ref[rows, :].astype(f32))
            out[at(k * seq_len + i * block, block), :] = (normal * gain[...] + bias[...]).astype(bf16)
        return carry

    lax.fori_loop(0, seq_len // block, step, 0)


def allowed_block(seg_col, seg_row, row_start, block, extent):
    row_place = row_start + lax.broadcasted_iota(jnp.int32, (block, extent), 0)
    col_place = lax.broadcasted_iota(jnp.int32, (block, extent), 1)
    return (row_place >= col_place) & (seg_col == seg_row)


def attend_kernel(chips, seq_len, place, norm_ref, cos_ref, sin_ref, segc_ref, segr_ref, *refs):
    *pieces, wide_ref, qkv_ref, ctx_ref, lse_ref = refs
    join(place, chips, pieces, [wide_ref])
    hd = HEAD_DIM
    block = seq_len // 2

    def project(i, carry):
        rows = at(i * block, block)
        joined = jnp.dot(norm_ref[rows, :], wide_ref[...], preferred_element_type=f32)
        table = at((i % 2) * block, block)
        cosine, sine = cos_ref[table, :], sin_ref[table, :]
        for h in range(2 * PAIR):
            part = joined[:, h * hd : (h + 1) * hd]
            qkv_ref[rows, h * hd : (h + 1) * hd] = (part * cosine + turn(part) * sine).astype(bf16)
        qkv_ref[rows, 2 * PAIR * hd :] = joined[:, 2 * PAIR * hd :].astype(bf16)
        return carry

    lax.fori_loop(0, 4, project, 0)

    lane = lax.broadcasted_iota(jnp.int32, (block, hd), 1)

    def sequence(s, carry):
        base = s * seq_len
        for r in range(2):
            extent = (r + 1) * block
            rows = at(base + r * block, block)
            cols = pl.ds(pl.multiple_of(base, block), extent)
            allowed = allowed_block(
                segc_ref[s, r * block : (r + 1) * block, :],
                segr_ref[s, :, :extent],
                r * block,
                block,
                extent,
            )
            logs = jnp.zeros((block, hd), f32)
            for h in range(PAIR):
                query = qkv_ref[rows, h * hd : (h + 1) * hd]
                key = qkv_ref[cols, (PAIR + h) * hd : (PAIR + h + 1) * hd]
                value = qkv_ref[cols, (2 * PAIR + h) * hd : (2 * PAIR + h + 1) * hd]
                scores = lax.dot_general(query, key, contract_cols, preferred_element_type=f32)
                scores = jnp.where(allowed, scores * score_scale, -1000000000.0)
                top = jnp.max(scores, axis=-1, keepdims=True)
                weight = jnp.exp(scores - top)
                total = jnp.sum(weight, axis=-1, keepdims=True)
                probs = (weight * (1.0 / total)).astype(bf16)
                ctx_ref[s, r * block : (r + 1) * block, h * hd : (h + 1) * hd] = jnp.dot(
                    probs, value, preferred_element_type=f32
                ).astype(bf16)
                logs = jnp.where(lane == h, top + jnp.log(total), logs)
            lse_ref[rows, :] = logs
        return carry

    lax.fori_loop(0, 2, sequence, 0)


def out_kernel(chunks, place, x_ref, *refs):
    mine, got = refs[:chunks], refs[chunks : 2 * chunks]
    w_mine, w_got, gain, bias, hidden, norm, ctx = refs[2 * chunks :]
    core = place[0]
    seq_len, width = x_ref.shape
    half = width // 2
    own_cols, got_cols = lanes(core * half, half), lanes((1 - core) * half, half)
    for p in range(chunks):
        here = lanes(core * half + p * LANES, LANES)
        there = lanes((1 - core) * half + p * LANES, LANES)
        ctx[:, here] = mine[p][...]
        ctx[:, there] = got[p][...]
    block = 128

    def step(i, carry):
        rows = at(i * block, block)
        hidden[rows, own_cols] = jnp.dot(ctx[rows, :], w_mine[...], preferred_element_type=f32)
        hidden[rows, got_cols] = jnp.dot(ctx[rows, :], w_got[...], preferred_element_type=f32)
        values = hidden[rows, :] + x_ref[rows, :].astype(f32)
        hidden[rows, :] = values
        normal, _ = normal_of(values)
        norm[rows, :] = (normal * gain[...] + bias[...]).astype(bf16)
        return carry

    lax.fori_loop(0, seq_len // block, step, 0)


def out_back_kernel(place, grad, w_mine, w_got, keep, send, grad_send):
    core = place[0]
    seq_len, width = grad.shape
    half = width // 2
    own_cols, got_cols = lanes(core * half, half), lanes((1 - core) * half, half)
    grad_send[...] = grad[:, got_cols]
    for out, part in ((send, 1 - core), (keep, core)):
        rows = at(part * half, half)

        def step(i, carry):
            here = at(i * 256, 256)
            out[here, :] = (
                lax.dot_general(grad[here, own_cols], w_mine[rows, :], contract_cols, preferred_element_type=f32)
                + lax.dot_general(grad[here, got_cols], w_got[rows, :], contract_cols, preferred_element_type=f32)
            ).astype(bf16)
            return carry

        lax.fori_loop(0, seq_len // 256, step, 0)


def spread(place, outs, product):
    if len(outs) > 1:
        span = outs[0].shape[0]
        for j, out in enumerate(outs[:3]):
            out[...] = product(lanes(place[1 + j], span)).astype(bf16)
        corner = product(lanes(place[4], span)).astype(bf16)
        outs[3][...] = corner[: span // 2, :]
        outs[4][...] = corner[span // 2 :, :]
    else:
        for start in range(0, outs[0].shape[0], 256):
            here = slice(start, start + 256)
            outs[0][here, :] = product(here).astype(bf16)


def out_weight_kernel(chunks, place, ctx, grad, grad_got, *refs):
    mine, got, outs, other = refs[:chunks], refs[chunks : 2 * chunks], refs[2 * chunks : -1], refs[-1]
    core = place[0]
    seq_len, width = grad.shape
    half = width // 2
    cols = lanes(core * half, half)
    for p in range(chunks):
        other[:, lanes(core * half + p * LANES, LANES)] = mine[p][...]
        other[:, lanes((1 - core) * half + p * LANES, LANES)] = got[p][...]

    def product(here):
        return lax.dot_general(
            ctx[:, here], grad[:, cols], contract_rows, preferred_element_type=f32
        ) + lax.dot_general(other[:, here], grad_got[...], contract_rows, preferred_element_type=f32)

    spread(place, outs, product)


def attend_back_kernel(
    chunk, place, qkv_ref, lse_ref, keep, got, norm, cos_ref, sin_ref, segc_ref, segr_ref, out_ref, *refs
):
    *pieces, gq, gk, gv = refs
    hd = HEAD_DIM
    seq_len = keep.shape[0]
    block = seq_len // 2
    for s, grad_ref in enumerate((keep, got)):
        base = s * seq_len
        for h in range(PAIR):
            lane = slice(chunk * LANES + h * hd, chunk * LANES + (h + 1) * hd)
            for r in (1, 0):
                extent = (r + 1) * block
                rows = slice(base + r * block, base + (r + 1) * block)
                cols = slice(base, base + extent)
                allowed = allowed_block(
                    segc_ref[s, r * block : (r + 1) * block, :],
                    segr_ref[s, :, :extent],
                    r * block,
                    block,
                    extent,
                )
                query = qkv_ref[rows, h * hd : (h + 1) * hd]
                key = qkv_ref[cols, (PAIR + h) * hd : (PAIR + h + 1) * hd]
                value = qkv_ref[cols, (2 * PAIR + h) * hd : (2 * PAIR + h + 1) * hd]
                grad = grad_ref[r * block : (r + 1) * block, lane]
                scores = lax.dot_general(query, key, contract_cols, preferred_element_type=f32)
                scores = jnp.where(allowed, scores * score_scale, -1000000000.0)
                probs = jnp.exp(scores - lse_ref[rows, h : h + 1])
                grad_probs = lax.dot_general(grad, value, contract_cols, preferred_element_type=f32)
                weighted = jnp.sum(probs * grad_probs, axis=-1, keepdims=True)
                grad_scores = (probs * (grad_probs - weighted) * score_scale).astype(bf16)
                probs = probs.astype(bf16)
                gq[r * block : (r + 1) * block, :] = jnp.dot(grad_scores, key, preferred_element_type=f32)
                grad_key = lax.dot_general(grad_scores, query, contract_rows, preferred_element_type=f32)
                grad_value = lax.dot_general(probs, grad, contract_rows, preferred_element_type=f32)
                if r == 1:
                    gk[...] = grad_key
                    gv[...] = grad_value
                else:
                    gk[:block, :] = gk[:block, :] + grad_key
                    gv[:block, :] = gv[:block, :] + grad_value
            sine, cosine = sin_ref[...], cos_ref[...]
            rows = slice(base, base + seq_len)
            grad_query, grad_key = gq[...], gk[...]
            out_ref[rows, h * hd : (h + 1) * hd] = (
                grad_query * cosine + turn_back(grad_query * sine)
            ).astype(bf16)
            out_ref[rows, (PAIR + h) * hd : (PAIR + h + 1) * hd] = (
                grad_key * cosine + turn_back(grad_key * sine)
            ).astype(bf16)
            out_ref[rows, (2 * PAIR + h) * hd : (2 * PAIR + h + 1) * hd] = gv[...].astype(bf16)

    def product(here):
        return lax.dot_general(norm[:, here], out_ref[...], contract_rows, preferred_element_type=f32)

    spread(place, pieces, product)


def ff_act_kernel(chips, place, limits, norm_a, norm_b, cot_a, cot_b, *refs):
    if chips:
        *pieces, act_a, act_b, grad_a, grad_b, up, down = refs
        join(place, chips, pieces, [up, down])
    else:
        up, down, act_a, act_b, grad_a, grad_b = refs
    seq_len = norm_a.shape[0]
    units = up.shape[1]
    block, tile = 256, 256 if units % 256 == 0 else 128
    for s, (norm, cot, act, grad) in enumerate(((norm_a, cot_a, act_a, grad_a), (norm_b, cot_b, act_b, grad_b))):
        limit = limits[s]

        def step(i, carry):
            rows = at(i * block, block)
            for n in range(0, units, tile):
                cols = slice(n, n + tile)
                preact = jnp.dot(norm[rows, :], up[:, cols], preferred_element_type=f32)
                grad_active = jnp.dot(cot[rows, :], down[:, cols], preferred_element_type=f32)
                mask = n + lax.broadcasted_iota(jnp.int32, (block, tile), 1) < limit
                cdf = 0.5 * (1.0 + lax.erf(preact * 0.7071067811865476))
                slope = cdf + preact * jnp.exp(-0.5 * preact * preact) * 0.3989422804014327
                act[rows, cols] = jnp.where(mask, preact * cdf, 0.0).astype(bf16)
                grad[rows, cols] = jnp.where(mask, grad_active * slope, 0.0).astype(bf16)
            return carry

        lax.fori_loop(0, seq_len // block, step, 0)


def rows_back_kernel(count, base, *refs):
    grads, weights, outs = refs[:count], refs[count : 2 * count], refs[2 * count :]
    total = outs[0].shape[0]
    for k, out in enumerate(outs):

        def step(i, carry):
            rows = at(base + k * total + i * 256, 256)
            acc = 0.0
            for g, w in zip(grads, weights):
                acc = acc + lax.dot_general(g[rows, :], w[...], contract_cols, preferred_element_type=f32)
            out[at(i * 256, 256), :] = acc.astype(out.dtype)
            return carry

        lax.fori_loop(0, total // 256, step, 0)


def ff_weight_kernel(count, place, *refs):
    norms, cots = refs[:count], refs[count : 2 * count]
    acts, grads, outs = refs[2 * count : 3 * count], refs[3 * count : 4 * count], refs[4 * count :]
    span = norms[0].shape[1]
    corner = len(outs) == 5
    for j in range(4 if corner else len(outs)):

        @pl.when(pl.program_id(0) == j)
        def _():
            for i, (lefts, rights) in enumerate(((norms, grads), (cots, acts))):
                acc = 0.0
                for left, right in zip(lefts, rights):
                    acc = acc + lax.dot_general(
                        left[...], right[...], contract_rows, preferred_element_type=f32
                    )
                if corner and j == 3:
                    outs[3 + i][...] = acc.astype(bf16)
                else:
                    outs[j][i * span : (i + 1) * span, :] = acc.astype(bf16)


def ff_weight(order, chips, norms, cots, acts, grads):
    seq_len, width = norms[0].shape
    units = acts[0].shape[1]
    span = width // chips
    count = len(norms)
    outs = [(2 * span, units)] * chips
    if chips == 4:
        outs = [(2 * span, units)] * 3 + [(span, units)] * 2
    wide = pl.BlockSpec((seq_len, span), lambda j, order: (0, order[j]))
    whole = pl.BlockSpec((seq_len, units), lambda j, order: (0, 0))
    return pl.pallas_call(
        functools.partial(ff_weight_kernel, count),
        out_shape=[shape(v) for v in outs],
        grid_spec=pltpu.PrefetchScalarGridSpec(
            num_scalar_prefetch=1,
            grid=(chips,),
            in_specs=[wide] * (2 * count) + [whole] * (2 * count),
            out_specs=[pl.BlockSpec(v, lambda j, order: (0, 0)) for v in outs],
        ),
        cost_estimate=COST,
        compiler_params=pltpu.CompilerParams(vmem_limit_bytes=VMEM_LIMIT),
        name="ff_weight",
    )(order, *norms, *cots, *acts, *grads)


def second_back_kernel(own, beside_a, beside_b, near, hidden, cot, gain, grad_hidden, grad_low, sums):
    seq_len, width = own.shape
    block = 64
    sums[...] = jnp.zeros_like(sums)

    def step(i, carry, first, beside):
        rows = at(first + i * block, block)
        grad = own[rows, :] + beside[at(i * block, block), :].astype(f32) + near[rows, :].astype(f32)
        normal, inverse = normal_of(hidden[rows, :])
        sums[0:1, :] += jnp.sum(grad * normal, axis=0, keepdims=True)
        sums[1:2, :] += jnp.sum(grad, axis=0, keepdims=True)
        back = cot[rows, :].astype(f32) + norm_back(grad, normal, inverse, gain[...])
        grad_hidden[rows, :] = back
        grad_low[rows, :] = back.astype(bf16)
        return carry

    for k, ref in enumerate((beside_a, beside_b)):
        part = functools.partial(step, first=k * seq_len // 2, beside=ref)
        lax.fori_loop(0, seq_len // 2 // block, part, 0)


def first_back_kernel(own, beside_a, beside_b, x_ref, grad_hidden, gain, out, sums):
    seq_len, width = own.shape
    block = 64
    sums[...] = jnp.zeros_like(sums)

    def step(i, carry, first, beside):
        rows = at(first + i * block, block)
        grad = own[rows, :] + beside[at(i * block, block), :].astype(f32)
        normal, inverse = normal_of(x_ref[rows, :].astype(f32))
        sums[0:1, :] += jnp.sum(grad * normal, axis=0, keepdims=True)
        sums[1:2, :] += jnp.sum(grad, axis=0, keepdims=True)
        out[rows, :] = grad_hidden[rows, :] + norm_back(grad, normal, inverse, gain[...])
        return carry

    for k, ref in enumerate((beside_a, beside_b)):
        part = functools.partial(step, first=k * seq_len // 2, beside=ref)
        lax.fori_loop(0, seq_len // 2 // block, part, 0)


def place_attention_kernel(count, place, *refs):
    mine, got, out = refs[:count], refs[count : 2 * count], refs[2 * count]
    core = place[0]
    rows = out.shape[0]
    width = out.shape[1] // 3
    half = width // 2
    here = at(core * rows, rows)
    for p in range(count):
        for part in range(3):
            cols = slice(part * LANES, (part + 1) * LANES)
            base = part * width + p * LANES
            out[:, lanes(core * half + base, LANES)] = mine[p][here, cols].astype(f32)
            out[:, lanes((1 - core) * half + base, LANES)] = got[p][here, cols].astype(f32)


def place_halves_kernel(place, *refs):
    mine, got, outs = refs[0], refs[1], refs[2:]
    core = place[0]
    rows = outs[0].shape[0]
    half = outs[0].shape[1] // 2
    for i, out in enumerate(outs):
        here = at(core * rows + i * 2 * rows, rows)
        out[:, lanes(core * half, half)] = mine[here, :].astype(f32)
        out[:, lanes((1 - core) * half, half)] = got[here, :].astype(f32)


def tie(value, *others):
    return lax.optimization_barrier((value, *others))[0]


def build(dp_size, mp_size):
    total = dp_size * mp_size
    chip_bits = []
    bit = 2 * mp_size
    while bit < total:
        chip_bits.append(bit)
        bit *= 2
    core_bit = mp_size
    near_bit = 1
    far_bits = []
    bit = 2
    while bit < mp_size:
        far_bits.append(bit)
        bit *= 2
    chips = dp_size // 2

    def flip(value, bit):
        return lax.ppermute(value, AXES, [(i, i ^ bit) for i in range(total)])

    def add(a, b):
        return a.astype(f32) + b.astype(f32)

    def add_low(a, b):
        return add(a, b).astype(bf16)

    class Line:
        def __init__(self):
            self.last = []
            self.open = {}

        def end(self, *values):
            for v in values:
                self.open.pop(id(v), None)

        def after(self, value, *waits):
            self.end(value, *waits)
            waits = list(waits) + self.last
            return tie(value, *waits) if waits else value

        def wait(self, *transfers):
            self.end(*transfers)
            self.last = self.last + list(transfers)

        def send(self, value, bit):
            result = flip(self.after(value), bit)
            self.open[id(result)] = (result, bit)
            return result

        def kernel(self, name, kernel, outs, scalars, *args, wait=(), scratch=()):
            self.end(*args)
            args = (self.after(args[0], *wait),) + args[1:]
            result = run(name, kernel, outs, scalars, *args, scratch=scratch)
            self.last = [result[0] if isinstance(result, (tuple, list)) else result]
            return result

        def op(self, function, *args):
            self.end(*args)
            result = function(self.after(args[0]), *args[1:])
            self.last = [result[0] if isinstance(result, (tuple, list)) else result]
            return result

    two = len(chip_bits) == 2

    class Gather:
        def __init__(self, line, piece):
            self.line, self.piece = line, piece
            if two:
                self.x = line.send(piece, chip_bits[0])
                self.y = line.send(piece, chip_bits[1])
            else:
                held = [line.after(piece)]
                for bit in chip_bits:
                    held = held + [flip(value, bit) for value in held]
                self.all = held

        def turn(self):
            if two:
                half = self.piece.shape[0] // 2
                self.line.wait(self.x, self.y)
                low = self.line.op(lambda v: v[:half], self.x)
                self.low = self.line.send(low, chip_bits[1])
                high = self.line.op(lambda v: v[half:], self.y)
                self.high = self.line.send(high, chip_bits[0])

        def wait(self):
            if two:
                self.line.wait(self.low, self.high)

        def send_first(self, bit):
            if two:
                return [self.line.send(v, bit) for v in (self.x, self.y)]
            return [flip(v, bit) for v in self.all[1:]]

        def send_last(self, bit):
            if two:
                corner = self.line.op(lambda a, b: jnp.concatenate([a, b]), self.low, self.high)
                return [self.line.send(corner, bit)]
            return []

        def pieces(self):
            return [self.piece, self.x, self.y, self.low, self.high] if two else self.all

    class Scatter:
        def __init__(self, line, parts):
            self.line, self.parts = line, parts
            if two:
                self.low = line.send(parts[3], chip_bits[0])
                self.high = line.send(parts[4], chip_bits[1])

        def turn(self):
            if two:
                _, to_x, to_y, low, high = self.parts
                half = low.shape[0]
                self.line.wait(self.low, self.high)
                to_y = self.line.op(lambda v, g: v.at[:half].set(add_low(v[:half], g)), to_y, self.low)
                self.y = self.line.send(to_y, chip_bits[1])
                to_x = self.line.op(lambda v, g: v.at[half:].set(add_low(v[half:], g)), to_x, self.high)
                self.x = self.line.send(to_x, chip_bits[0])

        def close(self):
            if two:
                return self.line.op(
                    lambda own, a, b: (add(own, a) + b.astype(f32)).astype(bf16),
                    self.parts[0],
                    self.x,
                    self.y,
                )
            held = list(self.parts)
            for bit in reversed(chip_bits):
                middle = len(held) // 2
                held = [add_low(a, flip(b, bit)) for a, b in zip(held[:middle], held[middle:])]
            return held[0]

    class OverMp:
        def __init__(self, line, share):
            self.line = line
            size = share.shape[0] // 2
            self.upper = lax.axis_index("mp") % 2
            send = line.op(lambda v: lax.dynamic_slice_in_dim(v, (1 - self.upper) * size, size, axis=0), share)
            self.keep = lax.dynamic_slice_in_dim(share, self.upper * size, size, axis=0)
            self.got = line.send(send, near_bit)

        def turn(self):
            value = self.line.op(add_low, self.keep, self.got)
            for bit in far_bits[:-1]:
                value = add_low(value, flip(value, bit))
            self.keep = value
            self.got = self.line.send(value, far_bits[-1])

        def back(self):
            self.keep = self.line.op(add_low, self.keep, self.got)
            self.got = self.line.send(self.keep, near_bit)

        def close(self):
            def joined(keep, got):
                low = jnp.where(self.upper == 0, keep, got)
                return jnp.concatenate([low, jnp.where(self.upper == 0, got, keep)])

            return self.line.op(joined, self.keep, self.got)

    class SumAll:
        def __init__(self, line, value):
            self.line, self.value, self.bit = line, value, 1
            self.got = line.send(value, 1)

        def turn(self):
            if self.bit < total:
                self.value = self.line.op(jnp.add, self.value, self.got)
                self.bit *= 2
                if self.bit < total:
                    self.got = self.line.send(self.value, self.bit)

        def close(self):
            while self.bit < total:
                self.turn()
            return self.value

    def on_device(
        block_in,
        cotangent,
        segment_ids,
        granularity,
        w_qkv,
        w_out,
        w_up,
        w_down,
        norm1_gain,
        norm1_bias,
        norm2_gain,
        norm2_bias,
    ):
        seq_len, width = block_in.shape
        rows = width // dp_size
        units = w_up.shape[1]
        half_units = units // 2
        half = width // 2
        dp = lax.axis_index("dp")
        mp = lax.axis_index("mp")
        core = dp % 2
        chip = dp // 2
        span = 2 * rows
        order = jnp.stack([chip ^ j for j in range(chips)]).astype(jnp.int32)
        place = jnp.concatenate([core[None].astype(jnp.int32), order * span])
        chunks = HEADS // 2 // PAIR
        chunk_cols = 3 * LANES
        gain1, bias1 = norm1_gain[None], norm1_bias[None]
        gain2, bias2 = norm2_gain[None], norm2_bias[None]
        line = Line()

        def parts_shapes(cols):
            if span % 128 == 0 and chips == 4:
                return [shape((span, cols))] * 3 + [shape((rows, cols))] * 2
            return [shape((width, cols))]

        def by_chip(parts):
            if len(parts) > 1:
                return parts
            return [lax.dynamic_slice_in_dim(parts[0], place[1 + j], span, axis=0) for j in range(chips)]

        def ff_parts(*groups):
            if span % 128 == 0 and chips == 4:
                return ff_weight(order, chips, *groups)
            blocks = width // 256
            parts = ff_weight(jnp.arange(blocks, dtype=jnp.int32), blocks, *groups)
            sides = [
                by_chip([jnp.concatenate([v[i * 256 : (i + 1) * 256] for v in parts])]) for i in range(2)
            ]
            return [jnp.concatenate(v) for v in zip(*sides)]

        w_down_t = w_down.T
        qkv_other = line.send(w_qkv, core_bit)
        tokens = jnp.concatenate([block_in, cotangent])
        tokens_other = line.send(tokens, core_bit)
        if units == width:
            rest = jnp.concatenate([w_out, w_up, w_down_t])
        else:
            rest = jnp.concatenate([w_out, jnp.concatenate([w_up, w_down_t], axis=1)])
        rest_other = line.send(rest, core_bit)
        small = jnp.concatenate([segment_ids, jnp.broadcast_to(granularity[:, None], (mp_size, seq_len))])
        small_other = line.send(small, core_bit)

        qkv_pieces = line.kernel(
            "cut_attention",
            cut_attention_kernel,
            [shape((span, chunk_cols))] * chunks,
            [place],
            w_qkv,
            qkv_other,
        )
        heads = [Gather(line, qkv_pieces[0])]
        normed1 = line.kernel(
            "norm",
            norm_kernel,
            shape((2 * seq_len, width)),
            [],
            block_in,
            tokens_other,
            gain1,
            bias1,
        )
        out_piece, out_piece_got, ff_piece = line.kernel(
            "cut_rest",
            cut_rest_kernel,
            [shape((span, half))] * 2 + [shape((2 * span, half_units))],
            [place],
            w_out,
            w_up,
            w_down_t,
            rest_other,
            wait=(small_other,),
        )
        heads.append(Gather(line, qkv_pieces[1]))
        small_other = line.after(small_other)
        segments = jnp.stack([small[0], small_other[0]])
        seg_col = segments[:, :, None]
        seg_row = segments[:, None, :]
        cosine, sine = rotary_tables(seq_len, HEAD_DIM)
        levels = jnp.stack([small[1:, 0], small_other[1:, 0]])
        limits = BLOCK * jnp.power(2, levels)
        limits = jnp.stack([limits[0, mp], limits[1, mp], limits[0, mp ^ 1], limits[1, mp ^ 1]])
        starts = [(mp ^ (2 * k)) * units + core * half_units for k in range(mp_size // 2)]
        limits = [(limits - start).astype(jnp.int32) for start in starts]
        last = mp_size // 2 - 1

        qkv_wide, qkv_low, contexts, logs = [], [], [], []

        def attend(p):
            a, b, c, d = line.kernel(
                "attend",
                functools.partial(attend_kernel, chips, seq_len),
                [
                    shape((width, chunk_cols)),
                    shape((2 * seq_len, chunk_cols)),
                    shape((2, seq_len, LANES)),
                    shape((2 * seq_len, HEAD_DIM), f32),
                ],
                [place],
                normed1,
                cosine,
                sine,
                seg_col,
                seg_row,
                *heads[p].pieces(),
            )
            qkv_wide.append(a)
            qkv_low.append(b)
            contexts.append(c)
            logs.append(d)

        heads[0].turn()
        slices = [ff_piece]
        for bit in far_bits:
            slices = slices + [line.send(v, bit) for v in slices]
        heads[1].turn()
        heads[0].wait()
        heads.append(Gather(line, qkv_pieces[2]))
        attend(0)
        heads[1].wait()
        heads[2].turn()
        outs = Gather(line, out_piece)
        attend(1)
        heads[2].wait()
        ctx_near = [line.send(c[1], core_bit) for c in contexts]
        outs.turn()
        line.wait(*ctx_near)
        outs_other = [out_piece_got] + outs.send_first(core_bit)
        line.wait(*outs_other[1:], *slices[1:])
        ffs = {last: Gather(line, slices[last])}
        cot_near = line.send(cotangent, near_bit)
        attend(2)
        outs.wait()
        ctx_near.append(line.send(contexts[2][1], core_bit))
        outs_other += outs.send_last(core_bit)
        out_mine, out_got = line.kernel(
            "join",
            functools.partial(join_kernel, chips, len(outs.pieces())),
            [shape((width, half))] * 2,
            [place],
            *outs.pieces(),
            *outs_other,
        )
        line.wait(ctx_near[2])
        ffs[last].turn()
        hidden1, normed2, context = line.kernel(
            "out",
            functools.partial(out_kernel, chunks),
            [shape((seq_len, width), f32), shape((seq_len, width)), shape((seq_len, width))],
            [place],
            block_in,
            *[c[0] for c in contexts],
            *ctx_near,
            out_mine,
            out_got,
            gain2,
            bias2,
        )

        norm_near = line.send(normed2, near_bit)
        norm_core = line.send(normed2, core_bit)
        ffs[last].wait()
        line.wait(norm_core, cot_near)
        for k in range(last - 1, -1, -1):
            ffs[k] = Gather(line, slices[k])
        cot_both = line.send(cot_near, core_bit)
        cot_core = line.after(tokens_other)[seq_len:]
        cot_rows = [cotangent, cot_core, cot_near, cot_both]
        outs_ff = [shape((seq_len, half_units))] * 4
        wide_ff = [shape((width, half_units))] * 2
        acts, grads, ups, downs = {}, {}, {}, {}

        def ff_own(k):
            act_a, act_b, grad_a, grad_b, up, down = line.kernel(
                "ff_own",
                functools.partial(ff_act_kernel, chips),
                outs_ff + wide_ff,
                [place, limits[k][:2]],
                normed2,
                norm_core,
                *cot_rows[:2],
                *ffs[k].pieces(),
            )
            acts[k] = [act_a, act_b]
            grads[k] = [grad_a, grad_b]
            ups[k] = up
            downs[k] = down

        def ff_near(k):
            act_a, act_b, grad_a, grad_b = line.kernel(
                "ff_near",
                functools.partial(ff_act_kernel, 0),
                outs_ff,
                [place, limits[k][2:]],
                norm_near,
                norm_both,
                *cot_rows[2:],
                ups[k],
                downs[k],
            )
            acts[k] += [act_a, act_b]
            grads[k] += [grad_a, grad_b]

        def ff_grads(k):
            lefts = [line.after(normed2), norm_core, norm_near, norm_both]
            parts = ff_parts(lefts, cot_rows, acts[k], grads[k])
            line.last = [parts[0]]
            return Scatter(line, parts)

        def rows_back(name, lefts, i, weights, kind):
            outs = [shape((seq_len, width), kind)] if kind == f32 else [shape((seq_len // 2, width))] * 2
            result = line.kernel(
                name,
                functools.partial(rows_back_kernel, len(weights), 0),
                outs,
                [],
                *[v[i] for v in lefts.values()],
                *weights.values(),
            )
            return result[0] if kind == f32 else result

        def add_halves(a, low, high):
            middle = a.shape[0] // 2
            return jnp.concatenate([add_low(a[:middle], low), add_low(a[middle:], high)])

        ff_own(last)
        line.wait(cot_both)
        for k in range(last - 1, -1, -1):
            ffs[k].turn()
        line.wait(norm_near)
        norm_both = line.send(norm_near, core_bit)
        ctx_far = [line.send(c[0], core_bit) for c in contexts[:2]]
        ff_near(last)
        ctx_far.append(line.send(contexts[2][0], core_bit))
        line.wait(*ctx_far)
        scatters = {last: ff_grads(last)}
        for k in range(last - 1, -1, -1):
            ff_own(k)
            if k == last - 1:
                scatters[last].turn()
            ff_near(k)
        back_both = rows_back("ff_back", grads, 3, ups, bf16)
        back_both = [line.send(v, core_bit) for v in back_both]
        back_near = rows_back("ff_back", grads, 2, ups, f32)
        back_near = line.op(add_halves, back_near, *back_both)
        back_near = line.send(back_near, near_bit)
        held = {last: scatters[last].close()}
        for k in range(last - 1, -1, -1):
            scatters[k] = ff_grads(k)
        back_beside = rows_back("ff_back", grads, 1, ups, bf16)
        for k in range(last - 1, -1, -1):
            scatters[k].turn()
        back_beside = [line.send(v, core_bit) for v in back_beside]
        back_own = rows_back("ff_back", grads, 0, ups, f32)

        grad_hidden1, grad_attn, sums2 = line.kernel(
            "second_back",
            second_back_kernel,
            [shape((seq_len, width), f32), shape((seq_len, width)), shape((8, width), f32)],
            [],
            back_own,
            *back_beside,
            back_near,
            hidden1,
            cotangent,
            gain2,
        )
        far_got = line.send(held[last], far_bits[0]) if len(far_bits) == 1 else None
        keep, send, grad_send = line.kernel(
            "out_back",
            out_back_kernel,
            [shape((seq_len, half))] * 3,
            [place],
            grad_attn,
            out_mine,
            out_got,
        )
        context_got = line.send(send, core_bit)
        grad_got = line.send(grad_send, core_bit)
        fore_both = rows_back("ff_fore", acts, 3, downs, bf16)
        line.wait(context_got, grad_got)
        grad_low, qkv_scatters = [], []

        def attend_back(p):
            low, *parts = line.kernel(
                "attend_back",
                functools.partial(attend_back_kernel, p),
                [shape((2 * seq_len, chunk_cols))] + parts_shapes(chunk_cols),
                [place],
                qkv_low[p],
                logs[p],
                keep,
                context_got,
                normed1,
                cosine,
                sine,
                seg_col,
                seg_row,
                scratch=[pltpu.VMEM((seq_len, HEAD_DIM), f32)] * 3,
            )
            grad_low.append(low)
            return by_chip(parts)

        parts = attend_back(0)
        if len(far_bits) == 1:
            own_sum = scatters[0].close()
        else:
            for k in range(last - 1, -1, -1):
                held[k] = scatters[k].close()
        qkv_scatters.append(Scatter(line, parts))
        fore_both = [line.send(v, core_bit) for v in fore_both]
        fore_near = rows_back("ff_fore", acts, 2, downs, f32)
        fore_near = line.op(add_halves, fore_near, *fore_both)
        qkv_scatters[0].turn()
        fore_near = line.send(fore_near, near_bit)
        parts = attend_back(1)
        if len(far_bits) == 1:
            ff_share = line.op(add_low, own_sum, far_got)
        else:
            held = [held[k] for k in range(len(slices))]
            for bit in reversed(far_bits):
                middle = len(held) // 2
                held = [add_low(a, flip(c, bit)) for a, c in zip(held[:middle], held[middle:])]
            ff_share = held[0]
        qkv_scatters.append(Scatter(line, parts))
        out_parts = line.kernel(
            "out_weight",
            functools.partial(out_weight_kernel, chunks),
            parts_shapes(half),
            [place],
            context,
            grad_attn,
            grad_got,
            *[c[1] for c in contexts],
            *ctx_far,
            scratch=[pltpu.VMEM((seq_len, width), bf16)],
        )
        qkv_z = [OverMp(line, qkv_scatters[0].close())]
        qkv_scatters[1].turn()
        parts = attend_back(2)
        line.wait(fore_near)
        qkv_scatters.append(Scatter(line, parts))
        qkv_z[0].turn()
        qkv_z.append(OverMp(line, qkv_scatters[1].close()))
        qkv_scatters[2].turn()
        back_other = line.kernel(
            "qkv_back",
            functools.partial(rows_back_kernel, chunks, seq_len),
            [shape((seq_len // 2, width))] * 2,
            [],
            *grad_low,
            *qkv_wide,
        )
        qkv_z[0].back()
        qkv_z[1].turn()
        shares = [qkv_z[0].close()]
        out_scatter = Scatter(line, by_chip(out_parts))
        qkv_z.append(OverMp(line, qkv_scatters[2].close()))
        out_scatter.turn()
        qkv_z[1].back()
        back_mine = line.kernel(
            "qkv_back",
            functools.partial(rows_back_kernel, chunks, 0),
            [shape((seq_len, width), f32)],
            [],
            *grad_low,
            *qkv_wide,
        )[0]
        qkv_z[2].turn()
        shares.append(qkv_z[1].close())
        back_other_got = [line.send(v, core_bit) for v in back_other]
        out_z = OverMp(line, out_scatter.close())
        grad_input, sums1 = line.kernel(
            "first_back",
            first_back_kernel,
            [shape((seq_len, width), f32), shape((8, width), f32)],
            [],
            back_mine,
            *back_other_got,
            block_in,
            grad_hidden1,
            gain1,
        )
        qkv_z[2].back()
        out_z.turn()
        sums = SumAll(line, jnp.concatenate([sums1[:2], sums2[:2]]))
        fore_beside = rows_back("ff_fore", acts, 1, downs, bf16)
        shares.append(qkv_z[2].close())
        out_z.back()
        sums.turn()
        shares_got = [line.send(v, core_bit) for v in shares]
        fore_own = rows_back("ff_fore", acts, 0, downs, f32)
        line.wait(*shares_got)
        sums.turn()
        out_share = out_z.close()
        ff_share_got = line.send(ff_share, core_bit)
        out_share_got = line.send(out_share, core_bit)
        fore_beside = [line.send(v, core_bit) for v in fore_beside]
        grad_w_qkv = line.kernel(
            "place_qkv",
            functools.partial(place_attention_kernel, chunks),
            shape((rows, 3 * width), f32),
            [place],
            *shares,
            *shares_got,
        )
        sums.turn()
        grad_w_up, grad_w_down = line.kernel(
            "place_ff",
            place_halves_kernel,
            [shape((rows, units), f32)] * 2,
            [place],
            ff_share,
            ff_share_got,
        )
        grad_w_down = grad_w_down.T
        sums.turn()
        grad_w_out = line.kernel(
            "place_out",
            place_halves_kernel,
            [shape((rows, width), f32)],
            [place],
            out_share,
            out_share_got,
        )[0]
        sums = sums.close()

        def finish(base, own, near, low, high):
            middle = own.shape[0] // 2
            total_rows = base + own + near.astype(f32)
            return jnp.concatenate(
                [total_rows[:middle] + low.astype(f32), total_rows[middle:] + high.astype(f32)]
            ).astype(bf16)

        block_out = line.op(finish, hidden1, fore_own, fore_near, *fore_beside)
        return (
            block_out,
            grad_input,
            grad_w_qkv,
            grad_w_out,
            grad_w_up,
            grad_w_down,
            sums[0],
            sums[1],
            sums[2],
            sums[3],
        )

    return on_device


def solution(mesh):
    return jax.shard_map(
        build(mesh.shape["dp"], mesh.shape["mp"]),
        mesh=mesh,
        in_specs=(
            P(("dp", "mp"), None),
            P(("dp", "mp"), None),
            P(("dp", "mp"), None),
            P("dp"),
            P("dp", None),
            P("dp", None),
            P("dp", "mp"),
            P("mp", "dp"),
            P(),
            P(),
            P(),
            P(),
        ),
        out_specs=(
            P(("dp", "mp"), None),
            P(("dp", "mp"), None),
            P("dp", None),
            P("dp", None),
            P("dp", "mp"),
            P("mp", "dp"),
            P(),
            P(),
            P(),
            P(),
        ),
        check_vma=False,
    )
```

time: 768 us -> 657 us (0.86)
  Pallas kernels: 58 us -> 302 us
  matrix products: 163 us -> 0 us
  waiting for transfers between devices: 284 us -> 178 us
  other arithmetic: 98.6 us -> 37.4 us
  local copies, waits for them, and re-layouts: 75.4 us -> 38 us
  starting transfers between devices: 77.1 us -> 89.1 us
    pallas_call x6 -> x34, Pallas kernels: 58 us -> 302 us  [the longest x32 265 us: run(): pl.pallas_call(kernel, out_shape=outs, in_specs=[SMEM_SPEC] * len(scalars...]
    dot_general x31 -> x0, matrix products: 163 us -> none  [the longest x2 27.7 us: on_device(): lax.dot_general(grad_preact, up_k, contract_cols, preferred_element_type=...]
    ppermute x90 -> x104, waiting for transfers between devices: 284 us -> 178 us  [flip(): return lax.ppermute(value, AXES, [(i, i ^ bit) for i in range(total)])]
    concatenate x18 -> x11, other arithmetic: 27 us -> 8.6 us  [the longest x1 3.87 us: on_device(): tokens = jnp.concatenate([block_in, cotangent])]
    select_n x25 -> x4, other arithmetic: 17.1 us -> 0.17 us  [joined(): low = jnp.where(self.upper == 0, keep, got)]
    slice x20 -> x19, local copies, waits for them, and re-layouts: 24.8 us -> 11.2 us  [the longest x1 2.66 us: on_device(): cot_core = line.after(tokens_other)[seq_len:]]
    ppermute x90 -> x104, starting transfers between devices: 77.1 us -> 89.1 us  [flip(): return lax.ppermute(value, AXES, [(i, i ^ bit) for i in range(total)])]
    convert_element_type x2 -> x0, local copies, waits for them, and re-layouts: 11.1 us -> none  [on_device(): sides.transpose(0, 3, 1, 2, 4).reshape(rows, 3 * width).astype(f32)]
  transfers between devices with their start and end apart: 90 -> 104, of which waited for: 35 -> 35; matrix products, arithmetic and copies ran while one was open for 29% -> 8% of each run, Pallas kernels for 8% -> 41%
where the time goes in v2:
time: 657 us; the launch traced here: 647 us
  Pallas kernels  302 us (46%)
  waiting for transfers between devices  178 us (27%)
  starting transfers between devices  89.1 us (14%)
  local copies, waits for them, and re-layouts  38 us (6%)
  other arithmetic  37.4 us (6%)
    pallas_call x32, Pallas kernels, run(): pl.pallas_call(kernel, out_shape=outs, in_specs=[SMEM_SPEC] * len(scalars...  265 us
    ppermute x104, waiting for transfers between devices, flip(): return lax.ppermute(value, AXES, [(i, i ^ bit) for i in range(total)])  178 us
    ppermute x104, starting transfers between devices, flip(): return lax.ppermute(value, AXES, [(i, i ^ bit) for i in range(total)])  89.1 us
    pallas_call x2, Pallas kernels, ff_weight(): pl.pallas_call(functools.partial(ff_weight_kernel, count), out_shape=[sha...  37 us
    unnamed x185, local copies, waits for them, and re-layouts  16.4 us
  transfers between devices with their start and end apart: 104, of which 35 were waited for; matrix products, arithmetic and copies ran while one was open for 8% of the time, Pallas kernels for 41%

profile of v2, /device:TPU:0, one launch (start us, length us, event | category | flops | bytes accessed | tf_op | source)
XLA Modules:
  0.0 646.8 jit_solution(14481687569244159522)
XLA Ops:
  0.7 3.9 pad_maximum_fusion
  8.0 5.0 collective-permute-done.1.got_qkv
  13.1 3.4 cut_attention.1
  16.5 2.6 collective-permute-start.4
  23.6 6.3 norm.1.norm_ref
  29.9 3.6 cut_rest.1
  37.8 11.9 %collective-permute-done.7.refs_2_ = bf16[384,768]{1,0:T(8,128)(2,1)S(1)} collective-permute-done((bf16[384,768]{1,0:T(8,128)(2,1)S(1)}, bf16[384,768]{1,0:T(8,128)(2,1)S(1)}, u32[]{:S(2)}, u32[]{:S(2)}) %collective-permute-start.7) | collective-permute-done | bytes 589856 | tf_op jit(solution)/shard_map/ppermute | solution.py:537
  51.7 4.1 collective-permute-done.10.refs_4_
  64.3 2.6 collective-permute-start.6
  66.9 11.3 %attend.3 = (bf16[1536,768]{1,0:T(8,128)(2,1)}, bf16[1024,768]{1,0:T(8,128)(2,1)}, bf16[2,512,256]{2,1,0:T(8,128)(2,1)}, f32[1024,128]{1,0:T(8,128)}) custom-call(s32[5]{0:T(128)} %pad_add_fusion.4.place, bf16[1024,1536]{1,0:T(8,128)(2,1)} %norm.1.norm_ref, f32[512,128]{1,0:T(8,128)} %get-tuple-element.735.cos_ref, f32[512,128]{1,0:T(8,128)} %get-tuple-element.734.sin_ref, ...), custom_call_target="tpu_custom_call" | custom-call | flops 1000000 | tf_op jit(solution)/shard_map/attend/pallas_call | solution.py:75
  85.1 11.3 %attend.4 = (bf16[1536,768]{1,0:T(8,128)(2,1)}, bf16[1024,768]{1,0:T(8,128)(2,1)}, bf16[2,512,256]{2,1,0:T(8,128)(2,1)}, f32[1024,128]{1,0:T(8,128)}) custom-call(s32[5]{0:T(128)} %pad_add_fusion.4.place, bf16[1024,1536]{1,0:T(8,128)(2,1)} %norm.1.norm_ref, f32[512,128]{1,0:T(8,128)} %get-tuple-element.735.cos_ref, f32[512,128]{1,0:T(8,128)} %get-tuple-element.734.sin_ref, ...), custom_call_target="tpu_custom_call" | custom-call | flops 1000000 | tf_op jit(solution)/shard_map/attend/pallas_call | solution.py:75
  102.2 14.5 %collective-permute-done.6.refs_0_ = bf16[768,768]{1,0:T(8,128)(2,1)} collective-permute-done((bf16[768,768]{1,0:T(8,128)(2,1)S(1)}, bf16[768,768]{1,0:T(8,128)(2,1)}, u32[]{:S(2)}, u32[]{:S(2)}) %collective-permute-start.6) | collective-permute-done | bytes 1179680 | tf_op jit(solution)/shard_map/ppermute | solution.py:537
  122.5 11.2 %attend.5 = (bf16[1536,768]{1,0:T(8,128)(2,1)}, bf16[1024,768]{1,0:T(8,128)(2,1)}, bf16[2,512,256]{2,1,0:T(8,128)(2,1)}, f32[1024,128]{1,0:T(8,128)}) custom-call(s32[5]{0:T(128)} %pad_add_fusion.4.place, bf16[1024,1536]{1,0:T(8,128)(2,1)} %norm.1.norm_ref, f32[512,128]{1,0:T(8,128)} %get-tuple-element.735.cos_ref, f32[512,128]{1,0:T(8,128)} %get-tuple-element.734.sin_ref, ...), custom_call_target="tpu_custom_call" | custom-call | flops 1000000 | tf_op jit(solution)/shard_map/attend/pallas_call | solution.py:75
  133.8 19.2 %collective-permute-done.26.refs_4_ = bf16[192,768]{1,0:T(8,128)(2,1)S(1)} collective-permute-done((bf16[192,768]{1,0:T(8,128)(2,1)S(1)}, bf16[192,768]{1,0:T(8,128)(2,1)S(1)}, u32[]{:S(2)}, u32[]{:S(2)}) %collective-permute-start.26) | collective-permute-done | bytes 294944 | tf_op jit(solution)/shard_map/ppermute | solution.py:537
  159.1 4.8 join.1
  164.5 10.7 %out.1 = (f32[512,1536]{1,0:T(8,128)}, bf16[512,1536]{1,0:T(8,128)(2,1)}, bf16[512,1536]{1,0:T(8,128)(2,1)}) custom-call(s32[5]{0:T(128)} %pad_add_fusion.4.place, bf16[512,1536]{1,0:T(8,128)(2,1)} %x_ref.2, bf16[512,256]{1,0:T(8,128)(2,1)} %get-tuple-element.503.refs_0_, bf16[512,256]{1,0:T(8,128)(2,1)} %get-tuple-element.504.refs_1_, ...), custom_call_target="tpu_custom_call" | custom-call | flops 1000000 | tf_op jit(solution)/shard_map/out/pallas_call | solution.py:75
  176.4 16.6 %collective-permute-done.33.cot_a.refs_6_ = bf16[512,1536]{1,0:T(8,128)(2,1)S(1)} collective-permute-done((bf16[512,1536]{1,0:T(8,128)(2,1)S(1)}, bf16[512,1536]{1,0:T(8,128)(2,1)S(1)}, u32[]{:S(2)}, u32[]{:S(2)}) %collective-permute-start.33) | collective-permute-done | bytes 1572896 | tf_op jit(solution)/shard_map/ppermute | solution.py:537
  198.8 2.6 broadcast_subtract_fusion
  202.1 2.7 slice.378.cot_b.refs_5_
  204.7 12.7 %ff_own.2 = (bf16[512,768]{1,0:T(8,128)(2,1)}, bf16[512,768]{1,0:T(8,128)(2,1)}, bf16[512,768]{1,0:T(8,128)(2,1)}, bf16[512,768]{1,0:T(8,128)(2,1)}, bf16[1536,7...) custom-call(s32[5]{0:T(128)} %pad_add_fusion.4.place, s32[2]{0:T(128)} %get-tuple-element.744.limits, ...), custom_call_target="tpu_custom_call" | custom-call | flops 1000000 | tf_op jit(solution)/shard_map/ff_own/pallas_call | solution.py:75
  217.4 7.3 %collective-permute-done.34.refs_2_ = bf16[768,768]{1,0:T(8,128)(2,1)} collective-permute-done((bf16[768,768]{1,0:T(8,128)(2,1)}, bf16[768,768]{1,0:T(8,128)(2,1)}, u32[]{:S(2)}, u32[]{:S(2)}) %collective-permute-start.34) | collective-permute-done | bytes 1179680 | tf_op jit(solution)/shard_map/ppermute | solution.py:537
  227.6 4.2 collective-permute-done.29.norm_a.refs_2_
  232.4 3.8 collective-permute-done.37.norm_b.refs_3_
  237.4 11.6 %ff_near.2 = (bf16[512,768]{1,0:T(8,128)(2,1)}, bf16[512,768]{1,0:T(8,128)(2,1)}, bf16[512,768]{1,0:T(8,128)(2,1)}, bf16[512,768]{1,0:T(8,128)(2,1)}) custom-call(s32[5]{0:T(128)} %pad_add_fusion.4.place, s32[2]{0:T(128)} %get-tuple-element.745.limits, bf16[512,1536]{1,0:T(8,128)(2,1)} %collective-permute-done.29.norm_a.refs_2_, ...), custom_call_target="tpu_custom_call" | custom-call | flops 1000000 | tf_op jit(solution)/shard_map/ff_near/pallas_call | solution.py:75
  250.5 18.6 %ff_weight.2 = (bf16[768,768]{1,0:T(8,128)(2,1)}, bf16[768,768]{1,0:T(8,128)(2,1)}, bf16[768,768]{1,0:T(8,128)(2,1)}, bf16[384,768]{1,0:T(8,128)(2,1)}, bf16[384,768]{1,0:T(8,128)(2,1)}) custom-call(s32[4]{0:T(128)} %get-tuple-element.713.place, bf16[512,1536]{1,0:T(8,128)(2,1)} %get-tuple-element.539.norm_a.refs_0_, ...), custom_call_target="tpu_custom_call" | custom-call | flops 1000000 | tf_op jit(solution)/shard_map/ff_weight/pallas_call | solution.py:435
  273.5 12.5 %ff_own.3 = (bf16[512,768]{1,0:T(8,128)(2,1)}, bf16[512,768]{1,0:T(8,128)(2,1)}, bf16[512,768]{1,0:T(8,128)(2,1)}, bf16[512,768]{1,0:T(8,128)(2,1)}, bf16[1536,7...) custom-call(s32[5]{0:T(128)} %pad_add_fusion.4.place, s32[2]{0:T(128)} %get-tuple-element.743.limits, ...), custom_call_target="tpu_custom_call" | custom-call | flops 1000000 | tf_op jit(solution)/shard_map/ff_own/pallas_call | solution.py:75
  287.6 11.5 %ff_near.3 = (bf16[512,768]{1,0:T(8,128)(2,1)}, bf16[512,768]{1,0:T(8,128)(2,1)}, bf16[512,768]{1,0:T(8,128)(2,1)}, bf16[512,768]{1,0:T(8,128)(2,1)}) custom-call(s32[5]{0:T(128)} %pad_add_fusion.4.place, s32[2]{0:T(128)} %get-tuple-element.742.limits, bf16[512,1536]{1,0:T(8,128)(2,1)} %collective-permute-done.29.norm_a.refs_2_, ...), custom_call_target="tpu_custom_call" | custom-call | flops 1000000 | tf_op jit(solution)/shard_map/ff_near/pallas_call | solution.py:75
  299.1 6.4 ff_back.4
  307.3 7.4 %ff_back.5 = f32[512,1536]{1,0:T(8,128)} custom-call(bf16[512,768]{1,0:T(8,128)(2,1)} %get-tuple-element.531.refs_14_.refs_0_, bf16[512,768]{1,0:T(8,128)(2,1)} %get-tuple-element.532.refs_1_.refs_14_, bf16[1536,768]{1,0:T(8,128)(2,1)} %get-tuple-element.498.refs_0_.refs_2_, bf16[1536,768]{1,0:T(8,128)(2,1)} %get-tuple-element.525.refs_0_.refs_3_), custom_call_target="tpu_custom_call" | custom-call | flops 1000000 | tf_op jit(solution)/shard_map/ff_back/pallas_call | solution.py:75
  314.7 2.3 fusion.5
  317.2 16.7 %collective-permute-done.47 = bf16[768,768]{1,0:T(8,128)(2,1)S(1)} collective-permute-done((bf16[768,768]{1,0:T(8,128)(2,1)S(1)}, bf16[768,768]{1,0:T(8,128)(2,1)S(1)}, u32[]{:S(2)}, u32[]{:S(2)}) %collective-permute-start.47) | collective-permute-done | bytes 1179680 | tf_op jit(solution)/shard_map/ppermute | solution.py:537
  334.6 18.4 %ff_weight.3 = (bf16[768,768]{1,0:T(8,128)(2,1)}, bf16[768,768]{1,0:T(8,128)(2,1)}, bf16[768,768]{1,0:T(8,128)(2,1)}, bf16[384,768]{1,0:T(8,128)(2,1)}, bf16[384,768]{1,0:T(8,128)(2,1)}) custom-call(s32[4]{0:T(128)} %get-tuple-element.713.place, bf16[512,1536]{1,0:T(8,128)(2,1)} %get-tuple-element.539.norm_a.refs_0_, ...), custom_call_target="tpu_custom_call" | custom-call | flops 1000000 | tf_op jit(solution)/shard_map/ff_weight/pallas_call | solution.py:435
  357.1 6.4 ff_back.6
  363.4 4.0 collective-permute-done.50
  368.3 2.4 fusion.9
  373.9 7.8 %ff_back.7.own = f32[512,1536]{1,0:T(8,128)} custom-call(bf16[512,768]{1,0:T(8,128)(2,1)} %get-tuple-element.555.refs_12_.refs_0_, bf16[512,768]{1,0:T(8,128)(2,1)} %get-tuple-element.542.refs_12_.refs_1_, bf16[1536,768]{1,0:T(8,128)(2,1)} %get-tuple-element.498.refs_0_.refs_2_, bf16[1536,768]{1,0:T(8,128)(2,1)} %get-tuple-element.525.refs_0_.refs_3_), custom_call_target="tpu_custom_call" | custom-call | flops 1000000 | tf_op jit(solution)/shard_map/ff_back/pallas_call | solution.py:75
  381.7 8.3 %collective-permute-done.53.near = bf16[512,1536]{1,0:T(8,128)(2,1)S(1)} collective-permute-done((bf16[512,1536]{1,0:T(8,128)(2,1)S(1)}, bf16[512,1536]{1,0:T(8,128)(2,1)S(1)}, u32[]{:S(2)}, u32[]{:S(2)}) %collective-permute-start.53) | collective-permute-done | bytes 1572896 | tf_op jit(solution)/shard_map/ppermute | solution.py:537
  391.3 9.9 %second_back.1 = (f32[512,1536]{1,0:T(8,128)}, bf16[512,1536]{1,0:T(8,128)(2,1)}, f32[8,1536]{1,0:T(8,128)}) custom-call(f32[512,1536]{1,0:T(8,128)} %ff_back.7.own, bf16[256,1536]{1,0:T(8,128)(2,1)} %collective-permute-done.51.beside_a, bf16[256,1536]{1,0:T(8,128)(2,1)} %copy-done.40, bf16[512,1536]{1,0:T(8,128)(2,1)} %copy-done.18, ...), custom_call_target="tpu_custom_call" | custom-call | flops 1000000 | tf_op jit(solution)/shard_map/second_back/pallas_call | solution.py:75
  401.2 7.0 %out_back.1 = (bf16[512,768]{1,0:T(8,128)(2,1)}, bf16[512,768]{1,0:T(8,128)(2,1)}, bf16[512,768]{1,0:T(8,128)(2,1)}) custom-call(s32[5]{0:T(128)} %pad_add_fusion.4.place, bf16[512,1536]{1,0:T(8,128)(2,1)} %get-tuple-element.562.grad, bf16[1536,768]{1,0:T(8,128)(2,1)} %get-tuple-element.476.refs_6_.w_mine, bf16[1536,768]{1,0:T(8,128)(2,1)} %get-tuple-element.482.refs_7_.w_got), custom_call_target="tpu_custom_call" | custom-call | flops 1000000 | tf_op jit(solution)/shard_map/out_back/pallas_call | solution.py:75
  408.7 6.4 ff_fore.4
  416.1 12.6 %attend_back.3 = (bf16[1024,768]{1,0:T(8,128)(2,1)}, bf16[384,768]{1,0:T(8,128)(2,1)}, bf16[384,768]{1,0:T(8,128)(2,1)}, bf16[384,768]{1,0:T(8,128)(2,1)}, bf16[...) custom-call(s32[5]{0:T(128)} %pad_add_fusion.4.place, bf16[1024,768]{1,0:T(8,128)(2,1)} %get-tuple-element.570.qkv_ref, ...), custom_call_target="tpu_custom_call" | custom-call | flops 1000000 | tf_op jit(solution)/shard_map/attend_back/pallas_call | solution.py:75
  429.8 3.4 collective-permute-start.62
  435.0 7.5 %ff_fore.5 = f32[512,1536]{1,0:T(8,128)} custom-call(bf16[512,768]{1,0:T(8,128)(2,1)} %get-tuple-element.579.refs_10_.refs_0_, bf16[512,768]{1,0:T(8,128)(2,1)} %get-tuple-element.527.refs_10_.refs_1_, bf16[1536,768]{1,0:T(8,128)(2,1)} %get-tuple-element.499.refs_1_.refs_2_, bf16[1536,768]{1,0:T(8,128)(2,1)} %get-tuple-element.526.refs_1_.refs_3_), custom_call_target="tpu_custom_call" | custom-call | flops 1000000 | tf_op jit(solution)/shard_map/ff_fore/pallas_call | solution.py:75
  442.5 2.3 fusion.3
  453.6 12.5 %attend_back.4 = (bf16[1024,768]{1,0:T(8,128)(2,1)}, bf16[384,768]{1,0:T(8,128)(2,1)}, bf16[384,768]{1,0:T(8,128)(2,1)}, bf16[384,768]{1,0:T(8,128)(2,1)}, bf16[...) custom-call(s32[5]{0:T(128)} %pad_add_fusion.4.place, bf16[1024,768]{1,0:T(8,128)(2,1)} %get-tuple-element.589.qkv_ref, ...), custom_call_target="tpu_custom_call" | custom-call | flops 1000000 | tf_op jit(solution)/shard_map/attend_back/pallas_call | solution.py:75
  466.2 19.2 %collective-permute-done.62 = bf16[768,768]{1,0:T(8,128)(2,1)} collective-permute-done((bf16[768,768]{1,0:T(8,128)(2,1)S(1)}, bf16[768,768]{1,0:T(8,128)(2,1)}, u32[]{:S(2)}, u32[]{:S(2)}) %collective-permute-start.62) | collective-permute-done | bytes 1179680 | tf_op jit(solution)/shard_map/ppermute | solution.py:537
  488.8 6.2 out_weight.1
  502.4 12.8 %attend_back.5 = (bf16[1024,768]{1,0:T(8,128)(2,1)}, bf16[384,768]{1,0:T(8,128)(2,1)}, bf16[384,768]{1,0:T(8,128)(2,1)}, bf16[384,768]{1,0:T(8,128)(2,1)}, bf16[...) custom-call(s32[5]{0:T(128)} %pad_add_fusion.4.place, bf16[1024,768]{1,0:T(8,128)(2,1)} %get-tuple-element.612.qkv_ref, ...), custom_call_target="tpu_custom_call" | custom-call | flops 1000000 | tf_op jit(solution)/shard_map/attend_back/pallas_call | solution.py:75
  518.2 3.5 collective-permute-start.73
  523.6 9.2 %qkv_back.2 = (bf16[256,1536]{1,0:T(8,128)(2,1)}, bf16[256,1536]{1,0:T(8,128)(2,1)}) custom-call(bf16[1024,768]{1,0:T(8,128)(2,1)} %get-tuple-element.653.refs_0_, bf16[1024,768]{1,0:T(8,128)(2,1)} %get-tuple-element.594.refs_1_, bf16[1024,768]{1,0:T(8,128)(2,1)} %get-tuple-element.614.refs_2_, bf16[1536,768]{1,0:T(8,128)(2,1)} %get-tuple-element.449.refs_3_, ...), custom_call_target="tpu_custom_call" | custom-call | flops 1000000 | tf_op jit(solution)/shard_map/qkv_back/pallas_call | solution.py:75
  536.6 2.6 collective-permute-start.80
  539.2 6.8 %collective-permute-done.75 = bf16[192,768]{1,0:T(8,128)(2,1)S(1)} collective-permute-done((bf16[192,768]{1,0:T(8,128)(2,1)S(1)}, bf16[192,768]{1,0:T(8,128)(2,1)S(1)}, u32[]{:S(2)}, u32[]{:S(2)}) %collective-permute-start.75) | collective-permute-done | bytes 294944 | tf_op jit(solution)/shard_map/ppermute | solution.py:537
  550.6 4.4 collective-permute-done.79
  557.6 10.2 %qkv_back.3.own = f32[512,1536]{1,0:T(8,128)} custom-call(bf16[1024,768]{1,0:T(8,128)(2,1)} %get-tuple-element.653.refs_0_, bf16[1024,768]{1,0:T(8,128)(2,1)} %get-tuple-element.594.refs_1_, bf16[1024,768]{1,0:T(8,128)(2,1)} %get-tuple-element.614.refs_2_, bf16[1536,768]{1,0:T(8,128)(2,1)} %get-tuple-element.449.refs_3_, ...), custom_call_target="tpu_custom_call" | custom-call | flops 1000000 | tf_op jit(solution)/shard_map/qkv_back/pallas_call | solution.py:75
  571.6 2.9 collective-permute-start.87
  574.5 6.5 collective-permute-done.83
  585.9 8.6 %first_back.1 = (f32[512,1536]{1,0:T(8,128)}, f32[8,1536]{1,0:T(8,128)}) custom-call(f32[512,1536]{1,0:T(8,128)} %qkv_back.3.own, bf16[256,1536]{1,0:T(8,128)(2,1)} %copy-done.39, bf16[256,1536]{1,0:T(8,128)(2,1)} %copy-done.38, bf16[512,1536]{1,0:T(8,128)(2,1)} %x_ref.2, f32[512,1536]{1,0:T(8,128)} %get-tuple-element.561.grad_hidden, ...), custom_call_target="tpu_custom_call" | custom-call | flops 1000000 | tf_op jit(solution)/shard_map/first_back/pallas_call | solution.py:75
  597.7 6.4 ff_fore.6
  604.4 11.7 %collective-permute-done.90 = bf16[192,768]{1,0:T(8,128)(2,1)S(1)} collective-permute-done((bf16[192,768]{1,0:T(8,128)(2,1)S(1)}, bf16[192,768]{1,0:T(8,128)(2,1)S(1)}, u32[]{:S(2)}, u32[]{:S(2)}) %collective-permute-start.90) | collective-permute-done | bytes 294944 | tf_op jit(solution)/shard_map/ppermute | solution.py:537
  618.4 7.4 %ff_fore.7 = f32[512,1536]{1,0:T(8,128)} custom-call(bf16[512,768]{1,0:T(8,128)(2,1)} %get-tuple-element.681.refs_8_.refs_0_, bf16[512,768]{1,0:T(8,128)(2,1)} %get-tuple-element.517.refs_8_.refs_1_, bf16[1536,768]{1,0:T(8,128)(2,1)} %get-tuple-element.499.refs_1_.refs_2_, bf16[1536,768]{1,0:T(8,128)(2,1)} %get-tuple-element.526.refs_1_.refs_3_), custom_call_target="tpu_custom_call" | custom-call | flops 1000000 | tf_op jit(solution)/shard_map/ff_fore/pallas_call | solution.py:75
  627.5 4.1 place_qkv.1
  632.3 3.3 place_ff.1
  638.2 2.3 place_out.1
  641.2 2.2 convert_add_fusion
  (463 shorter events, 142.1 us)
Async XLA Ops:
  4.6 17.4 %collective-permute-start.2 = (bf16[1024,1536]{1,0:T(8,128)(2,1)}, bf16[1024,1536]{1,0:T(8,128)(2,1)S(1)}, u32[]{:S(2)}, u32[]{:S(2)}) collective-permute-start(bf16[1024,1536]{1,0:T(8,128)(2,1)} %pad_maximum_fusion), channel_id=1, source_target_pairs={{0,4},{1,5},{2,6},{3,7},{4,0},{5,1},{6,2},{7,3},{8,12},{9,13},{10,... | collective-permute-start | bytes 9437192 | tf_op jit(solution)/shard_map/ppermute | solution.py:537
  6.4 23.5 %collective-permute-start.3 = (bf16[576,1536]{1,0:T(8,128)(2,1)}, bf16[576,1536]{1,0:T(8,128)(2,1)}, u32[]{:S(2)}, u32[]{:S(2)}) collective-permute-start(bf16[576,1536]{1,0:T(8,128)(2,1)} %pad_maximum_fusion.1), channel_id=1, source_target_pairs={{0,4},{1,5},{2,6},{3,7},{4,0},{5,1},{6,2},{7,3},{8,12},{9,13},{10,... | collective-permute-start | bytes 5308424 | tf_op jit(solution)/shard_map/ppermute | solution.py:537
  16.5 17.7 %collective-permute-start.4 = (bf16[384,768]{1,0:T(8,128)(2,1)}, bf16[384,768]{1,0:T(8,128)(2,1)S(1)}, u32[]{:S(2)}, u32[]{:S(2)}) collective-permute-start(bf16[384,768]{1,0:T(8,128)(2,1)} %get-tuple-element.434.refs_0_), channel_id=1, source_target_pairs={{0,16},{1,17},{2,18},{3,19},{4,20},{5,21},{6,22},{7,23},{8,24},{9,... | collective-permute-start | bytes 1769480 | tf_op jit(solution)/shard_map/ppermute | solution.py:537
  19.1 15.5 %collective-permute-start.5 = (bf16[384,768]{1,0:T(8,128)(2,1)}, bf16[384,768]{1,0:T(8,128)(2,1)S(1)}, u32[]{:S(2)}, u32[]{:S(2)}) collective-permute-start(bf16[384,768]{1,0:T(8,128)(2,1)} %get-tuple-element.434.refs_0_), channel_id=1, source_target_pairs={{0,8},{1,9},{2,10},{3,11},{4,12},{5,13},{6,14},{7,15},{8,0},{9,1},... | collective-permute-start | bytes 1769480 | tf_op jit(solution)/shard_map/ppermute | solution.py:537
  33.5 16.1 %collective-permute-start.7 = (bf16[384,768]{1,0:T(8,128)(2,1)S(1)}, bf16[384,768]{1,0:T(8,128)(2,1)S(1)}, u32[]{:S(2)}, u32[]{:S(2)}) collective-permute-start(bf16[384,768]{1,0:T(8,128)(2,1)S(1)} %copy-done.43), channel_id=1, source_target_pairs={{0,16},{1,17},{2,18},{3,19},{4,20},{5,21},{6,22},{7,23},{8,24},{9,... | collective-permute-start | bytes 1769480 | tf_op jit(solution)/shard_map/ppermute | solution.py:537
  34.1 16.2 %collective-permute-start.8 = (bf16[384,768]{1,0:T(8,128)(2,1)S(1)}, bf16[384,768]{1,0:T(8,128)(2,1)S(1)}, u32[]{:S(2)}, u32[]{:S(2)}) collective-permute-start(bf16[384,768]{1,0:T(8,128)(2,1)S(1)} %copy-done.43), channel_id=1, source_target_pairs={{0,8},{1,9},{2,10},{3,11},{4,12},{5,13},{6,14},{7,15},{8,0},{9,1},... | collective-permute-start | bytes 1769480 | tf_op jit(solution)/shard_map/ppermute | solution.py:537
  34.7 21.1 %collective-permute-start.10 = (bf16[192,768]{1,0:T(8,128)(2,1)S(1)}, bf16[192,768]{1,0:T(8,128)(2,1)S(1)}, u32[]{:S(2)}, u32[]{:S(2)}) collective-permute-start(bf16[192,768]{1,0:T(8,128)(2,1)S(1)} %slice.359), channel_id=1, source_target_pairs={{0,8},{1,9},{2,10},{3,11},{4,12},{5,13},{6,14},{7,15},{8,0},{9,1},... | collective-permute-start | bytes 884744 | tf_op jit(solution)/shard_map/ppermute | solution.py:537
  36.3 19.6 %collective-permute-start.9 = (bf16[192,768]{1,0:T(8,128)(2,1)S(1)}, bf16[192,768]{1,0:T(8,128)(2,1)S(1)}, u32[]{:S(2)}, u32[]{:S(2)}) collective-permute-start(bf16[192,768]{1,0:T(8,128)(2,1)S(1)} %slice.358), channel_id=1, source_target_pairs={{0,16},{1,17},{2,18},{3,19},{4,20},{5,21},{6,22},{7,23},{8,24},{9,... | collective-permute-start | bytes 884744 | tf_op jit(solution)/shard_map/ppermute | solution.py:537
  56.6 22.5 %collective-permute-start.11 = (bf16[384,768]{1,0:T(8,128)(2,1)}, bf16[384,768]{1,0:T(8,128)(2,1)S(1)}, u32[]{:S(2)}, u32[]{:S(2)}) collective-permute-start(bf16[384,768]{1,0:T(8,128)(2,1)} %get-tuple-element.446.refs_0_), channel_id=1, source_target_pairs={{0,16},{1,17},{2,18},{3,19},{4,20},{5,21},{6,22},{7,23},{8,24},{9,... | collective-permute-start | bytes 1769480 | tf_op jit(solution)/shard_map/ppermute | solution.py:537
  58.2 21.0 %collective-permute-start.12 = (bf16[384,768]{1,0:T(8,128)(2,1)}, bf16[384,768]{1,0:T(8,128)(2,1)S(1)}, u32[]{:S(2)}, u32[]{:S(2)}) collective-permute-start(bf16[384,768]{1,0:T(8,128)(2,1)} %get-tuple-element.446.refs_0_), channel_id=1, source_target_pairs={{0,8},{1,9},{2,10},{3,11},{4,12},{5,13},{6,14},{7,15},{8,0},{9,1},... | collective-permute-start | bytes 1769480 | tf_op jit(solution)/shard_map/ppermute | solution.py:537
  58.7 20.5 %collective-permute-start.14 = (bf16[192,768]{1,0:T(8,128)(2,1)}, bf16[192,768]{1,0:T(8,128)(2,1)}, u32[]{:S(2)}, u32[]{:S(2)}) collective-permute-start(bf16[192,768]{1,0:T(8,128)(2,1)} %slice.361), channel_id=1, source_target_pairs={{0,8},{1,9},{2,10},{3,11},{4,12},{5,13},{6,14},{7,15},{8,0},{9,1},... | collective-permute-start | bytes 884744 | tf_op jit(solution)/shard_map/ppermute | solution.py:537
  60.2 19.0 %collective-permute-start.13 = (bf16[192,768]{1,0:T(8,128)(2,1)}, bf16[192,768]{1,0:T(8,128)(2,1)}, u32[]{:S(2)}, u32[]{:S(2)}) collective-permute-start(bf16[192,768]{1,0:T(8,128)(2,1)} %slice.360), channel_id=1, source_target_pairs={{0,16},{1,17},{2,18},{3,19},{4,20},{5,21},{6,22},{7,23},{8,24},{9,... | collective-permute-start | bytes 884744 | tf_op jit(solution)/shard_map/ppermute | solution.py:537
  64.3 52.4 %collective-permute-start.6 = (bf16[768,768]{1,0:T(8,128)(2,1)S(1)}, bf16[768,768]{1,0:T(8,128)(2,1)}, u32[]{:S(2)}, u32[]{:S(2)}) collective-permute-start(bf16[768,768]{1,0:T(8,128)(2,1)S(1)} %copy-done.29), channel_id=1, source_target_pairs={{0,2},{1,3},{2,0},{3,1},{4,6},{5,7},{6,4},{7,5},{8,10},{9,11},{10,... | collective-permute-start | bytes 3538952 | tf_op jit(solution)/shard_map/ppermute | solution.py:537
  79.3 20.7 %collective-permute-start.15 = (bf16[384,768]{1,0:T(8,128)(2,1)S(1)}, bf16[384,768]{1,0:T(8,128)(2,1)S(1)}, u32[]{:S(2)}, u32[]{:S(2)}) collective-permute-start(bf16[384,768]{1,0:T(8,128)(2,1)S(1)} %copy-done.42), channel_id=1, source_target_pairs={{0,16},{1,17},{2,18},{3,19},{4,20},{5,21},{6,22},{7,23},{8,24},{9,... | collective-permute-start | bytes 1769480 | tf_op jit(solution)/shard_map/ppermute | solution.py:537
  79.9 20.1 %collective-permute-start.16 = (bf16[384,768]{1,0:T(8,128)(2,1)S(1)}, bf16[384,768]{1,0:T(8,128)(2,1)S(1)}, u32[]{:S(2)}, u32[]{:S(2)}) collective-permute-start(bf16[384,768]{1,0:T(8,128)(2,1)S(1)} %copy-done.42), channel_id=1, source_target_pairs={{0,8},{1,9},{2,10},{3,11},{4,12},{5,13},{6,14},{7,15},{8,0},{9,1},... | collective-permute-start | bytes 1769480 | tf_op jit(solution)/shard_map/ppermute | solution.py:537
  80.5 18.8 %collective-permute-start.18 = (bf16[192,768]{1,0:T(8,128)(2,1)S(1)}, bf16[192,768]{1,0:T(8,128)(2,1)S(1)}, u32[]{:S(2)}, u32[]{:S(2)}) collective-permute-start(bf16[192,768]{1,0:T(8,128)(2,1)S(1)} %slice.364), channel_id=1, source_target_pairs={{0,8},{1,9},{2,10},{3,11},{4,12},{5,13},{6,14},{7,15},{8,0},{9,1},... | collective-permute-start | bytes 884744 | tf_op jit(solution)/shard_map/ppermute | solution.py:537
  81.9 17.5 %collective-permute-start.17 = (bf16[192,768]{1,0:T(8,128)(2,1)S(1)}, bf16[192,768]{1,0:T(8,128)(2,1)S(1)}, u32[]{:S(2)}, u32[]{:S(2)}) collective-permute-start(bf16[192,768]{1,0:T(8,128)(2,1)S(1)} %slice.363), channel_id=1, source_target_pairs={{0,16},{1,17},{2,18},{3,19},{4,20},{5,21},{6,22},{7,23},{8,24},{9,... | collective-permute-start | bytes 884744 | tf_op jit(solution)/shard_map/ppermute | solution.py:537
  101.7 15.1 %collective-permute-start.22 = (bf16[384,768]{1,0:T(8,128)(2,1)S(1)}, bf16[384,768]{1,0:T(8,128)(2,1)S(1)}, u32[]{:S(2)}, u32[]{:S(2)}) collective-permute-start(bf16[384,768]{1,0:T(8,128)(2,1)S(1)} %collective-permute-done.15.refs_2_), channel_id=1, source_target_pairs={{0,4},{1,5},{2,6},{3,7},{4,0},{5,1},{6,2},{7,3},{8,12},{9,13},{10,... | collective-permute-start | bytes 1769480 | tf_op jit(solution)/shard_map/ppermute | solution.py:537
  101.8 14.9 %collective-permute-start.21 = (bf16[384,768]{1,0:T(8,128)(2,1)S(1)}, bf16[384,768]{1,0:T(8,128)(2,1)S(1)}, u32[]{:S(2)}, u32[]{:S(2)}) collective-permute-start(bf16[384,768]{1,0:T(8,128)(2,1)S(1)} %collective-permute-done.16.refs_1_), channel_id=1, source_target_pairs={{0,4},{1,5},{2,6},{3,7},{4,0},{5,1},{6,2},{7,3},{8,12},{9,13},{10,... | collective-permute-start | bytes 1769480 | tf_op jit(solution)/shard_map/ppermute | solution.py:537
  118.4 45.4 %collective-permute-start.23 = (bf16[768,768]{1,0:T(8,128)(2,1)}, bf16[768,768]{1,0:T(8,128)(2,1)S(1)}, u32[]{:S(2)}, u32[]{:S(2)}) collective-permute-start(bf16[768,768]{1,0:T(8,128)(2,1)} %collective-permute-done.6.refs_0_), channel_id=1, source_target_pairs={{0,16},{1,17},{2,18},{3,19},{4,20},{5,21},{6,22},{7,23},{8,24},{9,... | collective-permute-start | bytes 3538952 | tf_op jit(solution)/shard_map/ppermute | solution.py:537
  119.9 43.9 %collective-permute-start.24 = (bf16[768,768]{1,0:T(8,128)(2,1)}, bf16[768,768]{1,0:T(8,128)(2,1)S(1)}, u32[]{:S(2)}, u32[]{:S(2)}) collective-permute-start(bf16[768,768]{1,0:T(8,128)(2,1)} %collective-permute-done.6.refs_0_), channel_id=1, source_target_pairs={{0,8},{1,9},{2,10},{3,11},{4,12},{5,13},{6,14},{7,15},{8,0},{9,1},... | collective-permute-start | bytes 3538952 | tf_op jit(solution)/shard_map/ppermute | solution.py:537
  120.5 32.5 %collective-permute-start.26 = (bf16[192,768]{1,0:T(8,128)(2,1)S(1)}, bf16[192,768]{1,0:T(8,128)(2,1)S(1)}, u32[]{:S(2)}, u32[]{:S(2)}) collective-permute-start(bf16[192,768]{1,0:T(8,128)(2,1)S(1)} %slice.366), channel_id=1, source_target_pairs={{0,8},{1,9},{2,10},{3,11},{4,12},{5,13},{6,14},{7,15},{8,0},{9,1},... | collective-permute-start | bytes 884744 | tf_op jit(solution)/shard_map/ppermute | solution.py:537
  122.0 31.0 %collective-permute-start.25 = (bf16[192,768]{1,0:T(8,128)(2,1)S(1)}, bf16[192,768]{1,0:T(8,128)(2,1)S(1)}, u32[]{:S(2)}, u32[]{:S(2)}) collective-permute-start(bf16[192,768]{1,0:T(8,128)(2,1)S(1)} %slice.365), channel_id=1, source_target_pairs={{0,16},{1,17},{2,18},{3,19},{4,20},{5,21},{6,22},{7,23},{8,24},{9,... | collective-permute-start | bytes 884744 | tf_op jit(solution)/shard_map/ppermute | solution.py:537
  156.6 36.4 %collective-permute-start.33 = (bf16[512,1536]{1,0:T(8,128)(2,1)S(1)}, bf16[512,1536]{1,0:T(8,128)(2,1)S(1)}, u32[]{:S(2)}, u32[]{:S(2)}) collective-permute-start(bf16[512,1536]{1,0:T(8,128)(2,1)S(1)} %copy-done), channel_id=1, source_target_pairs={{0,1},{1,0},{2,3},{3,2},{4,5},{5,4},{6,7},{7,6},{8,9},{9,8},{10,11... | collective-permute-start | bytes 4718600 | tf_op jit(solution)/shard_map/ppermute | solution.py:537
  175.2 18.6 %collective-permute-start.32 = (bf16[512,1536]{1,0:T(8,128)(2,1)}, bf16[512,1536]{1,0:T(8,128)(2,1)}, u32[]{:S(2)}, u32[]{:S(2)}) collective-permute-start(bf16[512,1536]{1,0:T(8,128)(2,1)} %get-tuple-element.539.norm_a.refs_0_), channel_id=1, source_target_pairs={{0,4},{1,5},{2,6},{3,7},{4,0},{5,1},{6,2},{7,3},{8,12},{9,13},{10,... | collective-permute-start | bytes 4718600 | tf_op jit(solution)/shard_map/ppermute | solution.py:537
  175.3 17.7 %collective-permute-start.31 = (bf16[384,768]{1,0:T(8,128)(2,1)S(1)}, bf16[384,768]{1,0:T(8,128)(2,1)S(1)}, u32[]{:S(2)}, u32[]{:S(2)}) collective-permute-start(bf16[384,768]{1,0:T(8,128)(2,1)S(1)} %slice.371), channel_id=1, source_target_pairs={{0,8},{1,9},{2,10},{3,11},{4,12},{5,13},{6,14},{7,15},{8,0},{9,1},... | collective-permute-start | bytes 1769480 | tf_op jit(solution)/shard_map/ppermute | solution.py:537
  175.9 17.1 %collective-permute-start.30 = (bf16[384,768]{1,0:T(8,128)(2,1)S(1)}, bf16[384,768]{1,0:T(8,128)(2,1)S(1)}, u32[]{:S(2)}, u32[]{:S(2)}) collective-permute-start(bf16[384,768]{1,0:T(8,128)(2,1)S(1)} %slice.370), channel_id=1, source_target_pairs={{0,16},{1,17},{2,18},{3,19},{4,20},{5,21},{6,22},{7,23},{8,24},{9,... | collective-permute-start | bytes 1769480 | tf_op jit(solution)/shard_map/ppermute | solution.py:537
  194.7 30.3 %collective-permute-start.36 = (bf16[512,1536]{1,0:T(8,128)(2,1)S(1)}, bf16[512,1536]{1,0:T(8,128)(2,1)S(1)}, u32[]{:S(2)}, u32[]{:S(2)}) collective-permute-start(bf16[512,1536]{1,0:T(8,128)(2,1)S(1)} %collective-permute-done.33.cot_a.refs_6_), channel_id=1, source_target_pairs={{0,4},{1,5},{2,6},{3,7},{4,0},{5,1},{6,2},{7,3},{8,12},{9,13},{10,... | collective-permute-start | bytes 4718600 | tf_op jit(solution)/shard_map/ppermute | solution.py:537
  194.7 37.1 %collective-permute-start.29 = (bf16[512,1536]{1,0:T(8,128)(2,1)}, bf16[512,1536]{1,0:T(8,128)(2,1)}, u32[]{:S(2)}, u32[]{:S(2)}) collective-permute-start(bf16[512,1536]{1,0:T(8,128)(2,1)} %get-tuple-element.539.norm_a.refs_0_), channel_id=1, source_target_pairs={{0,1},{1,0},{2,3},{3,2},{4,5},{5,4},{6,7},{7,6},{8,9},{9,8},{10,11... | collective-permute-start | bytes 4718600 | tf_op jit(solution)/shard_map/ppermute | solution.py:537
  196.3 28.4 %collective-permute-start.34 = (bf16[768,768]{1,0:T(8,128)(2,1)}, bf16[768,768]{1,0:T(8,128)(2,1)}, u32[]{:S(2)}, u32[]{:S(2)}) collective-permute-start(bf16[768,768]{1,0:T(8,128)(2,1)} %get-tuple-element.490.refs_0_), channel_id=1, source_target_pairs={{0,16},{1,17},{2,18},{3,19},{4,20},{5,21},{6,22},{7,23},{8,24},{9,... | collective-permute-start | bytes 3538952 | tf_op jit(solution)/shard_map/ppermute | solution.py:537
  196.8 28.1 %collective-permute-start.35 = (bf16[768,768]{1,0:T(8,128)(2,1)}, bf16[768,768]{1,0:T(8,128)(2,1)}, u32[]{:S(2)}, u32[]{:S(2)}) collective-permute-start(bf16[768,768]{1,0:T(8,128)(2,1)} %get-tuple-element.490.refs_0_), channel_id=1, source_target_pairs={{0,8},{1,9},{2,10},{3,11},{4,12},{5,13},{6,14},{7,15},{8,0},{9,1},... | collective-permute-start | bytes 3538952 | tf_op jit(solution)/shard_map/ppermute | solution.py:537
  231.8 18.6 %collective-permute-start.39 = (bf16[512,256]{1,0:T(8,128)(2,1)S(1)}, bf16[512,256]{1,0:T(8,128)(2,1)S(1)}, u32[]{:S(2)}, u32[]{:S(2)}) collective-permute-start(bf16[512,256]{1,0:T(8,128)(2,1)S(1)} %copy-done.36), channel_id=1, source_target_pairs={{0,4},{1,5},{2,6},{3,7},{4,0},{5,1},{6,2},{7,3},{8,12},{9,13},{10,... | collective-permute-start | bytes 786440 | tf_op jit(solution)/shard_map/ppermute | solution.py:537
  232.3 18.1 %collective-permute-start.38 = (bf16[512,256]{1,0:T(8,128)(2,1)S(1)}, bf16[512,256]{1,0:T(8,128)(2,1)S(1)}, u32[]{:S(2)}, u32[]{:S(2)}) collective-permute-start(bf16[512,256]{1,0:T(8,128)(2,1)S(1)} %copy-done.35), channel_id=1, source_target_pairs={{0,4},{1,5},{2,6},{3,7},{4,0},{5,1},{6,2},{7,3},{8,12},{9,13},{10,... | collective-permute-start | bytes 786440 | tf_op jit(solution)/shard_map/ppermute | solution.py:537
  249.1 23.4 %collective-permute-start.42 = (bf16[384,768]{1,0:T(8,128)(2,1)S(1)}, bf16[384,768]{1,0:T(8,128)(2,1)S(1)}, u32[]{:S(2)}, u32[]{:S(2)}) collective-permute-start(bf16[384,768]{1,0:T(8,128)(2,1)S(1)} %slice.380), channel_id=1, source_target_pairs={{0,8},{1,9},{2,10},{3,11},{4,12},{5,13},{6,14},{7,15},{8,0},{9,1},... | collective-permute-start | bytes 1769480 | tf_op jit(solution)/shard_map/ppermute | solution.py:537
  249.6 22.8 %collective-permute-start.41 = (bf16[384,768]{1,0:T(8,128)(2,1)S(1)}, bf16[384,768]{1,0:T(8,128)(2,1)S(1)}, u32[]{:S(2)}, u32[]{:S(2)}) collective-permute-start(bf16[384,768]{1,0:T(8,128)(2,1)S(1)} %slice.379), channel_id=1, source_target_pairs={{0,16},{1,17},{2,18},{3,19},{4,20},{5,21},{6,22},{7,23},{8,24},{9,... | collective-permute-start | bytes 1769480 | tf_op jit(solution)/shard_map/ppermute | solution.py:537
  269.1 17.0 %collective-permute-start.44 = (bf16[384,768]{1,0:T(8,128)(2,1)}, bf16[384,768]{1,0:T(8,128)(2,1)S(1)}, u32[]{:S(2)}, u32[]{:S(2)}) collective-permute-start(bf16[384,768]{1,0:T(8,128)(2,1)} %get-tuple-element.521), channel_id=1, source_target_pairs={{0,16},{1,17},{2,18},{3,19},{4,20},{5,21},{6,22},{7,23},{8,24},{9,... | collective-permute-start | bytes 1769480 | tf_op jit(solution)/shard_map/ppermute | solution.py:537
  270.3 15.7 %collective-permute-start.43 = (bf16[384,768]{1,0:T(8,128)(2,1)}, bf16[384,768]{1,0:T(8,128)(2,1)S(1)}, u32[]{:S(2)}, u32[]{:S(2)}) collective-permute-start(bf16[384,768]{1,0:T(8,128)(2,1)} %get-tuple-element.519), channel_id=1, source_target_pairs={{0,8},{1,9},{2,10},{3,11},{4,12},{5,13},{6,14},{7,15},{8,0},{9,1},... | collective-permute-start | bytes 1769480 | tf_op jit(solution)/shard_map/ppermute | solution.py:537
  306.0 27.9 %collective-permute-start.47 = (bf16[768,768]{1,0:T(8,128)(2,1)S(1)}, bf16[768,768]{1,0:T(8,128)(2,1)S(1)}, u32[]{:S(2)}, u32[]{:S(2)}) collective-permute-start(bf16[768,768]{1,0:T(8,128)(2,1)S(1)} %fusion.7), channel_id=1, source_target_pairs={{0,8},{1,9},{2,10},{3,11},{4,12},{5,13},{6,14},{7,15},{8,0},{9,1},... | collective-permute-start | bytes 3538952 | tf_op jit(solution)/shard_map/ppermute | solution.py:537
  306.5 27.6 %collective-permute-start.48 = (bf16[768,768]{1,0:T(8,128)(2,1)S(1)}, bf16[768,768]{1,0:T(8,128)(2,1)S(1)}, u32[]{:S(2)}, u32[]{:S(2)}) collective-permute-start(bf16[768,768]{1,0:T(8,128)(2,1)S(1)} %fusion.6), channel_id=1, source_target_pairs={{0,16},{1,17},{2,18},{3,19},{4,20},{5,21},{6,22},{7,23},{8,24},{9,... | collective-permute-start | bytes 3538952 | tf_op jit(solution)/shard_map/ppermute | solution.py:537
  353.0 14.4 %collective-permute-start.50 = (bf16[384,768]{1,0:T(8,128)(2,1)}, bf16[384,768]{1,0:T(8,128)(2,1)S(1)}, u32[]{:S(2)}, u32[]{:S(2)}) collective-permute-start(bf16[384,768]{1,0:T(8,128)(2,1)} %get-tuple-element.552), channel_id=1, source_target_pairs={{0,16},{1,17},{2,18},{3,19},{4,20},{5,21},{6,22},{7,23},{8,24},{9,... | collective-permute-start | bytes 1769480 | tf_op jit(solution)/shard_map/ppermute | solution.py:537
  353.9 14.1 %collective-permute-start.49 = (bf16[384,768]{1,0:T(8,128)(2,1)}, bf16[384,768]{1,0:T(8,128)(2,1)S(1)}, u32[]{:S(2)}, u32[]{:S(2)}) collective-permute-start(bf16[384,768]{1,0:T(8,128)(2,1)} %get-tuple-element.550), channel_id=1, source_target_pairs={{0,8},{1,9},{2,10},{3,11},{4,12},{5,13},{6,14},{7,15},{8,0},{9,1},... | collective-permute-start | bytes 1769480 | tf_op jit(solution)/shard_map/ppermute | solution.py:537
  355.4 34.6 %collective-permute-start.53 = (bf16[512,1536]{1,0:T(8,128)(2,1)S(1)}, bf16[512,1536]{1,0:T(8,128)(2,1)S(1)}, u32[]{:S(2)}, u32[]{:S(2)}) collective-permute-start(bf16[512,1536]{1,0:T(8,128)(2,1)S(1)} %pad_maximum_fusion.2), channel_id=1, source_target_pairs={{0,1},{1,0},{2,3},{3,2},{4,5},{5,4},{6,7},{7,6},{8,9},{9,8},{10,11... | collective-permute-start | bytes 4718600 | tf_op jit(solution)/shard_map/ppermute | solution.py:537
  370.7 19.3 %collective-permute-start.52 = (bf16[256,1536]{1,0:T(8,128)(2,1)}, bf16[256,1536]{1,0:T(8,128)(2,1)S(1)}, u32[]{:S(2)}, u32[]{:S(2)}) collective-permute-start(bf16[256,1536]{1,0:T(8,128)(2,1)} %get-tuple-element.558), channel_id=1, source_target_pairs={{0,4},{1,5},{2,6},{3,7},{4,0},{5,1},{6,2},{7,3},{8,12},{9,13},{10,... | collective-permute-start | bytes 2359304 | tf_op jit(solution)/shard_map/ppermute | solution.py:537
  370.7 19.3 %collective-permute-start.51 = (bf16[256,1536]{1,0:T(8,128)(2,1)}, bf16[256,1536]{1,0:T(8,128)(2,1)}, u32[]{:S(2)}, u32[]{:S(2)}) collective-permute-start(bf16[256,1536]{1,0:T(8,128)(2,1)} %get-tuple-element.556), channel_id=1, source_target_pairs={{0,4},{1,5},{2,6},{3,7},{4,0},{5,1},{6,2},{7,3},{8,12},{9,13},{10,... | collective-permute-start | bytes 2359304 | tf_op jit(solution)/shard_map/ppermute | solution.py:537
  371.2 57.4 %collective-permute-start.56 = (bf16[768,768]{1,0:T(8,128)(2,1)}, bf16[768,768]{1,0:T(8,128)(2,1)S(1)}, u32[]{:S(2)}, u32[]{:S(2)}) collective-permute-start(bf16[768,768]{1,0:T(8,128)(2,1)} %fusion.9), channel_id=1, source_target_pairs={{0,8},{1,9},{2,10},{3,11},{4,12},{5,13},{6,14},{7,15},{8,0},{9,1},... | collective-permute-start | bytes 3538952 | tf_op jit(solution)/shard_map/ppermute | solution.py:537
  372.7 56.0 %collective-permute-start.57 = (bf16[768,768]{1,0:T(8,128)(2,1)}, bf16[768,768]{1,0:T(8,128)(2,1)S(1)}, u32[]{:S(2)}, u32[]{:S(2)}) collective-permute-start(bf16[768,768]{1,0:T(8,128)(2,1)} %copy-done.66), channel_id=1, source_target_pairs={{0,16},{1,17},{2,18},{3,19},{4,20},{5,21},{6,22},{7,23},{8,24},{9,... | collective-permute-start | bytes 3538952 | tf_op jit(solution)/shard_map/ppermute | solution.py:537
  429.1 13.4 %collective-permute-start.59 = (bf16[256,1536]{1,0:T(8,128)(2,1)}, bf16[256,1536]{1,0:T(8,128)(2,1)S(1)}, u32[]{:S(2)}, u32[]{:S(2)}) collective-permute-start(bf16[256,1536]{1,0:T(8,128)(2,1)} %get-tuple-element.582), channel_id=1, source_target_pairs={{0,4},{1,5},{2,6},{3,7},{4,0},{5,1},{6,2},{7,3},{8,12},{9,13},{10,... | collective-permute-start | bytes 2359304 | tf_op jit(solution)/shard_map/ppermute | solution.py:537
  429.8 55.5 %collective-permute-start.62 = (bf16[768,768]{1,0:T(8,128)(2,1)S(1)}, bf16[768,768]{1,0:T(8,128)(2,1)}, u32[]{:S(2)}, u32[]{:S(2)}) collective-permute-start(bf16[768,768]{1,0:T(8,128)(2,1)S(1)} %add_convert_fusion.2), channel_id=1, source_target_pairs={{0,2},{1,3},{2,0},{3,1},{4,6},{5,7},{6,4},{7,5},{8,10},{9,11},{10,... | collective-permute-start | bytes 3538952 | tf_op jit(solution)/shard_map/ppermute | solution.py:537
  449.6 45.3 %collective-permute-start.63 = (bf16[384,768]{1,0:T(8,128)(2,1)}, bf16[384,768]{1,0:T(8,128)(2,1)S(1)}, u32[]{:S(2)}, u32[]{:S(2)}) collective-permute-start(bf16[384,768]{1,0:T(8,128)(2,1)} %fusion.11), channel_id=1, source_target_pairs={{0,8},{1,9},{2,10},{3,11},{4,12},{5,13},{6,14},{7,15},{8,0},{9,1},... | collective-permute-start | bytes 1769480 | tf_op jit(solution)/shard_map/ppermute | solution.py:537
  451.1 43.9 %collective-permute-start.64 = (bf16[384,768]{1,0:T(8,128)(2,1)}, bf16[384,768]{1,0:T(8,128)(2,1)S(1)}, u32[]{:S(2)}, u32[]{:S(2)}) collective-permute-start(bf16[384,768]{1,0:T(8,128)(2,1)} %fusion.10), channel_id=1, source_target_pairs={{0,16},{1,17},{2,18},{3,19},{4,20},{5,21},{6,22},{7,23},{8,24},{9,... | collective-permute-start | bytes 1769480 | tf_op jit(solution)/shard_map/ppermute | solution.py:537
  451.9 63.2 %collective-permute-start.67 = (bf16[512,1536]{1,0:T(8,128)(2,1)}, bf16[512,1536]{1,0:T(8,128)(2,1)}, u32[]{:S(2)}, u32[]{:S(2)}) collective-permute-start(bf16[512,1536]{1,0:T(8,128)(2,1)} %pad_maximum_fusion.3), channel_id=1, source_target_pairs={{0,1},{1,0},{2,3},{3,2},{4,5},{5,4},{6,7},{7,6},{8,9},{9,8},{10,11... | collective-permute-start | bytes 4718600 | tf_op jit(solution)/shard_map/ppermute | solution.py:537
  500.2 17.8 %collective-permute-start.69 = (bf16[384,768]{1,0:T(8,128)(2,1)}, bf16[384,768]{1,0:T(8,128)(2,1)S(1)}, u32[]{:S(2)}, u32[]{:S(2)}) collective-permute-start(bf16[384,768]{1,0:T(8,128)(2,1)} %fusion.13), channel_id=1, source_target_pairs={{0,8},{1,9},{2,10},{3,11},{4,12},{5,13},{6,14},{7,15},{8,0},{9,1},... | collective-permute-start | bytes 1769480 | tf_op jit(solution)/shard_map/ppermute | solution.py:537
  500.8 17.2 %collective-permute-start.70 = (bf16[384,768]{1,0:T(8,128)(2,1)}, bf16[384,768]{1,0:T(8,128)(2,1)S(1)}, u32[]{:S(2)}, u32[]{:S(2)}) collective-permute-start(bf16[384,768]{1,0:T(8,128)(2,1)} %fusion.12), channel_id=1, source_target_pairs={{0,16},{1,17},{2,18},{3,19},{4,20},{5,21},{6,22},{7,23},{8,24},{9,... | collective-permute-start | bytes 1769480 | tf_op jit(solution)/shard_map/ppermute | solution.py:537
  501.6 16.2 %collective-permute-start.68 = (bf16[192,768]{1,0:T(8,128)(2,1)S(1)}, bf16[192,768]{1,0:T(8,128)(2,1)S(1)}, u32[]{:S(2)}, u32[]{:S(2)}) collective-permute-start(bf16[192,768]{1,0:T(8,128)(2,1)S(1)} %constant_dynamic-slice_fusion.6), channel_id=1, source_target_pairs={{0,1},{1,0},{2,3},{3,2},{4,5},{5,4},{6,7},{7,6},{8,9},{9,8},{10,11... | collective-permute-start | bytes 884744 | tf_op jit(solution)/shard_map/ppermute | solution.py:537
  518.2 14.6 %collective-permute-start.73 = (bf16[192,768]{1,0:T(8,128)(2,1)S(1)}, bf16[192,768]{1,0:T(8,128)(2,1)S(1)}, u32[]{:S(2)}, u32[]{:S(2)}) collective-permute-start(bf16[192,768]{1,0:T(8,128)(2,1)S(1)} %add_convert_fusion.22), channel_id=1, source_target_pairs={{0,2},{1,3},{2,0},{3,1},{4,6},{5,7},{6,4},{7,5},{8,10},{9,11},{10,... | collective-permute-start | bytes 884744 | tf_op jit(solution)/shard_map/ppermute | solution.py:537
  521.8 14.8 %collective-permute-start.74 = (bf16[192,768]{1,0:T(8,128)(2,1)S(1)}, bf16[192,768]{1,0:T(8,128)(2,1)S(1)}, u32[]{:S(2)}, u32[]{:S(2)}) collective-permute-start(bf16[192,768]{1,0:T(8,128)(2,1)S(1)} %constant_dynamic-slice_fusion.4), channel_id=1, source_target_pairs={{0,1},{1,0},{2,3},{3,2},{4,5},{5,4},{6,7},{7,6},{8,9},{9,8},{10,11... | collective-permute-start | bytes 884744 | tf_op jit(solution)/shard_map/ppermute | solution.py:537
  534.2 14.7 %collective-permute-start.76 = (bf16[384,768]{1,0:T(8,128)(2,1)S(1)}, bf16[384,768]{1,0:T(8,128)(2,1)S(1)}, u32[]{:S(2)}, u32[]{:S(2)}) collective-permute-start(bf16[384,768]{1,0:T(8,128)(2,1)S(1)} %fusion.15), channel_id=1, source_target_pairs={{0,8},{1,9},{2,10},{3,11},{4,12},{5,13},{6,14},{7,15},{8,0},{9,1},... | collective-permute-start | bytes 1769480 | tf_op jit(solution)/shard_map/ppermute | solution.py:537
  535.7 14.6 %collective-permute-start.77 = (bf16[384,768]{1,0:T(8,128)(2,1)S(1)}, bf16[384,768]{1,0:T(8,128)(2,1)S(1)}, u32[]{:S(2)}, u32[]{:S(2)}) collective-permute-start(bf16[384,768]{1,0:T(8,128)(2,1)S(1)} %fusion.14), channel_id=1, source_target_pairs={{0,16},{1,17},{2,18},{3,19},{4,20},{5,21},{6,22},{7,23},{8,24},{9,... | collective-permute-start | bytes 1769480 | tf_op jit(solution)/shard_map/ppermute | solution.py:537
  536.6 20.3 %collective-permute-start.80 = (bf16[192,768]{1,0:T(8,128)(2,1)S(1)}, bf16[192,768]{1,0:T(8,128)(2,1)S(1)}, u32[]{:S(2)}, u32[]{:S(2)}) collective-permute-start(bf16[192,768]{1,0:T(8,128)(2,1)S(1)} %add_convert_fusion.18), channel_id=1, source_target_pairs={{0,2},{1,3},{2,0},{3,1},{4,6},{5,7},{6,4},{7,5},{8,10},{9,11},{10,... | collective-permute-start | bytes 884744 | tf_op jit(solution)/shard_map/ppermute | solution.py:537
  555.1 14.9 %collective-permute-start.81 = (bf16[192,768]{1,0:T(8,128)(2,1)S(1)}, bf16[192,768]{1,0:T(8,128)(2,1)S(1)}, u32[]{:S(2)}, u32[]{:S(2)}) collective-permute-start(bf16[192,768]{1,0:T(8,128)(2,1)S(1)} %constant_dynamic-slice_fusion.3), channel_id=1, source_target_pairs={{0,1},{1,0},{2,3},{3,2},{4,5},{5,4},{6,7},{7,6},{8,9},{9,8},{10,11... | collective-permute-start | bytes 884744 | tf_op jit(solution)/shard_map/ppermute | solution.py:537
  570.2 13.9 %collective-permute-start.86 = (bf16[256,1536]{1,0:T(8,128)(2,1)S(1)}, bf16[256,1536]{1,0:T(8,128)(2,1)S(1)}, u32[]{:S(2)}, u32[]{:S(2)}) collective-permute-start(bf16[256,1536]{1,0:T(8,128)(2,1)S(1)} %copy-done.85), channel_id=1, source_target_pairs={{0,4},{1,5},{2,6},{3,7},{4,0},{5,1},{6,2},{7,3},{8,12},{9,13},{10,... | collective-permute-start | bytes 2359304 | tf_op jit(solution)/shard_map/ppermute | solution.py:537
  570.3 13.9 %collective-permute-start.85 = (bf16[256,1536]{1,0:T(8,128)(2,1)S(1)}, bf16[256,1536]{1,0:T(8,128)(2,1)S(1)}, u32[]{:S(2)}, u32[]{:S(2)}) collective-permute-start(bf16[256,1536]{1,0:T(8,128)(2,1)S(1)} %copy-done.84), channel_id=1, source_target_pairs={{0,4},{1,5},{2,6},{3,7},{4,0},{5,1},{6,2},{7,3},{8,12},{9,13},{10,... | collective-permute-start | bytes 2359304 | tf_op jit(solution)/shard_map/ppermute | solution.py:537
  571.6 23.0 %collective-permute-start.87 = (bf16[192,768]{1,0:T(8,128)(2,1)S(1)}, bf16[192,768]{1,0:T(8,128)(2,1)S(1)}, u32[]{:S(2)}, u32[]{:S(2)}) collective-permute-start(bf16[192,768]{1,0:T(8,128)(2,1)S(1)} %add_convert_fusion.14), channel_id=1, source_target_pairs={{0,2},{1,3},{2,0},{3,1},{4,6},{5,7},{6,4},{7,5},{8,10},{9,11},{10,... | collective-permute-start | bytes 884744 | tf_op jit(solution)/shard_map/ppermute | solution.py:537
  595.9 20.2 %collective-permute-start.91 = (f32[4,1536]{1,0:T(4,128)S(1)}, f32[4,1536]{1,0:T(4,128)S(1)}, u32[]{:S(2)}, u32[]{:S(2)}) collective-permute-start(f32[4,1536]{1,0:T(4,128)S(1)} %pad_maximum_fusion.10), channel_id=1, source_target_pairs={{0,1},{1,0},{2,3},{3,2},{4,5},{5,4},{6,7},{7,6},{8,9},{9,8},{10,11... | collective-permute-start | bytes 73736 | tf_op jit(solution)/shard_map/ppermute | solution.py:537
  (132 other events, 1568.8 us)

commit v3 on v2

--- a/solution.py
+++ b/solution.py
@@ -1,7 +1,9 @@
 import functools
+import math
 
 import jax
 import jax.numpy as jnp
+import numpy as np
 from jax import lax
 from jax.experimental import pallas as pl
 from jax.experimental.pallas import tpu as pltpu
@@ -21,17 +23,16 @@
 contract_cols = (((1,), (1,)), ((), ()))
 f32 = jnp.float32
 bf16 = jnp.bfloat16
-VMEM_LIMIT = 56 * 1024 * 1024
 SMEM_SPEC = pl.BlockSpec(memory_space=pltpu.SMEM)
 VMEM_SPEC = pl.BlockSpec(memory_space=pltpu.VMEM)
 
 
 def rotary_tables(length, head_width):
     halfway = head_width // 2
-    frequency = theta_base ** (-2.0 * jnp.arange(halfway, dtype=f32) / head_width)
-    angles = jnp.arange(length, dtype=f32)[:, None] * frequency[None, :]
-    angles = jnp.concatenate([angles, angles], axis=1)
-    return (jnp.cos(angles), jnp.sin(angles))
+    frequency = np.float32(theta_base) ** (np.float32(-2.0) * np.arange(halfway, dtype=np.float32) / head_width)
+    angles = np.arange(length, dtype=np.float32)[:, None] * frequency.astype(np.float32)[None, :]
+    angles = np.concatenate([angles, angles], axis=1).astype(np.float64)
+    return jnp.asarray(np.cos(angles), f32), jnp.asarray(np.sin(angles), f32)
 
 
 def turn(values):
@@ -70,8 +71,17 @@
 COST = pl.CostEstimate(flops=1000000, bytes_accessed=0, transcendentals=0)
 
 
+EXTRA = 6 * 1024 * 1024
+
+
+def room(value):
+    return math.prod(value.shape) * jnp.dtype(value.dtype).itemsize
+
+
 def run(name, kernel, outs, scalars, *args, scratch=()):
     many = isinstance(outs, (tuple, list))
+    held = sum(room(v) for v in args) + sum(room(v) for v in (outs if many else [outs]))
+    held += sum(room(v) for v in scratch)
     return pl.pallas_call(
         kernel,
         out_shape=outs,
@@ -79,7 +89,7 @@
         out_specs=[VMEM_SPEC] * len(outs) if many else VMEM_SPEC,
         scratch_shapes=list(scratch),
         cost_estimate=COST,
-        compiler_params=pltpu.CompilerParams(vmem_limit_bytes=VMEM_LIMIT),
+        compiler_params=pltpu.CompilerParams(vmem_limit_bytes=held + EXTRA),
         name=name,
     )(*scalars, *args)
 
@@ -357,32 +367,39 @@
     spread(place, pieces, product)
 
 
-def ff_act_kernel(chips, place, limits, norm_a, norm_b, cot_a, cot_b, *refs):
+def ff_act_kernel(chips, index, place, limits, *refs):
     if chips:
-        *pieces, act_a, act_b, grad_a, grad_b, up, down = refs
+        norm_a, norm_b, cot_a, cot_b, *pieces, act_a, act_b, grad_a, grad_b, up, down = refs
         join(place, chips, pieces, [up, down])
+        norms = ([norm_a], [norm_b])
+        first = 0
     else:
-        up, down, act_a, act_b, grad_a, grad_b = refs
-    seq_len = norm_a.shape[0]
+        norm_a, norm_low, norm_high, cot_a, cot_b, up, down, act_a, act_b, grad_a, grad_b = refs
+        norms = ([norm_a], [norm_low, norm_high])
+        first = 2
+    sides = zip(norms, (cot_a, cot_b), (act_a, act_b), (grad_a, grad_b))
     units = up.shape[1]
     block, tile = 256, 256 if units % 256 == 0 else 128
-    for s, (norm, cot, act, grad) in enumerate(((norm_a, cot_a, act_a, grad_a), (norm_b, cot_b, act_b, grad_b))):
-        limit = limits[s]
-
-        def step(i, carry):
-            rows = at(i * block, block)
-            for n in range(0, units, tile):
-                cols = slice(n, n + tile)
-                preact = jnp.dot(norm[rows, :], up[:, cols], preferred_element_type=f32)
-                grad_active = jnp.dot(cot[rows, :], down[:, cols], preferred_element_type=f32)
-                mask = n + lax.broadcasted_iota(jnp.int32, (block, tile), 1) < limit
-                cdf = 0.5 * (1.0 + lax.erf(preact * 0.7071067811865476))
-                slope = cdf + preact * jnp.exp(-0.5 * preact * preact) * 0.3989422804014327
-                act[rows, cols] = jnp.where(mask, preact * cdf, 0.0).astype(bf16)
-                grad[rows, cols] = jnp.where(mask, grad_active * slope, 0.0).astype(bf16)
-            return carry
-
-        lax.fori_loop(0, seq_len // block, step, 0)
+    for s, (norm_parts, cot, act, grad) in enumerate(sides):
+        limit = limits[index, first + s]
+        for k, norm in enumerate(norm_parts):
+            length = norm.shape[0]
+
+            def step(i, carry):
+                here = at(i * block, block)
+                rows = at(k * length + i * block, block)
+                for n in range(0, units, tile):
+                    cols = slice(n, n + tile)
+                    preact = jnp.dot(norm[here, :], up[:, cols], preferred_element_type=f32)
+                    grad_active = jnp.dot(cot[rows, :], down[:, cols], preferred_element_type=f32)
+                    mask = n + lax.broadcasted_iota(jnp.int32, (block, tile), 1) < limit
+                    cdf = 0.5 * (1.0 + lax.erf(preact * 0.7071067811865476))
+                    slope = cdf + preact * jnp.exp(-0.5 * preact * preact) * 0.3989422804014327
+                    act[rows, cols] = jnp.where(mask, preact * cdf, 0.0).astype(bf16)
+                    grad[rows, cols] = jnp.where(mask, grad_active * slope, 0.0).astype(bf16)
+                return carry
+
+            lax.fori_loop(0, length // block, step, 0)
 
 
 def rows_back_kernel(count, base, *refs):
@@ -442,7 +459,7 @@
             out_specs=[pl.BlockSpec(v, lambda j, order: (0, 0)) for v in outs],
         ),
         cost_estimate=COST,
-        compiler_params=pltpu.CompilerParams(vmem_limit_bytes=VMEM_LIMIT),
+        compiler_params=pltpu.CompilerParams(vmem_limit_bytes=40 * 1024 * 1024),
         name="ff_weight",
     )(order, *norms, *cots, *acts, *grads)
 
@@ -748,15 +765,14 @@
 
         w_down_t = w_down.T
         qkv_other = line.send(w_qkv, core_bit)
-        tokens = jnp.concatenate([block_in, cotangent])
-        tokens_other = line.send(tokens, core_bit)
+        small = jnp.concatenate([segment_ids, jnp.broadcast_to(granularity[:, None], (mp_size, seq_len))])
+        small_other = line.send(small, core_bit)
+        x_other = line.send(block_in, core_bit)
         if units == width:
             rest = jnp.concatenate([w_out, w_up, w_down_t])
         else:
             rest = jnp.concatenate([w_out, jnp.concatenate([w_up, w_down_t], axis=1)])
         rest_other = line.send(rest, core_bit)
-        small = jnp.concatenate([segment_ids, jnp.broadcast_to(granularity[:, None], (mp_size, seq_len))])
-        small_other = line.send(small, core_bit)
 
         qkv_pieces = line.kernel(
             "cut_attention",
@@ -765,15 +781,17 @@
             [place],
             w_qkv,
             qkv_other,
+            wait=(small_other,),
         )
         heads = [Gather(line, qkv_pieces[0])]
+        cot_near = line.send(cotangent, near_bit)
         normed1 = line.kernel(
             "norm",
             norm_kernel,
             shape((2 * seq_len, width)),
             [],
             block_in,
-            tokens_other,
+            x_other,
             gain1,
             bias1,
         )
@@ -786,19 +804,9 @@
             w_up,
             w_down_t,
             rest_other,
-            wait=(small_other,),
         )
         heads.append(Gather(line, qkv_pieces[1]))
-        small_other = line.after(small_other)
-        segments = jnp.stack([small[0], small_other[0]])
-        seg_col = segments[:, :, None]
-        seg_row = segments[:, None, :]
         cosine, sine = rotary_tables(seq_len, HEAD_DIM)
-        levels = jnp.stack([small[1:, 0], small_other[1:, 0]])
-        limits = BLOCK * jnp.power(2, levels)
-        limits = jnp.stack([limits[0, mp], limits[1, mp], limits[0, mp ^ 1], limits[1, mp ^ 1]])
-        starts = [(mp ^ (2 * k)) * units + core * half_units for k in range(mp_size // 2)]
-        limits = [(limits - start).astype(jnp.int32) for start in starts]
         last = mp_size // 2 - 1
 
         qkv_wide, qkv_low, contexts, logs = [], [], [], []
@@ -827,11 +835,23 @@
             logs.append(d)
 
         heads[0].turn()
+
+        def from_small(own, other):
+            segments = jnp.stack([own[0], other[0]])
+            levels = jnp.stack([own[1:, 0], other[1:, 0]])
+            ends = BLOCK * jnp.power(2, levels)
+            ends = jnp.stack([ends[0, mp], ends[1, mp], ends[0, mp ^ 1], ends[1, mp ^ 1]])
+            starts = [(mp ^ (2 * k)) * units + core * half_units for k in range(mp_size // 2)]
+            limits = (ends[None, :] - jnp.stack(starts)[:, None]).astype(jnp.int32)
+            return limits, segments[:, :, None], segments[:, None, :]
+
+        limits, seg_col, seg_row = line.op(from_small, small, small_other)
+        heads[1].turn()
+        heads[0].wait()
+        line.wait(cot_near)
         slices = [ff_piece]
         for bit in far_bits:
             slices = slices + [line.send(v, bit) for v in slices]
-        heads[1].turn()
-        heads[0].wait()
         heads.append(Gather(line, qkv_pieces[2]))
         attend(0)
         heads[1].wait()
@@ -843,11 +863,10 @@
         outs.turn()
         line.wait(*ctx_near)
         outs_other = [out_piece_got] + outs.send_first(core_bit)
-        line.wait(*outs_other[1:], *slices[1:])
-        ffs = {last: Gather(line, slices[last])}
-        cot_near = line.send(cotangent, near_bit)
         attend(2)
         outs.wait()
+        line.wait(*outs_other[1:], *slices[1:])
+        ffs = {0: Gather(line, slices[0])}
         ctx_near.append(line.send(contexts[2][1], core_bit))
         outs_other += outs.send_last(core_bit)
         out_mine, out_got = line.kernel(
@@ -857,9 +876,10 @@
             [place],
             *outs.pieces(),
             *outs_other,
+            wait=(ctx_near[2],),
         )
-        line.wait(ctx_near[2])
-        ffs[last].turn()
+        cot_both = line.send(cot_near, core_bit)
+        cot_core = line.send(cotangent, core_bit)
         hidden1, normed2, context = line.kernel(
             "out",
             functools.partial(out_kernel, chunks),
@@ -874,14 +894,14 @@
             bias2,
         )
 
+        line.wait(cot_both, cot_core)
         norm_near = line.send(normed2, near_bit)
         norm_core = line.send(normed2, core_bit)
-        ffs[last].wait()
-        line.wait(norm_core, cot_near)
-        for k in range(last - 1, -1, -1):
+        ffs[0].turn()
+        ffs[0].wait()
+        line.wait(norm_core)
+        for k in range(1, last + 1):
             ffs[k] = Gather(line, slices[k])
-        cot_both = line.send(cot_near, core_bit)
-        cot_core = line.after(tokens_other)[seq_len:]
         cot_rows = [cotangent, cot_core, cot_near, cot_both]
         outs_ff = [shape((seq_len, half_units))] * 4
         wide_ff = [shape((width, half_units))] * 2
@@ -890,9 +910,9 @@
         def ff_own(k):
             act_a, act_b, grad_a, grad_b, up, down = line.kernel(
                 "ff_own",
-                functools.partial(ff_act_kernel, chips),
+                functools.partial(ff_act_kernel, chips, k),
                 outs_ff + wide_ff,
-                [place, limits[k][:2]],
+                [place, limits],
                 normed2,
                 norm_core,
                 *cot_rows[:2],
@@ -906,11 +926,11 @@
         def ff_near(k):
             act_a, act_b, grad_a, grad_b = line.kernel(
                 "ff_near",
-                functools.partial(ff_act_kernel, 0),
+                functools.partial(ff_act_kernel, 0, k),
                 outs_ff,
-                [place, limits[k][2:]],
+                [place, limits],
                 norm_near,
-                norm_both,
+                *norm_both,
                 *cot_rows[2:],
                 ups[k],
                 downs[k],
@@ -919,13 +939,13 @@
             grads[k] += [grad_a, grad_b]
 
         def ff_grads(k):
-            lefts = [line.after(normed2), norm_core, norm_near, norm_both]
+            lefts = [line.after(normed2), norm_core, norm_near, norm_joined]
             parts = ff_parts(lefts, cot_rows, acts[k], grads[k])
             line.last = [parts[0]]
-            return Scatter(line, parts)
-
-        def rows_back(name, lefts, i, weights, kind):
-            outs = [shape((seq_len, width), kind)] if kind == f32 else [shape((seq_len // 2, width))] * 2
+            return parts
+
+        def rows_back(name, lefts, i, weights, kind, count=1):
+            outs = [shape((seq_len // count, width), kind)] * count
             result = line.kernel(
                 name,
                 functools.partial(rows_back_kernel, len(weights), 0),
@@ -934,40 +954,43 @@
                 *[v[i] for v in lefts.values()],
                 *weights.values(),
             )
-            return result[0] if kind == f32 else result
+            return result[0] if count == 1 else result
 
         def add_halves(a, low, high):
             middle = a.shape[0] // 2
             return jnp.concatenate([add_low(a[:middle], low), add_low(a[middle:], high)])
 
-        ff_own(last)
-        line.wait(cot_both)
-        for k in range(last - 1, -1, -1):
+        ff_own(0)
+        line.wait(norm_near)
+        arrived = line.after(norm_near)
+        middle = seq_len // 2
+        norm_both = [line.send(v, core_bit) for v in (arrived[:middle], arrived[middle:])]
+        line.wait(*norm_both)
+        ff_near(0)
+        norm_joined = line.op(lambda a, c: jnp.concatenate([a, c]), *norm_both)
+        for k in range(1, last + 1):
             ffs[k].turn()
-        line.wait(norm_near)
-        norm_both = line.send(norm_near, core_bit)
-        ctx_far = [line.send(c[0], core_bit) for c in contexts[:2]]
-        ff_near(last)
-        ctx_far.append(line.send(contexts[2][0], core_bit))
+        ctx_far = [line.send(c[0], core_bit) for c in contexts]
+        parts = ff_grads(0)
         line.wait(*ctx_far)
-        scatters = {last: ff_grads(last)}
-        for k in range(last - 1, -1, -1):
+        scatters = {0: Scatter(line, parts)}
+        for k in range(1, last + 1):
             ff_own(k)
-            if k == last - 1:
-                scatters[last].turn()
+            if k == 1:
+                scatters[0].turn()
             ff_near(k)
-        back_both = rows_back("ff_back", grads, 3, ups, bf16)
+        back_both = rows_back("ff_back", grads, 3, ups, bf16, 2)
         back_both = [line.send(v, core_bit) for v in back_both]
         back_near = rows_back("ff_back", grads, 2, ups, f32)
+        held = {0: scatters[0].close()}
         back_near = line.op(add_halves, back_near, *back_both)
         back_near = line.send(back_near, near_bit)
-        held = {last: scatters[last].close()}
-        for k in range(last - 1, -1, -1):
-            scatters[k] = ff_grads(k)
-        back_beside = rows_back("ff_back", grads, 1, ups, bf16)
-        for k in range(last - 1, -1, -1):
+        for k in range(1, last + 1):
+            scatters[k] = Scatter(line, ff_grads(k))
+        back_beside = rows_back("ff_back", grads, 1, ups, bf16, 2)
+        back_beside = [line.send(v, core_bit) for v in back_beside]
+        for k in range(1, last + 1):
             scatters[k].turn()
-        back_beside = [line.send(v, core_bit) for v in back_beside]
         back_own = rows_back("ff_back", grads, 0, ups, f32)
 
         grad_hidden1, grad_attn, sums2 = line.kernel(
@@ -982,7 +1005,6 @@
             cotangent,
             gain2,
         )
-        far_got = line.send(held[last], far_bits[0]) if len(far_bits) == 1 else None
         keep, send, grad_send = line.kernel(
             "out_back",
             out_back_kernel,
@@ -994,7 +1016,7 @@
         )
         context_got = line.send(send, core_bit)
         grad_got = line.send(grad_send, core_bit)
-        fore_both = rows_back("ff_fore", acts, 3, downs, bf16)
+        fore_both = rows_back("ff_fore", acts, 3, downs, bf16, 2)
         line.wait(context_got, grad_got)
         grad_low, qkv_scatters = [], []
 
@@ -1019,11 +1041,9 @@
             return by_chip(parts)
 
         parts = attend_back(0)
-        if len(far_bits) == 1:
-            own_sum = scatters[0].close()
-        else:
-            for k in range(last - 1, -1, -1):
-                held[k] = scatters[k].close()
+        for k in range(1, last + 1):
+            held[k] = scatters[k].close()
+        far_got = line.send(held[last], far_bits[0]) if len(far_bits) == 1 else None
         qkv_scatters.append(Scatter(line, parts))
         fore_both = [line.send(v, core_bit) for v in fore_both]
         fore_near = rows_back("ff_fore", acts, 2, downs, f32)
@@ -1031,14 +1051,6 @@
         qkv_scatters[0].turn()
         fore_near = line.send(fore_near, near_bit)
         parts = attend_back(1)
-        if len(far_bits) == 1:
-            ff_share = line.op(add_low, own_sum, far_got)
-        else:
-            held = [held[k] for k in range(len(slices))]
-            for bit in reversed(far_bits):
-                middle = len(held) // 2
-                held = [add_low(a, flip(c, bit)) for a, c in zip(held[:middle], held[middle:])]
-            ff_share = held[0]
         qkv_scatters.append(Scatter(line, parts))
         out_parts = line.kernel(
             "out_weight",
@@ -1056,6 +1068,14 @@
         qkv_scatters[1].turn()
         parts = attend_back(2)
         line.wait(fore_near)
+        if len(far_bits) == 1:
+            ff_share = line.op(add_low, held[0], far_got)
+        else:
+            held = [held[k] for k in range(len(slices))]
+            for bit in reversed(far_bits):
+                middle = len(held) // 2
+                held = [add_low(a, flip(c, bit)) for a, c in zip(held[:middle], held[middle:])]
+            ff_share = held[0]
         qkv_scatters.append(Scatter(line, parts))
         qkv_z[0].turn()
         qkv_z.append(OverMp(line, qkv_scatters[1].close()))
@@ -1101,7 +1121,7 @@
         qkv_z[2].back()
         out_z.turn()
         sums = SumAll(line, jnp.concatenate([sums1[:2], sums2[:2]]))
-        fore_beside = rows_back("ff_fore", acts, 1, downs, bf16)
+        fore_beside = rows_back("ff_fore", acts, 1, downs, bf16, 2)
         shares.append(qkv_z[2].close())
         out_z.back()
         sums.turn()

time: 657 us -> 542 us (0.82)
  Pallas kernels: 302 us -> 184 us
  local copies, waits for them, and re-layouts: 38 us -> 61.9 us
  waiting for transfers between devices: 178 us -> 163 us
  other arithmetic: 37.4 us -> 26.8 us
    pallas_call x32, Pallas kernels: 265 us -> 155 us  [run(): pl.pallas_call(kernel, out_shape=outs, in_specs=[SMEM_SPEC] * len(scalars...]
    unnamed x185 -> x280, local copies, waits for them, and re-layouts: 16.4 us -> 47.3 us
    ppermute x104 -> x106, waiting for transfers between devices: 178 us -> 163 us  [flip(): return lax.ppermute(value, AXES, [(i, i ^ bit) for i in range(total)])]
    pallas_call x2, Pallas kernels: 37 us -> 28.7 us  [ff_weight(): pl.pallas_call(functools.partial(ff_weight_kernel, count), out_shape=[sha...]
    ppermute x104 -> x106, starting transfers between devices: 89.1 us -> 92.5 us  [flip(): return lax.ppermute(value, AXES, [(i, i ^ bit) for i in range(total)])]
  transfers between devices with their start and end apart: 104 -> 106, of which waited for: 35 -> 47; matrix products, arithmetic and copies ran while one was open for 8% -> 6% of each run, Pallas kernels for 41% -> 34%
where the time goes in v3:
time: 542 us; the launch traced here: 532 us
  Pallas kernels  184 us (34%)
  waiting for transfers between devices  163 us (30%)
  starting transfers between devices  92.5 us (17%)
  local copies, waits for them, and re-layouts  61.9 us (11%)
  other arithmetic  26.8 us (5%)
    ppermute x106, waiting for transfers between devices, flip(): return lax.ppermute(value, AXES, [(i, i ^ bit) for i in range(total)])  163 us
    pallas_call x32, Pallas kernels, run(): pl.pallas_call(kernel, out_shape=outs, in_specs=[SMEM_SPEC] * len(scalars...  155 us
    ppermute x106, starting transfers between devices, flip(): return lax.ppermute(value, AXES, [(i, i ^ bit) for i in range(total)])  92.5 us
    unnamed x280, local copies, waits for them, and re-layouts  47.3 us
    pallas_call x2, Pallas kernels, ff_weight(): pl.pallas_call(functools.partial(ff_weight_kernel, count), out_shape=[sha...  28.7 us
  transfers between devices with their start and end apart: 106, of which 47 were waited for; matrix products, arithmetic and copies ran while one was open for 6% of the time, Pallas kernels for 34%

profile of v3, /device:TPU:0, one launch (start us, length us, event | category | flops | bytes accessed | tf_op | source)
XLA Modules:
  0.0 531.6 jit_solution(13587979903430587115)
XLA Ops:
  1.2 2.9 pad_maximum_fusion
  5.0 4.8 collective-permute-done
  9.7 2.8 cut_attention.1
  12.6 2.8 collective-permute-start.10
  19.9 3.8 norm.1.norm_ref
  29.1 2.5 collective-permute-done.7.refs_1_
  35.5 2.0 collective-permute-start.8
  38.3 2.7 pad_add_fusion.5
  41.0 3.5 collective-permute-done.5.refs_1_
  56.9 2.6 collective-permute-start.25
  63.4 9.0 %attend.3 = (bf16[1536,768]{1,0:T(8,128)(2,1)S(1)}, bf16[1024,768]{1,0:T(8,128)(2,1)S(1)}, bf16[2,512,256]{2,1,0:T(8,128)(2,1)S(1)}, f32[1024,128]{1,0:T(8,128)S(1)}) custom-call(s32[5]{0:T(128)S(1)} %pad_add_fusion.4.place, bf16[1024,1536]{1,0:T(8,128)(2,1)S(1)} %norm.1.norm_ref, f32[512,128]{1,0:T(8,128)S(1)} %copy-done.29, f32[512,128]{1,0:T(8,128)S(1)} %copy-done.28, ...), custom_call_target="tpu_custom_call" | custom-call | flops 1000000 | tf_op jit(solution)/shard_map/attend/pallas_call | solution.py:85
  82.1 9.2 %attend.4 = (bf16[1536,768]{1,0:T(8,128)(2,1)S(1)}, bf16[1024,768]{1,0:T(8,128)(2,1)S(1)}, bf16[2,512,256]{2,1,0:T(8,128)(2,1)S(1)}, f32[1024,128]{1,0:T(8,128)S(1)}) custom-call(s32[5]{0:T(128)S(1)} %pad_add_fusion.4.place, bf16[1024,1536]{1,0:T(8,128)(2,1)S(1)} %norm.1.norm_ref, f32[512,128]{1,0:T(8,128)S(1)} %copy-done.29, f32[512,128]{1,0:T(8,128)S(1)} %copy-done.28, ...), custom_call_target="tpu_custom_call" | custom-call | flops 1000000 | tf_op jit(solution)/shard_map/attend/pallas_call | solution.py:85
  94.4 2.2 collective-permute-done.18.refs_4_
  102.2 8.9 %attend.5 = (bf16[1536,768]{1,0:T(8,128)(2,1)S(1)}, bf16[1024,768]{1,0:T(8,128)(2,1)S(1)}, bf16[2,512,256]{2,1,0:T(8,128)(2,1)S(1)}, f32[1024,128]{1,0:T(8,128)S(1)}) custom-call(s32[5]{0:T(128)S(1)} %pad_add_fusion.4.place, bf16[1024,1536]{1,0:T(8,128)(2,1)S(1)} %norm.1.norm_ref, f32[512,128]{1,0:T(8,128)S(1)} %copy-done.29, f32[512,128]{1,0:T(8,128)S(1)} %copy-done.28, ...), custom_call_target="tpu_custom_call" | custom-call | flops 1000000 | tf_op jit(solution)/shard_map/attend/pallas_call | solution.py:85
  118.6 5.9 %out.1 = (f32[512,1536]{1,0:T(8,128)S(1)}, bf16[512,1536]{1,0:T(8,128)(2,1)S(1)}, bf16[512,1536]{1,0:T(8,128)(2,1)S(1)}) custom-call(s32[5]{0:T(128)S(1)} %pad_add_fusion.4.place, bf16[512,1536]{1,0:T(8,128)(2,1)S(1)} %copy-done.23, bf16[512,256]{1,0:T(8,128)(2,1)} %get-tuple-element.522.refs_0_, bf16[512,256]{1,0:T(8,128)(2,1)} %get-tuple-element.523.refs_1_, ...), custom_call_target="tpu_custom_call" | custom-call | flops 1000000 | tf_op jit(solution)/shard_map/out/pallas_call | solution.py:85
  128.9 16.1 %collective-permute-done.32.refs_5_ = bf16[768,768]{1,0:T(8,128)(2,1)S(1)} collective-permute-done((bf16[768,768]{1,0:T(8,128)(2,1)S(1)}, bf16[768,768]{1,0:T(8,128)(2,1)S(1)}, u32[]{:S(2)}, u32[]{:S(2)}) %collective-permute-start.32) | collective-permute-done | bytes 1179680 | tf_op jit(solution)/shard_map/ppermute | solution.py:554
  147.4 13.2 %collective-permute-done.34.refs_8_ = bf16[384,768]{1,0:T(8,128)(2,1)S(1)} collective-permute-done((bf16[384,768]{1,0:T(8,128)(2,1)S(1)}, bf16[384,768]{1,0:T(8,128)(2,1)S(1)}, u32[]{:S(2)}, u32[]{:S(2)}) %collective-permute-start.34) | collective-permute-done | bytes 589856 | tf_op jit(solution)/shard_map/ppermute | solution.py:554
  161.1 8.2 %ff_own.2 = (bf16[512,768]{1,0:T(8,128)(2,1)S(1)}, bf16[512,768]{1,0:T(8,128)(2,1)S(1)}, bf16[512,768]{1,0:T(8,128)(2,1)S(1)}, bf16[512,768]{1,0:T(8,128)(2,1)S(...) custom-call(s32[5]{0:T(128)S(1)} %pad_add_fusion.4.place, s32[2,4]{1,0:T(2,128)S(1)} %broadcast_subtract_fusion.limits, ...), custom_call_target="tpu_custom_call" | custom-call | flops 1000000 | tf_op jit(solution)/shard_map/ff_own/pallas_call | solution.py:85
  173.0 7.3 %ff_near.2 = (bf16[512,768]{1,0:T(8,128)(2,1)S(1)}, bf16[512,768]{1,0:T(8,128)(2,1)S(1)}, bf16[512,768]{1,0:T(8,128)(2,1)S(1)}, bf16[512,768]{1,0:T(8,128)(2,1)S(1)}) custom-call(s32[5]{0:T(128)S(1)} %pad_add_fusion.4.place, s32[2,4]{1,0:T(2,128)S(1)} %broadcast_subtract_fusion.limits, bf16[512,1536]{1,0:T(8,128)(2,1)S(1)} %collective-permute-done.30.refs_0_.refs_2_, ...), custom_call_target="tpu_custom_call" | custom-call | flops 1000000 | tf_op jit(solution)/shard_map/ff_near/pallas_call | solution.py:85
  181.6 16.4 %collective-permute-done.39.refs_5_ = bf16[768,768]{1,0:T(8,128)(2,1)S(1)} collective-permute-done((bf16[768,768]{1,0:T(8,128)(2,1)S(1)}, bf16[768,768]{1,0:T(8,128)(2,1)S(1)}, u32[]{:S(2)}, u32[]{:S(2)}) %collective-permute-start.39) | collective-permute-done | bytes 1179680 | tf_op jit(solution)/shard_map/ppermute | solution.py:554
  203.9 14.0 %ff_weight.2 = (bf16[768,768]{1,0:T(8,128)(2,1)S(1)}, bf16[768,768]{1,0:T(8,128)(2,1)S(1)}, bf16[768,768]{1,0:T(8,128)(2,1)S(1)}, bf16[384,768]{1,0:T(8,128)(2,1)S(1)}, bf16[384,768]{1,0:T(8,128)(2,1)S(1)}) custom-call(s32[4]{0:T(128)S(1)} %get-tuple-element.723.place, bf16[512,1536]{1,0:T(8,128)(2,1)S(1)} %copy-done.18, bf16[512,1536]{1,0:T(8,128)(2,1)S(1)} %copy-done.20, ...), custom_call_target="tpu_custom_call" | custom-call | flops 1000000 | tf_op jit(solution)/shard_map/ff_weight/pallas_call | solution.py:452
  229.2 7.9 %ff_own.3 = (bf16[512,768]{1,0:T(8,128)(2,1)S(1)}, bf16[512,768]{1,0:T(8,128)(2,1)S(1)}, bf16[512,768]{1,0:T(8,128)(2,1)S(1)}, bf16[512,768]{1,0:T(8,128)(2,1)S(...) custom-call(s32[5]{0:T(128)S(1)} %pad_add_fusion.4.place, s32[2,4]{1,0:T(2,128)S(1)} %broadcast_subtract_fusion.limits, ...), custom_call_target="tpu_custom_call" | custom-call | flops 1000000 | tf_op jit(solution)/shard_map/ff_own/pallas_call | solution.py:85
  244.3 7.1 %ff_near.3 = (bf16[512,768]{1,0:T(8,128)(2,1)S(1)}, bf16[512,768]{1,0:T(8,128)(2,1)S(1)}, bf16[512,768]{1,0:T(8,128)(2,1)S(1)}, bf16[512,768]{1,0:T(8,128)(2,1)S(1)}) custom-call(s32[5]{0:T(128)S(1)} %pad_add_fusion.4.place, s32[2,4]{1,0:T(2,128)S(1)} %broadcast_subtract_fusion.limits, bf16[512,1536]{1,0:T(8,128)(2,1)S(1)} %copy-done.8, ...), custom_call_target="tpu_custom_call" | custom-call | flops 1000000 | tf_op jit(solution)/shard_map/ff_near/pallas_call | solution.py:85
  251.4 2.6 ff_back.4
  254.7 2.8 ff_back.5
  257.5 11.2 %collective-permute-done.47 = bf16[768,768]{1,0:T(8,128)(2,1)S(1)} collective-permute-done((bf16[768,768]{1,0:T(8,128)(2,1)S(1)}, bf16[768,768]{1,0:T(8,128)(2,1)S(1)}, u32[]{:S(2)}, u32[]{:S(2)}) %collective-permute-start.47) | collective-permute-done | bytes 1179680 | tf_op jit(solution)/shard_map/ppermute | solution.py:554
  273.6 14.8 %ff_weight.3 = (bf16[768,768]{1,0:T(8,128)(2,1)S(1)}, bf16[768,768]{1,0:T(8,128)(2,1)S(1)}, bf16[768,768]{1,0:T(8,128)(2,1)S(1)}, bf16[384,768]{1,0:T(8,128)(2,1)}, bf16[384,768]{1,0:T(8,128)(2,1)}) custom-call(s32[4]{0:T(128)S(1)} %get-tuple-element.723.place, bf16[512,1536]{1,0:T(8,128)(2,1)S(1)} %copy-done.18, bf16[512,1536]{1,0:T(8,128)(2,1)S(1)} %copy-done.20, ...), custom_call_target="tpu_custom_call" | custom-call | flops 1000000 | tf_op jit(solution)/shard_map/ff_weight/pallas_call | solution.py:452
  293.0 2.6 ff_back.6
  296.3 5.7 %collective-permute-done.52 = bf16[384,768]{1,0:T(8,128)(2,1)S(1)} collective-permute-done((bf16[384,768]{1,0:T(8,128)(2,1)}, bf16[384,768]{1,0:T(8,128)(2,1)S(1)}, u32[]{:S(2)}, u32[]{:S(2)}) %collective-permute-start.52) | collective-permute-done | bytes 589856 | tf_op jit(solution)/shard_map/ppermute | solution.py:554
  305.6 3.3 ff_back.7.own
  309.0 5.5 %second_back.1 = (f32[512,1536]{1,0:T(8,128)S(1)}, bf16[512,1536]{1,0:T(8,128)(2,1)S(1)}, f32[8,1536]{1,0:T(8,128)S(1)}) custom-call(f32[512,1536]{1,0:T(8,128)S(1)} %ff_back.7.own, bf16[256,1536]{1,0:T(8,128)(2,1)S(1)} %collective-permute-done.53.beside_a, bf16[256,1536]{1,0:T(8,128)(2,1)S(1)} %collective-permute-done.54.beside_b, ...), custom_call_target="tpu_custom_call" | custom-call | flops 1000000 | tf_op jit(solution)/shard_map/second_back/pallas_call | solution.py:85
  314.5 3.8 out_back.1
  319.0 2.6 ff_fore.4
  321.9 9.5 %attend_back.3 = (bf16[1024,768]{1,0:T(8,128)(2,1)S(1)}, bf16[384,768]{1,0:T(8,128)(2,1)S(1)}, bf16[384,768]{1,0:T(8,128)(2,1)}, bf16[384,768]{1,0:T(8,128)(2,1)...) custom-call(s32[5]{0:T(128)S(1)} %pad_add_fusion.4.place, bf16[1024,768]{1,0:T(8,128)(2,1)S(1)} %copy-done.96, ...), custom_call_target="tpu_custom_call" | custom-call | flops 1000000 | tf_op jit(solution)/shard_map/attend_back/pallas_call | solution.py:85
  336.6 3.0 ff_fore.5
  341.5 2.9 collective-permute-done.62
  359.4 9.0 %attend_back.4 = (bf16[1024,768]{1,0:T(8,128)(2,1)S(1)}, bf16[384,768]{1,0:T(8,128)(2,1)S(1)}, bf16[384,768]{1,0:T(8,128)(2,1)S(1)}, bf16[384,768]{1,0:T(8,128)(...) custom-call(s32[5]{0:T(128)S(1)} %pad_add_fusion.4.place, bf16[1024,768]{1,0:T(8,128)(2,1)S(1)} %copy-done.94, ...), custom_call_target="tpu_custom_call" | custom-call | flops 1000000 | tf_op jit(solution)/shard_map/attend_back/pallas_call | solution.py:85
  368.5 3.9 out_weight.1
  376.8 2.4 collective-permute-done.67
  383.7 9.3 %attend_back.5 = (bf16[1024,768]{1,0:T(8,128)(2,1)S(1)}, bf16[384,768]{1,0:T(8,128)(2,1)S(1)}, bf16[384,768]{1,0:T(8,128)(2,1)S(1)}, bf16[384,768]{1,0:T(8,128)(...) custom-call(s32[5]{0:T(128)S(1)} %pad_add_fusion.4.place, bf16[1024,768]{1,0:T(8,128)(2,1)S(1)} %copy-done.92, ...), custom_call_target="tpu_custom_call" | custom-call | flops 1000000 | tf_op jit(solution)/shard_map/attend_back/pallas_call | solution.py:85
  393.0 19.6 %collective-permute-done.68 = bf16[512,1536]{1,0:T(8,128)(2,1)} collective-permute-done((bf16[512,1536]{1,0:T(8,128)(2,1)}, bf16[512,1536]{1,0:T(8,128)(2,1)}, u32[]{:S(2)}, u32[]{:S(2)}) %collective-permute-start.68) | collective-permute-done | bytes 1572896 | tf_op jit(solution)/shard_map/ppermute | solution.py:554
  414.3 2.4 collective-permute-done.70
  422.5 2.1 collective-permute-done.73
  426.1 3.8 qkv_back.2
  434.2 2.2 collective-permute-start.82
  436.4 7.1 %collective-permute-done.77 = bf16[192,768]{1,0:T(8,128)(2,1)S(1)} collective-permute-done((bf16[192,768]{1,0:T(8,128)(2,1)S(1)}, bf16[192,768]{1,0:T(8,128)(2,1)S(1)}, u32[]{:S(2)}, u32[]{:S(2)}) %collective-permute-start.77) | collective-permute-done | bytes 294944 | tf_op jit(solution)/shard_map/ppermute | solution.py:554
  444.1 2.6 collective-permute-start.81
  447.7 3.1 collective-permute-start.83
  455.2 4.0 qkv_back.3.own
  463.1 1.9 collective-permute-start.89
  465.1 7.5 %collective-permute-done.85 = bf16[384,768]{1,0:T(8,128)(2,1)S(1)} collective-permute-done((bf16[384,768]{1,0:T(8,128)(2,1)S(1)}, bf16[384,768]{1,0:T(8,128)(2,1)S(1)}, u32[]{:S(2)}, u32[]{:S(2)}) %collective-permute-start.85) | collective-permute-done | bytes 589856 | tf_op jit(solution)/shard_map/ppermute | solution.py:554
  474.8 4.9 first_back.1
  481.3 4.5 collective-permute-done.90
  486.0 2.6 ff_fore.6
  488.8 2.2 collective-permute-start.92
  491.0 2.0 collective-permute-done.91
  493.1 10.9 %collective-permute-done.92 = bf16[192,768]{1,0:T(8,128)(2,1)S(1)} collective-permute-done((bf16[192,768]{1,0:T(8,128)(2,1)S(1)}, bf16[192,768]{1,0:T(8,128)(2,1)S(1)}, u32[]{:S(2)}, u32[]{:S(2)}) %collective-permute-start.92) | collective-permute-done | bytes 294944 | tf_op jit(solution)/shard_map/ppermute | solution.py:554
  504.8 2.5 collective-permute-start.97
  507.2 2.8 ff_fore.7
  510.1 2.3 collective-permute-done.97
  512.4 2.2 collective-permute-done.98
  515.4 2.6 place_qkv.1
  520.1 2.1 place_ff.1
  527.0 2.3 convert_add_fusion
  (559 shorter events, 177.4 us)
Async XLA Ops:
  4.1 19.6 %collective-permute-start.3 = (bf16[576,1536]{1,0:T(8,128)(2,1)}, bf16[576,1536]{1,0:T(8,128)(2,1)}, u32[]{:S(2)}, u32[]{:S(2)}) collective-permute-start(bf16[576,1536]{1,0:T(8,128)(2,1)} %pad_maximum_fusion), channel_id=1, source_target_pairs={{0,4},{1,5},{2,6},{3,7},{4,0},{5,1},{6,2},{7,3},{8,12},{9,13},{10,... | collective-permute-start | bytes 5308424 | tf_op jit(solution)/shard_map/ppermute | solution.py:554
  4.1 14.3 %collective-permute-start.2 = (bf16[512,1536]{1,0:T(8,128)(2,1)S(1)}, bf16[512,1536]{1,0:T(8,128)(2,1)}, u32[]{:S(2)}, u32[]{:S(2)}) collective-permute-start(bf16[512,1536]{1,0:T(8,128)(2,1)S(1)} %copy-done.21), channel_id=1, source_target_pairs={{0,4},{1,5},{2,6},{3,7},{4,0},{5,1},{6,2},{7,3},{8,12},{9,13},{10,... | collective-permute-start | bytes 4718600 | tf_op jit(solution)/shard_map/ppermute | solution.py:554
  12.6 39.2 %collective-permute-start.10 = (bf16[512,1536]{1,0:T(8,128)(2,1)}, bf16[512,1536]{1,0:T(8,128)(2,1)}, u32[]{:S(2)}, u32[]{:S(2)}) collective-permute-start(bf16[512,1536]{1,0:T(8,128)(2,1)} %cot.1), channel_id=1, source_target_pairs={{0,1},{1,0},{2,3},{3,2},{4,5},{5,4},{6,7},{7,6},{8,9},{9,8},{10,11... | collective-permute-start | bytes 4718600 | tf_op jit(solution)/shard_map/ppermute | solution.py:554
  15.4 16.2 %collective-permute-start.7 = (bf16[384,768]{1,0:T(8,128)(2,1)}, bf16[384,768]{1,0:T(8,128)(2,1)}, u32[]{:S(2)}, u32[]{:S(2)}) collective-permute-start(bf16[384,768]{1,0:T(8,128)(2,1)} %get-tuple-element.444.refs_0_), channel_id=1, source_target_pairs={{0,8},{1,9},{2,10},{3,11},{4,12},{5,13},{6,14},{7,15},{8,0},{9,1},... | collective-permute-start | bytes 1769480 | tf_op jit(solution)/shard_map/ppermute | solution.py:554
  16.9 16.5 %collective-permute-start.6 = (bf16[384,768]{1,0:T(8,128)(2,1)}, bf16[384,768]{1,0:T(8,128)(2,1)}, u32[]{:S(2)}, u32[]{:S(2)}) collective-permute-start(bf16[384,768]{1,0:T(8,128)(2,1)} %get-tuple-element.444.refs_0_), channel_id=1, source_target_pairs={{0,16},{1,17},{2,18},{3,19},{4,20},{5,21},{6,22},{7,23},{8,24},{9,... | collective-permute-start | bytes 1769480 | tf_op jit(solution)/shard_map/ppermute | solution.py:554
  28.0 16.6 %collective-permute-start.5 = (bf16[384,768]{1,0:T(8,128)(2,1)}, bf16[384,768]{1,0:T(8,128)(2,1)}, u32[]{:S(2)}, u32[]{:S(2)}) collective-permute-start(bf16[384,768]{1,0:T(8,128)(2,1)} %get-tuple-element.443.refs_0_), channel_id=1, source_target_pairs={{0,8},{1,9},{2,10},{3,11},{4,12},{5,13},{6,14},{7,15},{8,0},{9,1},... | collective-permute-start | bytes 1769480 | tf_op jit(solution)/shard_map/ppermute | solution.py:554
  28.5 17.5 %collective-permute-start.4 = (bf16[384,768]{1,0:T(8,128)(2,1)}, bf16[384,768]{1,0:T(8,128)(2,1)}, u32[]{:S(2)}, u32[]{:S(2)}) collective-permute-start(bf16[384,768]{1,0:T(8,128)(2,1)} %get-tuple-element.443.refs_0_), channel_id=1, source_target_pairs={{0,16},{1,17},{2,18},{3,19},{4,20},{5,21},{6,22},{7,23},{8,24},{9,... | collective-permute-start | bytes 1769480 | tf_op jit(solution)/shard_map/ppermute | solution.py:554
  35.4 14.5 %collective-permute-start.9 = (bf16[192,768]{1,0:T(8,128)(2,1)S(1)}, bf16[192,768]{1,0:T(8,128)(2,1)S(1)}, u32[]{:S(2)}, u32[]{:S(2)}) collective-permute-start(bf16[192,768]{1,0:T(8,128)(2,1)S(1)} %slice.355), channel_id=1, source_target_pairs={{0,8},{1,9},{2,10},{3,11},{4,12},{5,13},{6,14},{7,15},{8,0},{9,1},... | collective-permute-start | bytes 884744 | tf_op jit(solution)/shard_map/ppermute | solution.py:554
  35.5 15.6 %collective-permute-start.8 = (bf16[192,768]{1,0:T(8,128)(2,1)S(1)}, bf16[192,768]{1,0:T(8,128)(2,1)S(1)}, u32[]{:S(2)}, u32[]{:S(2)}) collective-permute-start(bf16[192,768]{1,0:T(8,128)(2,1)S(1)} %slice.354), channel_id=1, source_target_pairs={{0,16},{1,17},{2,18},{3,19},{4,20},{5,21},{6,22},{7,23},{8,24},{9,... | collective-permute-start | bytes 884744 | tf_op jit(solution)/shard_map/ppermute | solution.py:554
  51.8 23.3 %collective-permute-start.12 = (bf16[384,768]{1,0:T(8,128)(2,1)}, bf16[384,768]{1,0:T(8,128)(2,1)}, u32[]{:S(2)}, u32[]{:S(2)}) collective-permute-start(bf16[384,768]{1,0:T(8,128)(2,1)} %get-tuple-element.453.refs_0_), channel_id=1, source_target_pairs={{0,8},{1,9},{2,10},{3,11},{4,12},{5,13},{6,14},{7,15},{8,0},{9,1},... | collective-permute-start | bytes 1769480 | tf_op jit(solution)/shard_map/ppermute | solution.py:554
  52.8 22.3 %collective-permute-start.11 = (bf16[384,768]{1,0:T(8,128)(2,1)}, bf16[384,768]{1,0:T(8,128)(2,1)}, u32[]{:S(2)}, u32[]{:S(2)}) collective-permute-start(bf16[384,768]{1,0:T(8,128)(2,1)} %get-tuple-element.453.refs_0_), channel_id=1, source_target_pairs={{0,16},{1,17},{2,18},{3,19},{4,20},{5,21},{6,22},{7,23},{8,24},{9,... | collective-permute-start | bytes 1769480 | tf_op jit(solution)/shard_map/ppermute | solution.py:554
  54.3 20.8 %collective-permute-start.14 = (bf16[192,768]{1,0:T(8,128)(2,1)}, bf16[192,768]{1,0:T(8,128)(2,1)}, u32[]{:S(2)}, u32[]{:S(2)}) collective-permute-start(bf16[192,768]{1,0:T(8,128)(2,1)} %slice.359), channel_id=1, source_target_pairs={{0,8},{1,9},{2,10},{3,11},{4,12},{5,13},{6,14},{7,15},{8,0},{9,1},... | collective-permute-start | bytes 884744 | tf_op jit(solution)/shard_map/ppermute | solution.py:554
  55.4 19.7 %collective-permute-start.13 = (bf16[192,768]{1,0:T(8,128)(2,1)}, bf16[192,768]{1,0:T(8,128)(2,1)}, u32[]{:S(2)}, u32[]{:S(2)}) collective-permute-start(bf16[192,768]{1,0:T(8,128)(2,1)} %slice.358), channel_id=1, source_target_pairs={{0,16},{1,17},{2,18},{3,19},{4,20},{5,21},{6,22},{7,23},{8,24},{9,... | collective-permute-start | bytes 884744 | tf_op jit(solution)/shard_map/ppermute | solution.py:554
  56.9 55.7 %collective-permute-start.25 = (bf16[768,768]{1,0:T(8,128)(2,1)}, bf16[768,768]{1,0:T(8,128)(2,1)S(1)}, u32[]{:S(2)}, u32[]{:S(2)}) collective-permute-start(bf16[768,768]{1,0:T(8,128)(2,1)} %copy-done.99), channel_id=1, source_target_pairs={{0,2},{1,3},{2,0},{3,1},{4,6},{5,7},{6,4},{7,5},{8,10},{9,11},{10,... | collective-permute-start | bytes 3538952 | tf_op jit(solution)/shard_map/ppermute | solution.py:554
  77.3 20.8 %collective-permute-start.16 = (bf16[384,768]{1,0:T(8,128)(2,1)S(1)}, bf16[384,768]{1,0:T(8,128)(2,1)S(1)}, u32[]{:S(2)}, u32[]{:S(2)}) collective-permute-start(bf16[384,768]{1,0:T(8,128)(2,1)S(1)} %copy-done.110), channel_id=1, source_target_pairs={{0,8},{1,9},{2,10},{3,11},{4,12},{5,13},{6,14},{7,15},{8,0},{9,1},... | collective-permute-start | bytes 1769480 | tf_op jit(solution)/shard_map/ppermute | solution.py:554
  78.3 19.7 %collective-permute-start.15 = (bf16[384,768]{1,0:T(8,128)(2,1)S(1)}, bf16[384,768]{1,0:T(8,128)(2,1)S(1)}, u32[]{:S(2)}, u32[]{:S(2)}) collective-permute-start(bf16[384,768]{1,0:T(8,128)(2,1)S(1)} %copy-done.110), channel_id=1, source_target_pairs={{0,16},{1,17},{2,18},{3,19},{4,20},{5,21},{6,22},{7,23},{8,24},{9,... | collective-permute-start | bytes 1769480 | tf_op jit(solution)/shard_map/ppermute | solution.py:554
  79.9 16.7 %collective-permute-start.18 = (bf16[192,768]{1,0:T(8,128)(2,1)S(1)}, bf16[192,768]{1,0:T(8,128)(2,1)S(1)}, u32[]{:S(2)}, u32[]{:S(2)}) collective-permute-start(bf16[192,768]{1,0:T(8,128)(2,1)S(1)} %slice.363), channel_id=1, source_target_pairs={{0,8},{1,9},{2,10},{3,11},{4,12},{5,13},{6,14},{7,15},{8,0},{9,1},... | collective-permute-start | bytes 884744 | tf_op jit(solution)/shard_map/ppermute | solution.py:554
  80.9 16.7 %collective-permute-start.17 = (bf16[192,768]{1,0:T(8,128)(2,1)S(1)}, bf16[192,768]{1,0:T(8,128)(2,1)S(1)}, u32[]{:S(2)}, u32[]{:S(2)}) collective-permute-start(bf16[192,768]{1,0:T(8,128)(2,1)S(1)} %slice.362), channel_id=1, source_target_pairs={{0,16},{1,17},{2,18},{3,19},{4,20},{5,21},{6,22},{7,23},{8,24},{9,... | collective-permute-start | bytes 884744 | tf_op jit(solution)/shard_map/ppermute | solution.py:554
  99.5 13.2 %collective-permute-start.23 = (bf16[384,768]{1,0:T(8,128)(2,1)S(1)}, bf16[384,768]{1,0:T(8,128)(2,1)S(1)}, u32[]{:S(2)}, u32[]{:S(2)}) collective-permute-start(bf16[384,768]{1,0:T(8,128)(2,1)S(1)} %collective-permute-done.16.refs_1_), channel_id=1, source_target_pairs={{0,4},{1,5},{2,6},{3,7},{4,0},{5,1},{6,2},{7,3},{8,12},{9,13},{10,... | collective-permute-start | bytes 1769480 | tf_op jit(solution)/shard_map/ppermute | solution.py:554
  99.6 13.1 %collective-permute-start.24 = (bf16[384,768]{1,0:T(8,128)(2,1)S(1)}, bf16[384,768]{1,0:T(8,128)(2,1)S(1)}, u32[]{:S(2)}, u32[]{:S(2)}) collective-permute-start(bf16[384,768]{1,0:T(8,128)(2,1)S(1)} %collective-permute-done.15.refs_2_), channel_id=1, source_target_pairs={{0,4},{1,5},{2,6},{3,7},{4,0},{5,1},{6,2},{7,3},{8,12},{9,13},{10,... | collective-permute-start | bytes 1769480 | tf_op jit(solution)/shard_map/ppermute | solution.py:554
  116.7 28.3 %collective-permute-start.32 = (bf16[768,768]{1,0:T(8,128)(2,1)S(1)}, bf16[768,768]{1,0:T(8,128)(2,1)S(1)}, u32[]{:S(2)}, u32[]{:S(2)}) collective-permute-start(bf16[768,768]{1,0:T(8,128)(2,1)S(1)} %copy-done.100), channel_id=1, source_target_pairs={{0,8},{1,9},{2,10},{3,11},{4,12},{5,13},{6,14},{7,15},{8,0},{9,1},... | collective-permute-start | bytes 3538952 | tf_op jit(solution)/shard_map/ppermute | solution.py:554
  118.1 28.0 %collective-permute-start.31 = (bf16[768,768]{1,0:T(8,128)(2,1)S(1)}, bf16[768,768]{1,0:T(8,128)(2,1)S(1)}, u32[]{:S(2)}, u32[]{:S(2)}) collective-permute-start(bf16[768,768]{1,0:T(8,128)(2,1)S(1)} %copy-done.100), channel_id=1, source_target_pairs={{0,16},{1,17},{2,18},{3,19},{4,20},{5,21},{6,22},{7,23},{8,24},{9,... | collective-permute-start | bytes 3538952 | tf_op jit(solution)/shard_map/ppermute | solution.py:554
  127.5 33.6 %collective-permute-start.35 = (bf16[512,1536]{1,0:T(8,128)(2,1)S(1)}, bf16[512,1536]{1,0:T(8,128)(2,1)S(1)}, u32[]{:S(2)}, u32[]{:S(2)}) collective-permute-start(bf16[512,1536]{1,0:T(8,128)(2,1)S(1)} %get-tuple-element.551.refs_0_), channel_id=1, source_target_pairs={{0,4},{1,5},{2,6},{3,7},{4,0},{5,1},{6,2},{7,3},{8,12},{9,13},{10,... | collective-permute-start | bytes 4718600 | tf_op jit(solution)/shard_map/ppermute | solution.py:554
  127.5 41.8 %collective-permute-start.30 = (bf16[512,1536]{1,0:T(8,128)(2,1)S(1)}, bf16[512,1536]{1,0:T(8,128)(2,1)S(1)}, u32[]{:S(2)}, u32[]{:S(2)}) collective-permute-start(bf16[512,1536]{1,0:T(8,128)(2,1)S(1)} %get-tuple-element.551.refs_0_), channel_id=1, source_target_pairs={{0,1},{1,0},{2,3},{3,2},{4,5},{5,4},{6,7},{7,6},{8,9},{9,8},{10,11... | collective-permute-start | bytes 4718600 | tf_op jit(solution)/shard_map/ppermute | solution.py:554
  146.1 14.5 %collective-permute-start.34 = (bf16[384,768]{1,0:T(8,128)(2,1)S(1)}, bf16[384,768]{1,0:T(8,128)(2,1)S(1)}, u32[]{:S(2)}, u32[]{:S(2)}) collective-permute-start(bf16[384,768]{1,0:T(8,128)(2,1)S(1)} %slice.373), channel_id=1, source_target_pairs={{0,8},{1,9},{2,10},{3,11},{4,12},{5,13},{6,14},{7,15},{8,0},{9,1},... | collective-permute-start | bytes 1769480 | tf_op jit(solution)/shard_map/ppermute | solution.py:554
  146.9 14.2 %collective-permute-start.33 = (bf16[384,768]{1,0:T(8,128)(2,1)S(1)}, bf16[384,768]{1,0:T(8,128)(2,1)S(1)}, u32[]{:S(2)}, u32[]{:S(2)}) collective-permute-start(bf16[384,768]{1,0:T(8,128)(2,1)S(1)} %slice.372), channel_id=1, source_target_pairs={{0,16},{1,17},{2,18},{3,19},{4,20},{5,21},{6,22},{7,23},{8,24},{9,... | collective-permute-start | bytes 1769480 | tf_op jit(solution)/shard_map/ppermute | solution.py:554
  170.1 28.0 %collective-permute-start.39 = (bf16[768,768]{1,0:T(8,128)(2,1)S(1)}, bf16[768,768]{1,0:T(8,128)(2,1)S(1)}, u32[]{:S(2)}, u32[]{:S(2)}) collective-permute-start(bf16[768,768]{1,0:T(8,128)(2,1)S(1)} %collective-permute-done.25.refs_4_), channel_id=1, source_target_pairs={{0,8},{1,9},{2,10},{3,11},{4,12},{5,13},{6,14},{7,15},{8,0},{9,1},... | collective-permute-start | bytes 3538952 | tf_op jit(solution)/shard_map/ppermute | solution.py:554
  171.4 27.7 %collective-permute-start.38 = (bf16[768,768]{1,0:T(8,128)(2,1)S(1)}, bf16[768,768]{1,0:T(8,128)(2,1)S(1)}, u32[]{:S(2)}, u32[]{:S(2)}) collective-permute-start(bf16[768,768]{1,0:T(8,128)(2,1)S(1)} %collective-permute-done.25.refs_4_), channel_id=1, source_target_pairs={{0,16},{1,17},{2,18},{3,19},{4,20},{5,21},{6,22},{7,23},{8,24},{9,... | collective-permute-start | bytes 3538952 | tf_op jit(solution)/shard_map/ppermute | solution.py:554
  202.1 15.8 %collective-permute-start.40 = (bf16[512,256]{1,0:T(8,128)(2,1)}, bf16[512,256]{1,0:T(8,128)(2,1)S(1)}, u32[]{:S(2)}, u32[]{:S(2)}) collective-permute-start(bf16[512,256]{1,0:T(8,128)(2,1)} %get-tuple-element.522.refs_0_), channel_id=1, source_target_pairs={{0,4},{1,5},{2,6},{3,7},{4,0},{5,1},{6,2},{7,3},{8,12},{9,13},{10,... | collective-permute-start | bytes 786440 | tf_op jit(solution)/shard_map/ppermute | solution.py:554
  202.1 16.5 %collective-permute-start.41 = (bf16[512,256]{1,0:T(8,128)(2,1)}, bf16[512,256]{1,0:T(8,128)(2,1)}, u32[]{:S(2)}, u32[]{:S(2)}) collective-permute-start(bf16[512,256]{1,0:T(8,128)(2,1)} %get-tuple-element.523.refs_1_), channel_id=1, source_target_pairs={{0,4},{1,5},{2,6},{3,7},{4,0},{5,1},{6,2},{7,3},{8,12},{9,13},{10,... | collective-permute-start | bytes 786440 | tf_op jit(solution)/shard_map/ppermute | solution.py:554
  202.6 16.0 %collective-permute-start.42 = (bf16[512,256]{1,0:T(8,128)(2,1)}, bf16[512,256]{1,0:T(8,128)(2,1)}, u32[]{:S(2)}, u32[]{:S(2)}) collective-permute-start(bf16[512,256]{1,0:T(8,128)(2,1)} %get-tuple-element.524.refs_2_), channel_id=1, source_target_pairs={{0,4},{1,5},{2,6},{3,7},{4,0},{5,1},{6,2},{7,3},{8,12},{9,13},{10,... | collective-permute-start | bytes 786440 | tf_op jit(solution)/shard_map/ppermute | solution.py:554
  202.6 18.8 %collective-permute-start.44 = (bf16[384,768]{1,0:T(8,128)(2,1)}, bf16[384,768]{1,0:T(8,128)(2,1)S(1)}, u32[]{:S(2)}, u32[]{:S(2)}) collective-permute-start(bf16[384,768]{1,0:T(8,128)(2,1)} %slice.377), channel_id=1, source_target_pairs={{0,8},{1,9},{2,10},{3,11},{4,12},{5,13},{6,14},{7,15},{8,0},{9,1},... | collective-permute-start | bytes 1769480 | tf_op jit(solution)/shard_map/ppermute | solution.py:554
  203.4 19.0 %collective-permute-start.43 = (bf16[384,768]{1,0:T(8,128)(2,1)}, bf16[384,768]{1,0:T(8,128)(2,1)S(1)}, u32[]{:S(2)}, u32[]{:S(2)}) collective-permute-start(bf16[384,768]{1,0:T(8,128)(2,1)} %slice.376), channel_id=1, source_target_pairs={{0,16},{1,17},{2,18},{3,19},{4,20},{5,21},{6,22},{7,23},{8,24},{9,... | collective-permute-start | bytes 1769480 | tf_op jit(solution)/shard_map/ppermute | solution.py:554
  218.6 22.1 %collective-permute-start.46 = (bf16[384,768]{1,0:T(8,128)(2,1)S(1)}, bf16[384,768]{1,0:T(8,128)(2,1)S(1)}, u32[]{:S(2)}, u32[]{:S(2)}) collective-permute-start(bf16[384,768]{1,0:T(8,128)(2,1)S(1)} %get-tuple-element.532), channel_id=1, source_target_pairs={{0,16},{1,17},{2,18},{3,19},{4,20},{5,21},{6,22},{7,23},{8,24},{9,... | collective-permute-start | bytes 1769480 | tf_op jit(solution)/shard_map/ppermute | solution.py:554
  220.2 20.6 %collective-permute-start.45 = (bf16[384,768]{1,0:T(8,128)(2,1)S(1)}, bf16[384,768]{1,0:T(8,128)(2,1)S(1)}, u32[]{:S(2)}, u32[]{:S(2)}) collective-permute-start(bf16[384,768]{1,0:T(8,128)(2,1)S(1)} %get-tuple-element.530), channel_id=1, source_target_pairs={{0,8},{1,9},{2,10},{3,11},{4,12},{5,13},{6,14},{7,15},{8,0},{9,1},... | collective-permute-start | bytes 1769480 | tf_op jit(solution)/shard_map/ppermute | solution.py:554
  241.3 27.3 %collective-permute-start.47 = (bf16[768,768]{1,0:T(8,128)(2,1)S(1)}, bf16[768,768]{1,0:T(8,128)(2,1)S(1)}, u32[]{:S(2)}, u32[]{:S(2)}) collective-permute-start(bf16[768,768]{1,0:T(8,128)(2,1)S(1)} %fusion.5), channel_id=1, source_target_pairs={{0,8},{1,9},{2,10},{3,11},{4,12},{5,13},{6,14},{7,15},{8,0},{9,1},... | collective-permute-start | bytes 3538952 | tf_op jit(solution)/shard_map/ppermute | solution.py:554
  242.1 27.0 %collective-permute-start.48 = (bf16[768,768]{1,0:T(8,128)(2,1)S(1)}, bf16[768,768]{1,0:T(8,128)(2,1)S(1)}, u32[]{:S(2)}, u32[]{:S(2)}) collective-permute-start(bf16[768,768]{1,0:T(8,128)(2,1)S(1)} %fusion.4), channel_id=1, source_target_pairs={{0,16},{1,17},{2,18},{3,19},{4,20},{5,21},{6,22},{7,23},{8,24},{9,... | collective-permute-start | bytes 3538952 | tf_op jit(solution)/shard_map/ppermute | solution.py:554
  254.1 16.5 %collective-permute-start.49 = (bf16[256,1536]{1,0:T(8,128)(2,1)S(1)}, bf16[256,1536]{1,0:T(8,128)(2,1)S(1)}, u32[]{:S(2)}, u32[]{:S(2)}) collective-permute-start(bf16[256,1536]{1,0:T(8,128)(2,1)S(1)} %get-tuple-element.548), channel_id=1, source_target_pairs={{0,4},{1,5},{2,6},{3,7},{4,0},{5,1},{6,2},{7,3},{8,12},{9,13},{10,... | collective-permute-start | bytes 2359304 | tf_op jit(solution)/shard_map/ppermute | solution.py:554
  254.2 16.4 %collective-permute-start.50 = (bf16[256,1536]{1,0:T(8,128)(2,1)S(1)}, bf16[256,1536]{1,0:T(8,128)(2,1)S(1)}, u32[]{:S(2)}, u32[]{:S(2)}) collective-permute-start(bf16[256,1536]{1,0:T(8,128)(2,1)S(1)} %get-tuple-element.550), channel_id=1, source_target_pairs={{0,4},{1,5},{2,6},{3,7},{4,0},{5,1},{6,2},{7,3},{8,12},{9,13},{10,... | collective-permute-start | bytes 2359304 | tf_op jit(solution)/shard_map/ppermute | solution.py:554
  272.3 36.6 %collective-permute-start.55 = (bf16[512,1536]{1,0:T(8,128)(2,1)}, bf16[512,1536]{1,0:T(8,128)(2,1)}, u32[]{:S(2)}, u32[]{:S(2)}) collective-permute-start(bf16[512,1536]{1,0:T(8,128)(2,1)} %pad_maximum_fusion.1), channel_id=1, source_target_pairs={{0,1},{1,0},{2,3},{3,2},{4,5},{5,4},{6,7},{7,6},{8,9},{9,8},{10,11... | collective-permute-start | bytes 4718600 | tf_op jit(solution)/shard_map/ppermute | solution.py:554
  288.3 13.6 %collective-permute-start.52 = (bf16[384,768]{1,0:T(8,128)(2,1)}, bf16[384,768]{1,0:T(8,128)(2,1)S(1)}, u32[]{:S(2)}, u32[]{:S(2)}) collective-permute-start(bf16[384,768]{1,0:T(8,128)(2,1)} %get-tuple-element.564), channel_id=1, source_target_pairs={{0,16},{1,17},{2,18},{3,19},{4,20},{5,21},{6,22},{7,23},{8,24},{9,... | collective-permute-start | bytes 1769480 | tf_op jit(solution)/shard_map/ppermute | solution.py:554
  288.8 13.3 %collective-permute-start.51 = (bf16[384,768]{1,0:T(8,128)(2,1)}, bf16[384,768]{1,0:T(8,128)(2,1)S(1)}, u32[]{:S(2)}, u32[]{:S(2)}) collective-permute-start(bf16[384,768]{1,0:T(8,128)(2,1)} %get-tuple-element.562), channel_id=1, source_target_pairs={{0,8},{1,9},{2,10},{3,11},{4,12},{5,13},{6,14},{7,15},{8,0},{9,1},... | collective-permute-start | bytes 1769480 | tf_op jit(solution)/shard_map/ppermute | solution.py:554
  295.7 13.2 %collective-permute-start.53 = (bf16[256,1536]{1,0:T(8,128)(2,1)S(1)}, bf16[256,1536]{1,0:T(8,128)(2,1)S(1)}, u32[]{:S(2)}, u32[]{:S(2)}) collective-permute-start(bf16[256,1536]{1,0:T(8,128)(2,1)S(1)} %get-tuple-element.568), channel_id=1, source_target_pairs={{0,4},{1,5},{2,6},{3,7},{4,0},{5,1},{6,2},{7,3},{8,12},{9,13},{10,... | collective-permute-start | bytes 2359304 | tf_op jit(solution)/shard_map/ppermute | solution.py:554
  295.8 13.1 %collective-permute-start.54 = (bf16[256,1536]{1,0:T(8,128)(2,1)S(1)}, bf16[256,1536]{1,0:T(8,128)(2,1)S(1)}, u32[]{:S(2)}, u32[]{:S(2)}) collective-permute-start(bf16[256,1536]{1,0:T(8,128)(2,1)S(1)} %get-tuple-element.570), channel_id=1, source_target_pairs={{0,4},{1,5},{2,6},{3,7},{4,0},{5,1},{6,2},{7,3},{8,12},{9,13},{10,... | collective-permute-start | bytes 2359304 | tf_op jit(solution)/shard_map/ppermute | solution.py:554
  302.7 30.7 %collective-permute-start.58 = (bf16[768,768]{1,0:T(8,128)(2,1)S(1)}, bf16[768,768]{1,0:T(8,128)(2,1)S(1)}, u32[]{:S(2)}, u32[]{:S(2)}) collective-permute-start(bf16[768,768]{1,0:T(8,128)(2,1)S(1)} %fusion.7), channel_id=1, source_target_pairs={{0,8},{1,9},{2,10},{3,11},{4,12},{5,13},{6,14},{7,15},{8,0},{9,1},... | collective-permute-start | bytes 3538952 | tf_op jit(solution)/shard_map/ppermute | solution.py:554
  304.1 29.3 %collective-permute-start.59 = (bf16[768,768]{1,0:T(8,128)(2,1)S(1)}, bf16[768,768]{1,0:T(8,128)(2,1)S(1)}, u32[]{:S(2)}, u32[]{:S(2)}) collective-permute-start(bf16[768,768]{1,0:T(8,128)(2,1)S(1)} %fusion.6), channel_id=1, source_target_pairs={{0,16},{1,17},{2,18},{3,19},{4,20},{5,21},{6,22},{7,23},{8,24},{9,... | collective-permute-start | bytes 3538952 | tf_op jit(solution)/shard_map/ppermute | solution.py:554
  348.4 25.5 %collective-permute-start.64 = (bf16[384,768]{1,0:T(8,128)(2,1)}, bf16[384,768]{1,0:T(8,128)(2,1)}, u32[]{:S(2)}, u32[]{:S(2)}) collective-permute-start(bf16[384,768]{1,0:T(8,128)(2,1)} %fusion.9), channel_id=1, source_target_pairs={{0,8},{1,9},{2,10},{3,11},{4,12},{5,13},{6,14},{7,15},{8,0},{9,1},... | collective-permute-start | bytes 1769480 | tf_op jit(solution)/shard_map/ppermute | solution.py:554
  349.7 25.6 %collective-permute-start.65 = (bf16[384,768]{1,0:T(8,128)(2,1)}, bf16[384,768]{1,0:T(8,128)(2,1)}, u32[]{:S(2)}, u32[]{:S(2)}) collective-permute-start(bf16[384,768]{1,0:T(8,128)(2,1)} %fusion.8), channel_id=1, source_target_pairs={{0,16},{1,17},{2,18},{3,19},{4,20},{5,21},{6,22},{7,23},{8,24},{9,... | collective-permute-start | bytes 1769480 | tf_op jit(solution)/shard_map/ppermute | solution.py:554
  350.2 62.4 %collective-permute-start.68 = (bf16[512,1536]{1,0:T(8,128)(2,1)}, bf16[512,1536]{1,0:T(8,128)(2,1)}, u32[]{:S(2)}, u32[]{:S(2)}) collective-permute-start(bf16[512,1536]{1,0:T(8,128)(2,1)} %pad_maximum_fusion.2), channel_id=1, source_target_pairs={{0,1},{1,0},{2,3},{3,2},{4,5},{5,4},{6,7},{7,6},{8,9},{9,8},{10,11... | collective-permute-start | bytes 4718600 | tf_op jit(solution)/shard_map/ppermute | solution.py:554
  351.5 61.1 %collective-permute-start.69 = (bf16[768,768]{1,0:T(8,128)(2,1)}, bf16[768,768]{1,0:T(8,128)(2,1)}, u32[]{:S(2)}, u32[]{:S(2)}) collective-permute-start(bf16[768,768]{1,0:T(8,128)(2,1)} %add_convert_fusion.1), channel_id=1, source_target_pairs={{0,2},{1,3},{2,0},{3,1},{4,6},{5,7},{6,4},{7,5},{8,10},{9,11},{10,... | collective-permute-start | bytes 3538952 | tf_op jit(solution)/shard_map/ppermute | solution.py:554
  381.0 39.7 %collective-permute-start.71 = (bf16[384,768]{1,0:T(8,128)(2,1)S(1)}, bf16[384,768]{1,0:T(8,128)(2,1)S(1)}, u32[]{:S(2)}, u32[]{:S(2)}) collective-permute-start(bf16[384,768]{1,0:T(8,128)(2,1)S(1)} %fusion.11), channel_id=1, source_target_pairs={{0,8},{1,9},{2,10},{3,11},{4,12},{5,13},{6,14},{7,15},{8,0},{9,1},... | collective-permute-start | bytes 1769480 | tf_op jit(solution)/shard_map/ppermute | solution.py:554
  382.5 38.2 %collective-permute-start.72 = (bf16[384,768]{1,0:T(8,128)(2,1)S(1)}, bf16[384,768]{1,0:T(8,128)(2,1)S(1)}, u32[]{:S(2)}, u32[]{:S(2)}) collective-permute-start(bf16[384,768]{1,0:T(8,128)(2,1)S(1)} %fusion.10), channel_id=1, source_target_pairs={{0,16},{1,17},{2,18},{3,19},{4,20},{5,21},{6,22},{7,23},{8,24},{9,... | collective-permute-start | bytes 1769480 | tf_op jit(solution)/shard_map/ppermute | solution.py:554
  383.0 33.7 %collective-permute-start.70 = (bf16[192,768]{1,0:T(8,128)(2,1)S(1)}, bf16[192,768]{1,0:T(8,128)(2,1)S(1)}, u32[]{:S(2)}, u32[]{:S(2)}) collective-permute-start(bf16[192,768]{1,0:T(8,128)(2,1)S(1)} %constant_dynamic-slice_fusion.6), channel_id=1, source_target_pairs={{0,1},{1,0},{2,3},{3,2},{4,5},{5,4},{6,7},{7,6},{8,9},{9,8},{10,11... | collective-permute-start | bytes 884744 | tf_op jit(solution)/shard_map/ppermute | solution.py:554
  416.8 14.3 %collective-permute-start.75 = (bf16[192,768]{1,0:T(8,128)(2,1)S(1)}, bf16[192,768]{1,0:T(8,128)(2,1)S(1)}, u32[]{:S(2)}, u32[]{:S(2)}) collective-permute-start(bf16[192,768]{1,0:T(8,128)(2,1)S(1)} %add_convert_fusion.24), channel_id=1, source_target_pairs={{0,2},{1,3},{2,0},{3,1},{4,6},{5,7},{6,4},{7,5},{8,10},{9,11},{10,... | collective-permute-start | bytes 884744 | tf_op jit(solution)/shard_map/ppermute | solution.py:554
  421.0 13.2 %collective-permute-start.76 = (bf16[192,768]{1,0:T(8,128)(2,1)S(1)}, bf16[192,768]{1,0:T(8,128)(2,1)S(1)}, u32[]{:S(2)}, u32[]{:S(2)}) collective-permute-start(bf16[192,768]{1,0:T(8,128)(2,1)S(1)} %constant_dynamic-slice_fusion.4), channel_id=1, source_target_pairs={{0,1},{1,0},{2,3},{3,2},{4,5},{5,4},{6,7},{7,6},{8,9},{9,8},{10,11... | collective-permute-start | bytes 884744 | tf_op jit(solution)/shard_map/ppermute | solution.py:554
  432.0 15.4 %collective-permute-start.78 = (bf16[384,768]{1,0:T(8,128)(2,1)S(1)}, bf16[384,768]{1,0:T(8,128)(2,1)S(1)}, u32[]{:S(2)}, u32[]{:S(2)}) collective-permute-start(bf16[384,768]{1,0:T(8,128)(2,1)S(1)} %fusion.13), channel_id=1, source_target_pairs={{0,8},{1,9},{2,10},{3,11},{4,12},{5,13},{6,14},{7,15},{8,0},{9,1},... | collective-permute-start | bytes 1769480 | tf_op jit(solution)/shard_map/ppermute | solution.py:554
  432.7 14.7 %collective-permute-start.79 = (bf16[384,768]{1,0:T(8,128)(2,1)S(1)}, bf16[384,768]{1,0:T(8,128)(2,1)S(1)}, u32[]{:S(2)}, u32[]{:S(2)}) collective-permute-start(bf16[384,768]{1,0:T(8,128)(2,1)S(1)} %fusion.12), channel_id=1, source_target_pairs={{0,16},{1,17},{2,18},{3,19},{4,20},{5,21},{6,22},{7,23},{8,24},{9,... | collective-permute-start | bytes 1769480 | tf_op jit(solution)/shard_map/ppermute | solution.py:554
  434.2 19.0 %collective-permute-start.82 = (bf16[192,768]{1,0:T(8,128)(2,1)S(1)}, bf16[192,768]{1,0:T(8,128)(2,1)S(1)}, u32[]{:S(2)}, u32[]{:S(2)}) collective-permute-start(bf16[192,768]{1,0:T(8,128)(2,1)S(1)} %add_convert_fusion.20), channel_id=1, source_target_pairs={{0,2},{1,3},{2,0},{3,1},{4,6},{5,7},{6,4},{7,5},{8,10},{9,11},{10,... | collective-permute-start | bytes 884744 | tf_op jit(solution)/shard_map/ppermute | solution.py:554
  447.7 14.7 %collective-permute-start.83 = (bf16[192,768]{1,0:T(8,128)(2,1)S(1)}, bf16[192,768]{1,0:T(8,128)(2,1)S(1)}, u32[]{:S(2)}, u32[]{:S(2)}) collective-permute-start(bf16[192,768]{1,0:T(8,128)(2,1)S(1)} %constant_dynamic-slice_fusion.3), channel_id=1, source_target_pairs={{0,1},{1,0},{2,3},{3,2},{4,5},{5,4},{6,7},{7,6},{8,9},{9,8},{10,11... | collective-permute-start | bytes 884744 | tf_op jit(solution)/shard_map/ppermute | solution.py:554
  459.2 13.4 %collective-permute-start.85 = (bf16[384,768]{1,0:T(8,128)(2,1)S(1)}, bf16[384,768]{1,0:T(8,128)(2,1)S(1)}, u32[]{:S(2)}, u32[]{:S(2)}) collective-permute-start(bf16[384,768]{1,0:T(8,128)(2,1)S(1)} %fusion.15), channel_id=1, source_target_pairs={{0,8},{1,9},{2,10},{3,11},{4,12},{5,13},{6,14},{7,15},{8,0},{9,1},... | collective-permute-start | bytes 1769480 | tf_op jit(solution)/shard_map/ppermute | solution.py:554
  463.1 16.5 %collective-permute-start.89 = (bf16[192,768]{1,0:T(8,128)(2,1)S(1)}, bf16[192,768]{1,0:T(8,128)(2,1)S(1)}, u32[]{:S(2)}, u32[]{:S(2)}) collective-permute-start(bf16[192,768]{1,0:T(8,128)(2,1)S(1)} %add_convert_fusion.16), channel_id=1, source_target_pairs={{0,2},{1,3},{2,0},{3,1},{4,6},{5,7},{6,4},{7,5},{8,10},{9,11},{10,... | collective-permute-start | bytes 884744 | tf_op jit(solution)/shard_map/ppermute | solution.py:554
  479.8 13.3 %collective-permute-start.91 = (bf16[192,768]{1,0:T(8,128)(2,1)S(1)}, bf16[192,768]{1,0:T(8,128)(2,1)S(1)}, u32[]{:S(2)}, u32[]{:S(2)}) collective-permute-start(bf16[192,768]{1,0:T(8,128)(2,1)S(1)} %add_convert_fusion.15), channel_id=1, source_target_pairs={{0,1},{1,0},{2,3},{3,2},{4,5},{5,4},{6,7},{7,6},{8,9},{9,8},{10,11... | collective-permute-start | bytes 884744 | tf_op jit(solution)/shard_map/ppermute | solution.py:554
  488.7 15.4 %collective-permute-start.93 = (f32[4,1536]{1,0:T(4,128)S(1)}, f32[4,1536]{1,0:T(4,128)S(1)}, u32[]{:S(2)}, u32[]{:S(2)}) collective-permute-start(f32[4,1536]{1,0:T(4,128)S(1)} %pad_maximum_fusion.8), channel_id=1, source_target_pairs={{0,1},{1,0},{2,3},{3,2},{4,5},{5,4},{6,7},{7,6},{8,9},{9,8},{10,11... | collective-permute-start | bytes 73736 | tf_op jit(solution)/shard_map/ppermute | solution.py:554
  488.8 15.2 %collective-permute-start.92 = (bf16[192,768]{1,0:T(8,128)(2,1)S(1)}, bf16[192,768]{1,0:T(8,128)(2,1)S(1)}, u32[]{:S(2)}, u32[]{:S(2)}) collective-permute-start(bf16[192,768]{1,0:T(8,128)(2,1)S(1)} %add_convert_fusion.14), channel_id=1, source_target_pairs={{0,2},{1,3},{2,0},{3,1},{4,6},{5,7},{6,4},{7,5},{8,10},{9,11},{10,... | collective-permute-start | bytes 884744 | tf_op jit(solution)/shard_map/ppermute | solution.py:554
  (181 other events, 1592.1 us)
